TPU v7x, 32 devices: a whole 2x2x4 slice. The times are simulated.
32 devices in a mesh: sec: 2 (over x), row: 4 (over z), col: 4 (over y, core).
Axes of the slice: x: 2, y: 2, z: 4, core: 2. Of those that a mesh axis runs over, the one named last changes fastest.
Arguments:
- held_inverse: bfloat16 [12288, 12288], P('row', ('sec', 'col')), as said below
- factor_panels: bfloat16 [2, 12288, 1024], P(None, ('sec', 'col'), 'row'), may hold values from -0.125 to 0.125
- block_inverses: bfloat16 [2, 1024, 1024], P(None, 'row'), as said below
- covariance: float32 [12288, 12288], P('row', ('sec', 'col')), may hold values from -0.9 to 0.9
Outputs:
- updated: float32 [12288, 12288], P('row', ('sec', 'col'))
Inputs may be any that keep to these rules, and one draw needn't show every extreme that they name: held_inverse is lower triangular with a positive diagonal. Each block of block_inverses is lower triangular with a positive diagonal.
All inputs are finite; a program needn't handle non-finite values.
Results may differ from a plain program's by a relative error of at most 0.0038.
Values may be sent and summed in bfloat16 or wider, within the bound.
No kernel may reach another device: no remote copies, remote signals or barrier semaphores. Data moves between devices by JAX's collectives and lax.ppermute only.
A program may use at most 128 MiB of HBM per device.

v0:
```python
import jax
import jax.numpy as jnp
from jax import lax
from jax.sharding import PartitionSpec as P

PANELS = 2


def from_root(x, axis, root):
    mine = lax.axis_index(axis) == root
    return lax.psum(jnp.where(mine, x, jnp.zeros_like(x)), axis)


def body(held_inverse, factor_panels, block_inverses, covariance):
    total = covariance
    tile_cols = held_inverse.shape[1]
    groups = lax.axis_size(("sec", "col"))
    ratio = groups // lax.axis_size("row")
    column_index = lax.axis_index(("sec", "col"))
    root_row = column_index // ratio
    offset = column_index % ratio * tile_cols
    for panel in range(PANELS):
        partial_value = jnp.dot(
            factor_panels[panel], block_inverses[panel], preferred_element_type=jnp.float32
        )
        scaled = lax.psum_scatter(partial_value, "row", scatter_dimension=1, tiled=True).astype(
            jnp.bfloat16
        )
        terms = jnp.dot(
            held_inverse,
            lax.all_gather(scaled, "row", axis=1, tiled=True),
            preferred_element_type=jnp.float32,
        )
        shares = lax.psum_scatter(terms, ("sec", "col"), scatter_dimension=0, tiled=True)
        inverse = lax.all_gather((-shares).astype(jnp.bfloat16), ("sec", "col"), axis=0, tiled=True)
        own_block = lax.dynamic_slice_in_dim(inverse, offset, tile_cols, 0)
        column_block = from_root(own_block, "row", root_row)
        total = total + lax.dot_general(
            inverse, column_block, (((1,), (1,)), ((), ())), preferred_element_type=jnp.float32
        )
    return total


def solution(mesh):
    in_specs = (
        P("row", ("sec", "col")),
        P(None, ("sec", "col"), "row"),
        P(None, "row", None),
        P("row", ("sec", "col")),
    )
    out_specs = P("row", ("sec", "col"))
    return jax.shard_map(body, mesh=mesh, in_specs=in_specs, out_specs=out_specs, check_vma=False)
```

profile of v0, /device:TPU:0, one launch (start us, length us, event | category | flops | bytes accessed | tf_op | source)
XLA Modules:
  0.0 929.9 jit_solution(8675007073120743143)
XLA Ops:
  6.5 0.0 reduce-scatter.5.cloned.1.call-start
  6.5 5.0 fusion.2
  11.5 0.0 copy-start
  11.5 0.0 copy-start.1
  11.5 0.0 reduce-scatter.5.cloned.1.call-update
  11.5 0.0 reduce-scatter.9.cloned.1.call-start
  11.6 1.3 copy-done
  12.9 0.3 copy-done.1
  13.2 3.7 fusion
  16.9 0.0 reduce-scatter.9.cloned.1.call-update
  16.9 0.0 all-gather.5.cloned.1.call-start
  16.9 108.2 %reduce-scatter.5.cloned.1.call-done = f32[1536,256]{1,0:T(8,128)} async-done(((f32[1536,1024]{1,0:T(8,128)}), f32[1536,256]{1,0:T(8,128)}) %reduce-scatter.5.cloned.1.call-update) | async-done | bytes 1572880 | tf_op jit(solution)/shard_map/reduce_scatter | solution.py:26
  125.1 2.4 convert_element_type.12
  127.5 0.0 all-gather.5.cloned.1.call-update
  127.5 0.0 all-gather.9.cloned.1.call-start
  127.6 111.1 %reduce-scatter.9.cloned.1.call-done = f32[1536,256]{1,0:T(8,128)} async-done(((f32[1536,1024]{1,0:T(8,128)}), f32[1536,256]{1,0:T(8,128)}) %reduce-scatter.9.cloned.1.call-update) | async-done | bytes 1572880 | tf_op jit(solution)/shard_map/reduce_scatter | solution.py:26
  238.7 2.3 convert_element_type.14
  241.1 0.0 all-gather.9.cloned.1.call-update
  241.1 0.0 reduce-scatter.7.cloned.1.call-start
  241.2 63.1 %all-gather.5.cloned.1.call-done = bf16[1536,1024]{1,0:T(8,128)(2,1)} async-done(((bf16[1536,256]{1,0:T(8,128)(2,1)}), bf16[1536,1024]{1,0:T(8,128)(2,1)}) %all-gather.5.cloned.1.call-update) | async-done | bytes 3145744 | tf_op jit(solution)/shard_map/all_gather | solution.py:31
  304.3 16.2 %convolution_bitcast_fusion.1 = f32[3072,1024]{0,1:T(8,128)} fusion(bf16[1536,1024]{1,0:T(8,128)(2,1)} %all-gather.5.cloned.1.call-done, bf16[3072,1536]{1,0:T(8,128)(2,1)} %param.4), kind=kOutput, calls=%fused_computation.2 | convolution fusion | flops 9663676416 | bytes 25165824 | tf_op jit(solution)/shard_map/dot_general | solution.py:29
  320.5 0.0 reduce-scatter.7.cloned.1.call-update
  320.5 0.2 reduce-scatter.11.cloned.1.call-start
  320.8 46.6 %all-gather.9.cloned.1.call-done = bf16[1536,1024]{1,0:T(8,128)(2,1)} async-done(((bf16[1536,256]{1,0:T(8,128)(2,1)}), bf16[1536,1024]{1,0:T(8,128)(2,1)}) %all-gather.9.cloned.1.call-update) | async-done | bytes 3145744 | tf_op jit(solution)/shard_map/all_gather | solution.py:31
  367.4 17.3 %convolution_bitcast_fusion = f32[3072,1024]{0,1:T(8,128)} fusion(bf16[1536,1024]{1,0:T(8,128)(2,1)} %all-gather.9.cloned.1.call-done, bf16[3072,1536]{1,0:T(8,128)(2,1)} %param.4), kind=kOutput, calls=%fused_computation.1 | convolution fusion | flops 9663676416 | bytes 25165824 | tf_op jit(solution)/shard_map/dot_general | solution.py:29
  384.7 0.0 reduce-scatter.11.cloned.1.call-update
  384.7 0.0 all-gather.7.cloned.1.call-start
  384.7 76.6 %reduce-scatter.7.cloned.1.call-done = f32[384,1024]{0,1:T(8,128)} async-done(((f32[3072,1024]{0,1:T(8,128)}), f32[384,1024]{0,1:T(8,128)}) %reduce-scatter.7.cloned.1.call-update) | async-done | bytes 1572880 | tf_op jit(solution)/shard_map/reduce_scatter | solution.py:34
  461.3 2.4 negate_convert_fusion.1
  463.7 0.0 all-gather.7.cloned.1.call-update
  463.7 0.0 all-gather.11.cloned.1.call-start
  463.8 93.3 %reduce-scatter.11.cloned.1.call-done = f32[384,1024]{0,1:T(8,128)} async-done(((f32[3072,1024]{0,1:T(8,128)}), f32[384,1024]{0,1:T(8,128)}) %reduce-scatter.11.cloned.1.call-update) | async-done | bytes 1572880 | tf_op jit(solution)/shard_map/reduce_scatter | solution.py:34
  557.1 2.4 negate_convert_fusion
  559.6 0.0 all-gather.11.cloned.1.call-update
  559.6 0.3 all-reduce.3.cloned.1.call-start
  559.9 45.8 %all-gather.7.cloned.1.call-done = bf16[3072,1024]{0,1:T(8,128)(2,1)} async-done(((bf16[384,1024]{0,1:T(8,128)(2,1)}), bf16[3072,1024]{0,1:T(8,128)(2,1)}) %all-gather.7.cloned.1.call-update) | async-done | bytes 6291472 | tf_op jit(solution)/shard_map/all_gather | solution.py:35
  605.7 4.1 dynamic-slice_select_fusion.1
  609.8 44.5 %all-gather.11.cloned.1.call-done = bf16[3072,1024]{0,1:T(8,128)(2,1)} async-done(((bf16[384,1024]{0,1:T(8,128)(2,1)}), bf16[3072,1024]{0,1:T(8,128)(2,1)}) %all-gather.11.cloned.1.call-update) | async-done | bytes 6291472 | tf_op jit(solution)/shard_map/all_gather | solution.py:35
  654.2 4.1 dynamic-slice_select_fusion
  658.3 0.0 slice-start
  658.3 0.0 all-reduce.3.cloned.1.call-update
  658.4 223.4 %all-reduce.3.cloned.1.call-done = (bf16[1536,1024]{0,1:T(8,128)(2,1)}, bf16[1536,1024]{0,1:T(8,128)(2,1)}) async-done(((bf16[1536,1024]{0,1:T(8,128)(2,1)}, bf16[1536,1024]{0,1:T(8,128)(2,1)}), (bf16[1536,1024]{0,1:T(8,128)(2,1)}, bf16[1536,1024]{0,1:T(8,128)(2,1)})) %all-reduce.3.cloned.1.call-update) | async-done | bytes 6291472 | tf_op jit(solution)/shard_map/psum | solution.py:11
  881.7 0.0 slice-start.1
  881.7 17.0 %fusion.10 = f32[3072,1536]{1,0:T(8,128)} fusion(bf16[3072,1024]{0,1:T(8,128)(2,1)} %all-gather.7.cloned.1.call-done, bf16[1536,1024]{0,1:T(8,128)(2,1)} %get-tuple-element.5), kind=kOutput, calls=%fused_computation.17 | convolution fusion | flops 9663676416 | bytes 28311552 | tf_op jit(solution)/shard_map/dot_general | solution.py:38
  898.7 0.0 slice-done
  898.7 0.0 slice-done.1
  898.7 24.7 %add_add_fusion = f32[3072,1536]{1,0:T(8,128)} fusion(f32[3072,1536]{1,0:T(8,128)} %param.7, f32[3072,1536]{1,0:T(8,128)} %fusion.10, bf16[3072,1024]{0,1:T(8,128)(2,1)S(1)} %bitcast.25, bf16[1536,1024]{0,1:T(8,128)(2,1)} %get-tuple-element.6), kind=kOutput, calls=%fused_computation | convolution fusion | flops 9673113600 | bytes 66060288 | tf_op jit(solution)/shard_map/dot_general | solution.py:38
  (1 shorter events, 0.0 us)
Async XLA Ops:
  6.5 118.6 %reduce-scatter.5.cloned.1.call-start = ((), (), s32[]{:S(2)}) async-start(), calls=%async_computation.4 | async-start | bytes 7864320 | tf_op jit(solution)/shard_map/reduce_scatter | solution.py:26
  11.5 1.4 copy-start
  11.5 1.7 copy-start.1
  11.5 227.2 %reduce-scatter.9.cloned.1.call-start = ((), (), s32[]{:S(2)}) async-start(), calls=%async_computation.8 | async-start | bytes 7864320 | tf_op jit(solution)/shard_map/reduce_scatter | solution.py:26
  16.9 287.4 %all-gather.5.cloned.1.call-start = ((), (), s32[]{:S(2)}) async-start(), calls=%async_computation.5 | async-start | bytes 3932160 | tf_op jit(solution)/shard_map/all_gather | solution.py:31
  127.5 239.8 %all-gather.9.cloned.1.call-start = ((), (), s32[]{:S(2)}) async-start(), calls=%async_computation.9 | async-start | bytes 3932160 | tf_op jit(solution)/shard_map/all_gather | solution.py:31
  241.1 220.2 %reduce-scatter.7.cloned.1.call-start = ((), (), s32[]{:S(2)}) async-start(), calls=%async_computation.6 | async-start | bytes 14155776 | tf_op jit(solution)/shard_map/reduce_scatter | solution.py:34
  320.5 236.6 %reduce-scatter.11.cloned.1.call-start = ((), (), s32[]{:S(2)}) async-start(), calls=%async_computation.10 | async-start | bytes 14155776 | tf_op jit(solution)/shard_map/reduce_scatter | solution.py:34
  384.7 221.0 %all-gather.7.cloned.1.call-start = ((), (), s32[]{:S(2)}) async-start(), calls=%async_computation.7 | async-start | bytes 7077888 | tf_op jit(solution)/shard_map/all_gather | solution.py:35
  463.7 190.5 %all-gather.11.cloned.1.call-start = ((), (), s32[]{:S(2)}) async-start(), calls=%async_computation.11 | async-start | bytes 7077888 | tf_op jit(solution)/shard_map/all_gather | solution.py:35
  559.6 322.1 %all-reduce.3.cloned.1.call-start = ((), (), s32[]{:S(2)}) async-start(), calls=%async_computation.12 | async-start | bytes 12582912 | tf_op jit(solution)/shard_map/psum | solution.py:11
  658.3 240.4 %slice-start = ((s8[6291456]{0:T(1024)(128)(4,1)}), s8[2097152]{0:T(1024)(128)(4,1)S(1)}, s32[]{:S(2)}) async-start(s8[6291456]{0:T(1024)(128)(4,1)} %bitcast.24), calls=%async_computation.13 | async-start | bytes 4194304
  881.7 17.0 %slice-start.1 = ((s8[6291456]{0:T(1024)(128)(4,1)}), s8[4194304]{0:T(1024)(128)(4,1)S(1)}, s32[]{:S(2)}) async-start(s8[6291456]{0:T(1024)(128)(4,1)} %bitcast.24), calls=%async_computation.14 | async-start | bytes 8388608
Sparse Core Ops, SparseCore 0:
  11.7 113.4 reduce-scatter.4
  127.4 111.2 reduce-scatter.8
  240.3 63.9 all-gather.4
  305.7 61.5 all-gather.8
  370.7 90.5 reduce-scatter.6
  464.7 92.4 reduce-scatter.10
  559.0 46.6 all-gather.6
  607.5 46.6 all-gather.10
  658.5 223.1 all-reduce.2
where the time goes:
time: 930 us
  waiting for transfers between devices  813 us (87%)
  matrix products  83.8 us (9%)
  other arithmetic  17.8 us (2%)
  between operations  13.3 us (1%)
    psum x1, waiting for transfers between devices, from_root(): return lax.psum(jnp.where(mine, x, jnp.zeros_like(x)), axis)  223 us
    reduce_scatter x2, waiting for transfers between devices, body(): lax.psum_scatter(partial_value, 'row', scatter_dimension=1, tiled=True)  219 us
    reduce_scatter x2, waiting for transfers between devices, body(): lax.psum_scatter(terms, ('sec', 'col'), scatter_dimension=0, tiled=True)  170 us
    all_gather x2, waiting for transfers between devices, body(): lax.all_gather(scaled, 'row', axis=1, tiled=True)  110 us
    all_gather x2, waiting for transfers between devices, body(): lax.all_gather((-shares).astype(jnp.bfloat16), ('sec', 'col'), axis=0, ti...  90.3 us
    dot_general x2, matrix products, body(): lax.dot_general(inverse, column_block, (((1,), (1,)), ((), ())), preferre...  41.6 us
    dot_general x2, matrix products, body(): jnp.dot(held_inverse, lax.all_gather(scaled, 'row', axis=1, tiled=True),...  33.5 us
  transfers between devices with their start and end apart: 9, of which 9 were waited for; matrix products, arithmetic and copies ran while one was open for 5% of the time, Pallas kernels for 0%

commit v1 on v0

v1 whole, which is shorter than its diff:
```python
import jax
import jax.numpy as jnp
from jax import lax
from jax.sharding import PartitionSpec as P

AXES = ("sec", "row", "col")
SUBS = 1


def pick(array, index):
    return lax.dynamic_index_in_dim(array, index, 0, keepdims=False)


def make_body(shape):
    secs, rows, cols = (shape[axis] for axis in AXES)
    mates = secs * cols // rows
    lanes = cols // mates
    swaps = secs == lanes
    sizes = (secs, lanes)

    def send(value, route):
        pairs = []
        for s in range(secs):
            for r in range(rows):
                for y in range(lanes):
                    for k in range(mates):
                        to = route(s, r, y, k)
                        if to is not None:
                            t, q, v, m = to
                            source = (s * rows + r) * cols + y * mates + k
                            pairs.append((source, (t * rows + q) * cols + v * mates + m))
        return lax.ppermute(value, AXES, pairs)

    def to_mate(value, step):
        return send(value, lambda s, r, y, k: (s, r, y, (k + step) % mates))

    def to_plane(value, phase, step):
        def route(s, r, y, k):
            along_sec = phase == (1 if swaps and k % 2 else 0)
            if along_sec:
                return ((s + step) % secs, r, y, k)
            return (s, r, (y + step) % lanes, k)

        return send(value, route)

    def row_gather(value, wanted):
        ups, downs = [], []
        up = down = value
        for t in range(1, rows):

            def upward(s, r, y, k, t=t):
                return (s, r + 1, y, k) if r + 1 < rows and r + 1 - t >= 0 else None

            def downward(s, r, y, k, t=t):
                ok = r >= 1 and r - 1 + t < rows and wanted(r - 1, s * lanes + y)
                return (s, r - 1, y, k) if ok else None

            up, down = send(up, upward), send(down, downward)
            ups.append(up)
            downs.append(down)
        return ups, downs

    def body(held_inverse, factor_panels, block_inverses, covariance):
        panels, tile, depth = factor_panels.shape
        width = block_inverses.shape[2]
        sec, row = lax.axis_index("sec"), lax.axis_index("row")
        lane, mate = lax.axis_index("col") // mates, lax.axis_index("col") % mates
        block = sec * lanes + lane
        piece = tile // (secs * lanes)
        sub = piece // SUBS

        def first_second(mate):
            if not swaps:
                return sec, lane
            odd = mate % 2 == 1
            return jnp.where(odd, lane, sec), jnp.where(odd, sec, lane)

        def piece_of(mate, one, two):
            if not swaps:
                return one * lanes + two
            return jnp.where(mate % 2 == 1, two * lanes + one, one * lanes + two)

        def below(ups, downs, t):
            return jnp.where(row >= t, ups[t - 1], downs[rows - t - 1])

        part = block_inverses.shape[1] // (mates * rows)
        group = block * mates + mate
        slice_ = lax.dynamic_slice_in_dim(block_inverses, group * part, part, 1)
        ups, downs = row_gather(slice_, lambda r, q: True)
        slices = jnp.stack([slice_] + [below(ups, downs, t) for t in range(1, rows)], 1)
        inverses = []
        for panel in range(panels):
            order = (0, 1) if panel % 2 == 0 else (1, 0)

            def shifted(value, axis, step):
                if axis == 0:
                    return send(value, lambda s, r, y, k: ((s + step) % secs, r, y, k))
                return send(value, lambda s, r, y, k: (s, r, (y + step) % lanes, k))

            found = {(0, 0): slices[panel]}
            for axis in order:
                for at, value in list(found.items()):
                    for step in range(1, sizes[axis]):
                        key = (step, at[1]) if axis == 0 else (at[0], step)
                        found[key] = shifted(value, axis, step)
            whole = jnp.zeros((rows, secs * lanes * mates, part, width), jnp.bfloat16)
            mine = jnp.zeros((rows, secs * lanes, part, width), jnp.bfloat16)
            for (ds, dy), value in found.items():
                at = (sec - ds) % secs * lanes + (lane - dy) % lanes
                mine = lax.dynamic_update_slice(mine, value[:, None], (0, at, 0, 0))
            whole = whole.reshape(rows, secs * lanes, mates, part, width)
            for step in range(mates):
                value = mine if step == 0 else to_mate(mine, step)
                whole = lax.dynamic_update_slice(
                    whole, value[:, :, None], (0, 0, (mate - step) % mates, 0, 0)
                )
            inverses.append(whole.reshape(rows * depth, width))

        halves = held_inverse.reshape(mates, secs * lanes, piece, tile)

        def share(step):
            target = (mate + step) % mates
            half = pick(halves, target)
            one, two = first_second(target)
            n1, n2 = sizes
            parts = [
                pick(half, piece_of(target, (one + a) % n1, (two + b) % n2)).reshape(SUBS, sub, tile)
                for a in range(n1)
                for b in range(n2)
            ]
            return jnp.stack(parts, 1)

        held = [share(0)] + [to_mate(share(step), step) for step in range(1, mates)]

        one, two = first_second(mate)
        n1, n2 = sizes
        total = covariance
        gathered = [
            row_gather(factor_panels[panel], lambda r, q: r >= q) for panel in range(panels)
        ]
        for panel in range(panels):
            ups, downs = gathered[panel]
            factor = jnp.concatenate(
                [factor_panels[panel]] + [below(ups, downs, t) for t in range(1, rows)], 1
            )
            scaled = jnp.dot(
                factor, inverses[panel], preferred_element_type=jnp.float32
            ).astype(jnp.bfloat16)
            scaleds = [scaled] + [to_mate(scaled, step) for step in range(1, mates)]
            row_buffer = jnp.zeros((mates, secs * lanes, piece, width), jnp.bfloat16)
            col_buffer = jnp.zeros((secs * lanes, piece, width), jnp.bfloat16)
            for index in range(SUBS):
                terms = sum(
                    jnp.dot(
                        held[step][index].reshape(n1 * n2 * sub, tile),
                        scaleds[step],
                        preferred_element_type=jnp.float32,
                    )
                    for step in range(mates)
                ).reshape(n1, n2, sub, width)
                half_sum = terms[0]
                for step in range(1, n1):
                    half_sum = half_sum + to_plane(terms[step].astype(jnp.bfloat16), 0, step)
                whole_sum = half_sum[0]
                for step in range(1, n2):
                    whole_sum = whole_sum + to_plane(half_sum[step].astype(jnp.bfloat16), 1, step)
                own = whole_sum.astype(jnp.bfloat16)

                found = {(0, 0): own}
                for a in range(1, n1):
                    found[a, 0] = to_plane(own, 0, a)
                for a in range(n1):
                    for b in range(1, n2):
                        found[a, b] = to_plane(found[a, 0], 1, b)
                places = {
                    key: piece_of(mate, (one - key[0]) % n1, (two - key[1]) % n2) for key in found
                }
                for key, value in found.items():
                    row_buffer = lax.dynamic_update_slice(
                        row_buffer, value[None, None], (mate, places[key], index * sub, 0)
                    )

                ups, downs = row_gather(own, lambda r, q: True)
                arrived = {}
                for ds in range(secs):
                    for dy in range(lanes):
                        target = (sec + ds) % secs * lanes + (lane + dy) % lanes
                        sums = []
                        for t in range(1, rows):
                            value = jnp.where(row - t == target, ups[t - 1], downs[t - 1])
                            if ds == 0 and dy == 0:
                                value = jnp.where(abs(row - target) == t, value, 0)
                            else:

                                def route(s, r, y, k, t=t):
                                    v, w = (s + ds) % secs, (y + dy) % lanes
                                    return (v, r, w, k) if abs(r - v * lanes - w) == t else None

                                value = send(value, route)
                            sums.append(value)
                        arrived[ds, dy] = sum(sums[1:], sums[0])
                for (ds, dy), value in arrived.items():
                    place = (sec - ds) % secs * lanes + (lane - dy) % lanes
                    col_buffer = lax.dynamic_update_slice(
                        col_buffer, value[None], (place, index * sub, 0)
                    )
            own_half = pick(row_buffer, mate)
            for step in range(1, mates):
                row_buffer = lax.dynamic_update_slice(
                    row_buffer, to_mate(own_half, step)[None], ((mate - step) % mates, 0, 0, 0)
                )
            columns = jnp.where(row == block, own_half, col_buffer)
            total = total + lax.dot_general(
                row_buffer.reshape(-1, width),
                columns.reshape(-1, width),
                (((1,), (1,)), ((), ())),
                preferred_element_type=jnp.float32,
            )
        return total

    return body


def solution(mesh):
    in_specs = (
        P("row", ("sec", "col")),
        P(None, ("sec", "col"), "row"),
        P(None, "row", None),
        P("row", ("sec", "col")),
    )
    out_specs = P("row", ("sec", "col"))
    return jax.shard_map(
        make_body(dict(mesh.shape)), mesh=mesh, in_specs=in_specs, out_specs=out_specs, check_vma=False
    )
```

time: 930 us -> 493 us (0.53); the launches traced: 930 us -> 483 us
  waiting for transfers between devices: 813 us -> 228 us
  starting transfers between devices: 0.74 us -> 114 us
  local copies, waits for them, and re-layouts: 1.63 us -> 33.7 us
  between operations: 13.3 us -> 1.86 us
  other arithmetic: 17.8 us -> 29.1 us
    reduce_scatter x4 -> x0, waiting for transfers between devices: 389 us -> none  [the longest x2 219 us: body(): lax.psum_scatter(partial_value, 'row', scatter_dimension=1, tiled=True)]
    ppermute x0 -> x71, waiting for transfers between devices: none -> 228 us  [send(): return lax.ppermute(value, AXES, pairs)]
    psum x1 -> x0, waiting for transfers between devices: 223 us -> none  [from_root(): return lax.psum(jnp.where(mine, x, jnp.zeros_like(x)), axis)]
    all_gather x4 -> x0, waiting for transfers between devices: 200 us -> none  [the longest x2 110 us: body(): lax.all_gather(scaled, 'row', axis=1, tiled=True)]
    ppermute x0 -> x71, starting transfers between devices: none -> 114 us  [send(): return lax.ppermute(value, AXES, pairs)]
    dynamic_update_slice x0 -> x20, local copies, waits for them, and re-layouts: none -> 12.7 us  [the longest x6 8.02 us: body(): lax.dynamic_update_slice(row_buffer, value[None, None], (mate, places[key...]
    dynamic_update_slice x0 -> x10, other arithmetic: none -> 12.4 us  [the longest x8 7.12 us: body(): lax.dynamic_update_slice(col_buffer, value[None], (place, index * sub, 0))]
    convert_element_type x4 -> x0, other arithmetic: 9.57 us -> none  [the longest x2 4.85 us: body(): (-shares).astype(jnp.bfloat16)]
  transfers between devices with their start and end apart: 9 -> 71, of which waited for: 9 -> 26; matrix products, arithmetic and copies ran while one was open for 5% -> 22% of each run, Pallas kernels for 0% -> 0%
where the time goes in v1:
time: 493 us; the launch traced here: 483 us
  waiting for transfers between devices  228 us (46%)
  starting transfers between devices  114 us (23%)
  matrix products  76.8 us (16%)
  local copies, waits for them, and re-layouts  33.7 us (7%)
  other arithmetic  29.1 us (6%)
    ppermute x71, waiting for transfers between devices, send(): return lax.ppermute(value, AXES, pairs)  228 us
    ppermute x71, starting transfers between devices, send(): return lax.ppermute(value, AXES, pairs)  114 us
    dot_general x2, matrix products, body(): lax.dot_general(row_buffer.reshape(-1, width), columns.reshape(-1, width)...  41.7 us
    dot_general x4, matrix products, body(): jnp.dot(held[step][index].reshape(n1 * n2 * sub, tile), scaleds[step], pr...  27.9 us
  transfers between devices with their start and end apart: 71, of which 26 were waited for; matrix products, arithmetic and copies ran while one was open for 22% of the time, Pallas kernels for 0%

profile of v1, /device:TPU:0, one launch (start us, length us, event | category | flops | bytes accessed | tf_op | source)
XLA Modules:
  0.0 483.2 jit_solution(15562102048491825815)
XLA Ops:
  1.9 4.9 %collective-permute-start.6 = (bf16[2,32,1024]{2,1,0:T(8,128)(2,1)}, bf16[2,32,1024]{2,1,0:T(8,128)(2,1)S(1)}, u32[]{:S(2)}, u32[]{:S(2)}) collective-permute-start(bf16[2,32,1024]{2,1,0:T(8,128)(2,1)} %constant_dynamic-slice_fusion.4), channel_id=1, source_target_pairs={{0,4},{1,5},{2,6},{3,7},{4,8},{5,9},{6,10},{7,11},{8,12},{9,13},{1... | collective-permute-start | bytes 393224 | tf_op jit(solution)/shard_map/ppermute | solution.py:32
  11.2 4.3 constant_dynamic-slice_fusion.3
  15.5 2.5 pad_maximum_fusion
  20.6 2.5 pad_maximum_fusion.1
  23.8 10.2 %collective-permute-done.8 = bf16[2,32,1024]{2,1,0:T(8,128)(2,1)} collective-permute-done((bf16[2,32,1024]{2,1,0:T(8,128)(2,1)}, bf16[2,32,1024]{2,1,0:T(8,128)(2,1)}, u32[]{:S(2)}, u32[]{:S(2)}) %collective-permute-start.8) | collective-permute-done | bytes 131104 | tf_op jit(solution)/shard_map/ppermute | solution.py:32
  37.2 3.9 collective-permute-done.9
  47.7 2.9 collective-permute-start.39
  53.7 3.9 collective-permute-done.12
  57.6 3.4 collective-permute-start
  61.7 6.9 %collective-permute-done.47 = bf16[4,32,1024]{2,1,0:T(8,128)(2,1)S(1)} collective-permute-done((bf16[4,32,1024]{2,1,0:T(8,128)(2,1)S(1)}, bf16[4,32,1024]{2,1,0:T(8,128)(2,1)S(1)}, u32[]{:S(2)}, u32[]{:S(2)}) %collective-permute-start.47) | collective-permute-done | bytes 262176 | tf_op jit(solution)/shard_map/ppermute | solution.py:32
  73.7 10.3 %collective-permute-done = bf16[1536,256]{1,0:T(8,128)(2,1)S(1)} collective-permute-done((bf16[1536,256]{1,0:T(8,128)(2,1)S(1)}, bf16[1536,256]{1,0:T(8,128)(2,1)S(1)}, u32[]{:S(2)}, u32[]{:S(2)}) %collective-permute-start) | collective-permute-done | bytes 786464 | tf_op jit(solution)/shard_map/ppermute | solution.py:32
  86.7 5.8 %collective-permute-done.41 = bf16[1536,256]{1,0:T(8,128)(2,1)S(1)} collective-permute-done((bf16[1536,256]{1,0:T(8,128)(2,1)S(1)}, bf16[1536,256]{1,0:T(8,128)(2,1)S(1)}, u32[]{:S(2)}, u32[]{:S(2)}) %collective-permute-start.41) | collective-permute-done | bytes 786464 | tf_op jit(solution)/shard_map/ppermute | solution.py:32
  93.1 15.8 %collective-permute-done.2 = bf16[1536,256]{1,0:T(8,128)(2,1)S(1)} collective-permute-done((bf16[1536,256]{1,0:T(8,128)(2,1)S(1)}, bf16[1536,256]{1,0:T(8,128)(2,1)S(1)}, u32[]{:S(2)}, u32[]{:S(2)}) %collective-permute-start.2) | collective-permute-done | bytes 786464 | tf_op jit(solution)/shard_map/ppermute | solution.py:32
  113.7 25.2 %collective-permute-done.42 = bf16[1536,256]{1,0:T(8,128)(2,1)S(1)} collective-permute-done((bf16[1536,256]{1,0:T(8,128)(2,1)S(1)}, bf16[1536,256]{1,0:T(8,128)(2,1)S(1)}, u32[]{:S(2)}, u32[]{:S(2)}) %collective-permute-start.42) | collective-permute-done | bytes 786464 | tf_op jit(solution)/shard_map/ppermute | solution.py:32
  139.0 3.6 convolution_convert_fusion
  142.8 10.8 %collective-permute-done.3 = bf16[1536,256]{1,0:T(8,128)(2,1)S(1)} collective-permute-done((bf16[1536,256]{1,0:T(8,128)(2,1)S(1)}, bf16[1536,256]{1,0:T(8,128)(2,1)S(1)}, u32[]{:S(2)}, u32[]{:S(2)}) %collective-permute-start.3) | collective-permute-done | bytes 786464 | tf_op jit(solution)/shard_map/ppermute | solution.py:32
  153.7 3.6 convolution_convert_fusion.1
  157.5 5.3 %fusion.26 = f32[1536,1024]{1,0:T(8,128)S(1)} fusion(bf16[1536,1536]{1,0:T(8,128)(2,1)S(1)} %bitcast.156, bf16[1536,1024]{1,0:T(8,128)(2,1)S(1)} %convolution_convert_fusion), kind=kOutput, calls=%fused_computation.114 | convolution fusion | flops 4831838208 | bytes 14155776 | tf_op jit(solution)/shard_map/dot_general | solution.py:154
  162.8 7.3 %fusion.24 = f32[1536,1024]{1,0:T(8,128)} fusion(bf16[1536,1536]{1,0:T(8,128)(2,1)S(1)} %bitcast.157, bf16[1536,1024]{1,0:T(8,128)(2,1)S(1)} %convolution_convert_fusion.1), kind=kOutput, calls=%fused_computation.112 | convolution fusion | flops 4831838208 | bytes 14155776 | tf_op jit(solution)/shard_map/dot_general | solution.py:154
  170.1 5.3 %convolution_add_fusion = f32[1536,1024]{1,0:T(8,128)S(1)} fusion(f32[1536,1024]{1,0:T(8,128)S(1)} %fusion.26, bf16[1536,1536]{1,0:T(8,128)(2,1)S(1)} %bitcast.164, bf16[1536,1024]{1,0:T(8,128)(2,1)S(1)} %collective-permute-done.49), kind=kOutput, calls=%fused_computation.3 | convolution fusion | flops 4833411072 | bytes 20447232 | tf_op jit(solution)/shard_map/dot_general | solution.py:154
  175.8 10.0 %convolution_add_fusion.1 = f32[1536,1024]{1,0:T(8,128)S(1)} fusion(f32[1536,1024]{1,0:T(8,128)} %fusion.24, bf16[1536,1536]{1,0:T(8,128)(2,1)S(1)} %bitcast.165, bf16[1536,1024]{1,0:T(8,128)(2,1)} %collective-permute-done.17), kind=kOutput, calls=%fused_computation.4 | convolution fusion | flops 4833411072 | bytes 20447232 | tf_op jit(solution)/shard_map/dot_general | solution.py:154
  186.2 2.3 copy-done.2
  188.5 7.7 %collective-permute-done.50 = bf16[2,384,1024]{2,1,0:T(8,128)(2,1)S(1)} collective-permute-done((bf16[2,384,1024]{2,1,0:T(8,128)(2,1)S(1)}, bf16[2,384,1024]{2,1,0:T(8,128)(2,1)S(1)}, u32[]{:S(2)}, u32[]{:S(2)}) %collective-permute-start.50) | collective-permute-done | bytes 1572896 | tf_op jit(solution)/shard_map/ppermute | solution.py:32
  198.0 23.5 %collective-permute-done.18 = bf16[2,384,1024]{2,1,0:T(8,128)(2,1)S(1)} collective-permute-done((bf16[2,384,1024]{2,1,0:T(8,128)(2,1)S(1)}, bf16[2,384,1024]{2,1,0:T(8,128)(2,1)S(1)}, u32[]{:S(2)}, u32[]{:S(2)}) %collective-permute-start.18) | collective-permute-done | bytes 1572896 | tf_op jit(solution)/shard_map/ppermute | solution.py:32
  223.1 3.4 broadcast.37.clone.1
  226.5 2.6 bitcast_dynamic-update-slice_fusion.13
  229.1 2.3 collective-permute-start.56
  231.5 3.9 collective-permute-done.19
  235.4 3.5 broadcast.37.clone
  238.9 2.7 bitcast_dynamic-update-slice_fusion.21
  245.7 3.1 collective-permute-done.56
  248.8 15.6 %collective-permute-done.24 = bf16[384,1024]{1,0:T(8,128)(2,1)S(1)} collective-permute-done((bf16[384,1024]{1,0:T(8,128)(2,1)}, bf16[384,1024]{1,0:T(8,128)(2,1)S(1)}, u32[]{:S(2)}, u32[]{:S(2)}) %collective-permute-start.24) | collective-permute-done | bytes 786464 | tf_op jit(solution)/shard_map/ppermute | solution.py:32
  267.1 15.4 %collective-permute-done.57 = bf16[384,1024]{1,0:T(8,128)(2,1)S(1)} collective-permute-done((bf16[384,1024]{1,0:T(8,128)(2,1)}, bf16[384,1024]{1,0:T(8,128)(2,1)S(1)}, u32[]{:S(2)}, u32[]{:S(2)}) %collective-permute-start.57) | collective-permute-done | bytes 786464 | tf_op jit(solution)/shard_map/ppermute | solution.py:32
  286.7 12.7 %collective-permute-done.27 = bf16[384,1024]{1,0:T(8,128)(2,1)} collective-permute-done((bf16[384,1024]{1,0:T(8,128)(2,1)S(1)}, bf16[384,1024]{1,0:T(8,128)(2,1)}, u32[]{:S(2)}, u32[]{:S(2)}) %collective-permute-start.27) | collective-permute-done | bytes 786464 | tf_op jit(solution)/shard_map/ppermute | solution.py:32
  307.2 9.0 %collective-permute-done.59 = bf16[384,1024]{1,0:T(8,128)(2,1)S(1)} collective-permute-done((bf16[384,1024]{1,0:T(8,128)(2,1)S(1)}, bf16[384,1024]{1,0:T(8,128)(2,1)S(1)}, u32[]{:S(2)}, u32[]{:S(2)}) %collective-permute-start.59) | collective-permute-done | bytes 786464 | tf_op jit(solution)/shard_map/ppermute | solution.py:32
  317.6 12.9 %collective-permute-done.29 = bf16[384,1024]{1,0:T(8,128)(2,1)S(1)} collective-permute-done((bf16[384,1024]{1,0:T(8,128)(2,1)}, bf16[384,1024]{1,0:T(8,128)(2,1)S(1)}, u32[]{:S(2)}, u32[]{:S(2)}) %collective-permute-start.29) | collective-permute-done | bytes 786464 | tf_op jit(solution)/shard_map/ppermute | solution.py:32
  335.5 7.5 %collective-permute-start.34 = (bf16[384,1024]{1,0:T(8,128)(2,1)S(1)}, bf16[384,1024]{1,0:T(8,128)(2,1)S(1)}, u32[]{:S(2)}, u32[]{:S(2)}) collective-permute-start(bf16[384,1024]{1,0:T(8,128)(2,1)S(1)} %get-tuple-element.22), channel_id=1, source_target_pairs={{0,16},{1,17},{6,22},{7,23},{24,8},{25,9},{30,14},{31,15}} | collective-permute-start | bytes 2359304 | tf_op jit(solution)/shard_map/ppermute | solution.py:32
  343.0 6.5 %collective-permute-done.61 = bf16[384,1024]{1,0:T(8,128)(2,1)S(1)} collective-permute-done((bf16[384,1024]{1,0:T(8,128)(2,1)S(1)}, bf16[384,1024]{1,0:T(8,128)(2,1)S(1)}, u32[]{:S(2)}, u32[]{:S(2)}) %collective-permute-start.61) | collective-permute-done | bytes 786464 | tf_op jit(solution)/shard_map/ppermute | solution.py:32
  353.6 3.4 collective-permute-start.38
  363.2 23.8 %collective-permute-start.54 = (bf16[384,1024]{1,0:T(8,128)(2,1)}, bf16[384,1024]{1,0:T(8,128)(2,1)S(1)}, u32[]{:S(2)}, u32[]{:S(2)}) collective-permute-start(bf16[384,1024]{1,0:T(8,128)(2,1)} %collective-permute-done.52), channel_id=1, source_target_pairs={{0,2},{1,17},{2,0},{3,19},{4,6},{5,21},{6,4},{7,23},{8,10},{9,25},... | collective-permute-start | bytes 2359304 | tf_op jit(solution)/shard_map/ppermute | solution.py:32
  389.0 2.3 broadcast_select_fusion.1
  391.3 3.6 collective-permute-start.66
  401.1 6.8 %collective-permute-done.66 = bf16[384,1024]{1,0:T(8,128)(2,1)S(1)} collective-permute-done((bf16[384,1024]{1,0:T(8,128)(2,1)S(1)}, bf16[384,1024]{1,0:T(8,128)(2,1)S(1)}, u32[]{:S(2)}, u32[]{:S(2)}) %collective-permute-start.66) | collective-permute-done | bytes 786464 | tf_op jit(solution)/shard_map/ppermute | solution.py:32
  408.6 10.7 %collective-permute-start.70 = (bf16[384,1024]{1,0:T(8,128)(2,1)S(1)}, bf16[384,1024]{1,0:T(8,128)(2,1)S(1)}, u32[]{:S(2)}, u32[]{:S(2)}) collective-permute-start(bf16[384,1024]{1,0:T(8,128)(2,1)S(1)} %get-tuple-element.38), channel_id=1, source_target_pairs={{0,18},{1,19},{30,12},{31,13}} | collective-permute-start | bytes 2359304 | tf_op jit(solution)/shard_map/ppermute | solution.py:32
  422.9 11.5 %collective-permute-done.70 = bf16[384,1024]{1,0:T(8,128)(2,1)S(1)} collective-permute-done((bf16[384,1024]{1,0:T(8,128)(2,1)S(1)}, bf16[384,1024]{1,0:T(8,128)(2,1)S(1)}, u32[]{:S(2)}, u32[]{:S(2)}) %collective-permute-start.70) | collective-permute-done | bytes 786464 | tf_op jit(solution)/shard_map/ppermute | solution.py:32
  434.8 2.3 broadcast_select_fusion
  439.3 16.1 %fusion.25 = f32[3072,1536]{1,0:T(8,128)} fusion(bf16[3072,1024]{1,0:T(8,128)(2,1)} %bitcast.32, bf16[1536,1024]{1,0:T(8,128)(2,1)S(1)} %bitcast.158), kind=kOutput, calls=%fused_computation.113 | convolution fusion | flops 9663676416 | bytes 28311552 | tf_op jit(solution)/shard_map/dot_general | solution.py:213
  457.3 25.6 %add_add_fusion = f32[3072,1536]{1,0:T(8,128)} fusion(f32[3072,1536]{1,0:T(8,128)} %param.7, f32[3072,1536]{1,0:T(8,128)} %fusion.25, bf16[3072,1024]{1,0:T(8,128)(2,1)} %bitcast.63, bf16[1536,1024]{1,0:T(8,128)(2,1)S(1)} %bitcast.159), kind=kOutput, calls=%fused_computation | convolution fusion | flops 9673113600 | bytes 66060288 | tf_op jit(solution)/shard_map/dot_general | solution.py:213
  (194 shorter events, 92.0 us)
Async XLA Ops:
  9.6 60.6 %collective-permute-start.40 = (bf16[1536,256]{1,0:T(8,128)(2,1)S(1)}, bf16[1536,256]{1,0:T(8,128)(2,1)S(1)}, u32[]{:S(2)}, u32[]{:S(2)}) collective-permute-start(bf16[1536,256]{1,0:T(8,128)(2,1)S(1)} %get-tuple-element.31), channel_id=1, source_target_pairs={{4,0},{5,1},{8,4},{9,5},{10,6},{11,7},{12,8},{13,9},{14,10},{15,11... | collective-permute-start | bytes 2359304 | tf_op jit(solution)/shard_map/ppermute | solution.py:32
  47.7 22.6 %collective-permute-start.39 = (bf16[1536,256]{1,0:T(8,128)(2,1)S(1)}, bf16[1536,256]{1,0:T(8,128)(2,1)S(1)}, u32[]{:S(2)}, u32[]{:S(2)}) collective-permute-start(bf16[1536,256]{1,0:T(8,128)(2,1)S(1)} %get-tuple-element.31), channel_id=1, source_target_pairs={{0,4},{1,5},{2,6},{3,7},{4,8},{5,9},{6,10},{7,11},{8,12},{9,13},{1... | collective-permute-start | bytes 2359304 | tf_op jit(solution)/shard_map/ppermute | solution.py:32
  52.5 20.5 %collective-permute-start.1 = (bf16[1536,256]{1,0:T(8,128)(2,1)S(1)}, bf16[1536,256]{1,0:T(8,128)(2,1)S(1)}, u32[]{:S(2)}, u32[]{:S(2)}) collective-permute-start(bf16[1536,256]{1,0:T(8,128)(2,1)S(1)} %get-tuple-element.30), channel_id=1, source_target_pairs={{4,0},{5,1},{8,4},{9,5},{10,6},{11,7},{12,8},{13,9},{14,10},{15,11... | collective-permute-start | bytes 2359304 | tf_op jit(solution)/shard_map/ppermute | solution.py:32
  57.6 26.3 %collective-permute-start = (bf16[1536,256]{1,0:T(8,128)(2,1)S(1)}, bf16[1536,256]{1,0:T(8,128)(2,1)S(1)}, u32[]{:S(2)}, u32[]{:S(2)}) collective-permute-start(bf16[1536,256]{1,0:T(8,128)(2,1)S(1)} %get-tuple-element.30), channel_id=1, source_target_pairs={{0,4},{1,5},{2,6},{3,7},{4,8},{5,9},{6,10},{7,11},{8,12},{9,13},{1... | collective-permute-start | bytes 2359304 | tf_op jit(solution)/shard_map/ppermute | solution.py:32
  70.2 99.9 %collective-permute-start.16 = (bf16[1,4,384,1536]{3,2,1,0:T(8,128)(2,1)S(1)}, bf16[1,4,384,1536]{3,2,1,0:T(8,128)(2,1)S(1)}, u32[]{:S(2)}, u32[]{:S(2)}) collective-permute-start(bf16[1,4,384,1536]{3,2,1,0:T(8,128)(2,1)S(1)} %copy-done.6), channel_id=1, source_target_pairs={{0,1},{1,0},{2,3},{3,2},{4,5},{5,4},{6,7},{7,6},{8,9},{9,8},{10,11... | collective-permute-start | bytes 14155784 | tf_op jit(solution)/shard_map/ppermute | solution.py:32
  70.3 22.2 %collective-permute-start.41 = (bf16[1536,256]{1,0:T(8,128)(2,1)S(1)}, bf16[1536,256]{1,0:T(8,128)(2,1)S(1)}, u32[]{:S(2)}, u32[]{:S(2)}) collective-permute-start(bf16[1536,256]{1,0:T(8,128)(2,1)S(1)} %collective-permute-done.40), channel_id=1, source_target_pairs={{4,0},{5,1},{8,4},{9,5},{10,6},{11,7}} | collective-permute-start | bytes 2359304 | tf_op jit(solution)/shard_map/ppermute | solution.py:32
  72.9 19.6 %collective-permute-start.43 = (bf16[1536,256]{1,0:T(8,128)(2,1)S(1)}, bf16[1536,256]{1,0:T(8,128)(2,1)S(1)}, u32[]{:S(2)}, u32[]{:S(2)}) collective-permute-start(bf16[1536,256]{1,0:T(8,128)(2,1)S(1)} %collective-permute-done.39), channel_id=1, source_target_pairs={{4,8},{5,9},{6,10},{7,11},{8,12},{9,13},{10,14},{11,15},{20,24},{2... | collective-permute-start | bytes 2359304 | tf_op jit(solution)/shard_map/ppermute | solution.py:32
  83.9 25.0 %collective-permute-start.2 = (bf16[1536,256]{1,0:T(8,128)(2,1)S(1)}, bf16[1536,256]{1,0:T(8,128)(2,1)S(1)}, u32[]{:S(2)}, u32[]{:S(2)}) collective-permute-start(bf16[1536,256]{1,0:T(8,128)(2,1)S(1)} %collective-permute-done.1), channel_id=1, source_target_pairs={{4,0},{5,1},{8,4},{9,5},{10,6},{11,7}} | collective-permute-start | bytes 2359304 | tf_op jit(solution)/shard_map/ppermute | solution.py:32
  85.2 24.4 %collective-permute-start.4 = (bf16[1536,256]{1,0:T(8,128)(2,1)S(1)}, bf16[1536,256]{1,0:T(8,128)(2,1)S(1)}, u32[]{:S(2)}, u32[]{:S(2)}) collective-permute-start(bf16[1536,256]{1,0:T(8,128)(2,1)S(1)} %collective-permute-done), channel_id=1, source_target_pairs={{4,8},{5,9},{6,10},{7,11},{8,12},{9,13},{10,14},{11,15},{20,24},{2... | collective-permute-start | bytes 2359304 | tf_op jit(solution)/shard_map/ppermute | solution.py:32
  92.5 19.4 %collective-permute-start.15 = (bf16[4,4,32,1024]{3,2,1,0:T(8,128)(2,1)S(1)}, bf16[4,4,32,1024]{3,2,1,0:T(8,128)(2,1)S(1)}, u32[]{:S(2)}, u32[]{:S(2)}) collective-permute-start(bf16[4,4,32,1024]{3,2,1,0:T(8,128)(2,1)S(1)} %bitcast_dynamic-update-slice_fusion.29), channel_id=1, source_target_pairs={{0,1},{1,0},{2,3},{3,2},{4,5},{5,4},{6,7},{7,6},{8,9},{9,8},{10,11... | collective-permute-start | bytes 3145736 | tf_op jit(solution)/shard_map/ppermute | solution.py:32
  109.7 29.2 %collective-permute-start.42 = (bf16[1536,256]{1,0:T(8,128)(2,1)S(1)}, bf16[1536,256]{1,0:T(8,128)(2,1)S(1)}, u32[]{:S(2)}, u32[]{:S(2)}) collective-permute-start(bf16[1536,256]{1,0:T(8,128)(2,1)S(1)} %collective-permute-done.41), channel_id=1, source_target_pairs={{4,0},{5,1}} | collective-permute-start | bytes 2359304 | tf_op jit(solution)/shard_map/ppermute | solution.py:32
  111.1 31.6 %collective-permute-start.5 = (bf16[1536,256]{1,0:T(8,128)(2,1)S(1)}, bf16[1536,256]{1,0:T(8,128)(2,1)S(1)}, u32[]{:S(2)}, u32[]{:S(2)}) collective-permute-start(bf16[1536,256]{1,0:T(8,128)(2,1)S(1)} %collective-permute-done.4), channel_id=1, source_target_pairs={{8,12},{9,13},{10,14},{11,15},{24,28},{25,29},{26,30},{27,31}} | collective-permute-start | bytes 2359304 | tf_op jit(solution)/shard_map/ppermute | solution.py:32
  111.9 41.7 %collective-permute-start.3 = (bf16[1536,256]{1,0:T(8,128)(2,1)S(1)}, bf16[1536,256]{1,0:T(8,128)(2,1)S(1)}, u32[]{:S(2)}, u32[]{:S(2)}) collective-permute-start(bf16[1536,256]{1,0:T(8,128)(2,1)S(1)} %collective-permute-done.2), channel_id=1, source_target_pairs={{4,0},{5,1}} | collective-permute-start | bytes 2359304 | tf_op jit(solution)/shard_map/ppermute | solution.py:32
  142.6 27.5 %collective-permute-start.49 = (bf16[1536,1024]{1,0:T(8,128)(2,1)S(1)}, bf16[1536,1024]{1,0:T(8,128)(2,1)S(1)}, u32[]{:S(2)}, u32[]{:S(2)}) collective-permute-start(bf16[1536,1024]{1,0:T(8,128)(2,1)S(1)} %convolution_convert_fusion), channel_id=1, source_target_pairs={{0,1},{1,0},{2,3},{3,2},{4,5},{5,4},{6,7},{7,6},{8,9},{9,8},{10,11... | collective-permute-start | bytes 9437192 | tf_op jit(solution)/shard_map/ppermute | solution.py:32
  175.7 20.5 %collective-permute-start.50 = (bf16[2,384,1024]{2,1,0:T(8,128)(2,1)S(1)}, bf16[2,384,1024]{2,1,0:T(8,128)(2,1)S(1)}, u32[]{:S(2)}, u32[]{:S(2)}) collective-permute-start(bf16[2,384,1024]{2,1,0:T(8,128)(2,1)S(1)} %bitcast.162), channel_id=1, source_target_pairs={{0,16},{1,3},{2,18},{3,1},{4,20},{5,7},{6,22},{7,5},{8,24},{9,11},... | collective-permute-start | bytes 4718600 | tf_op jit(solution)/shard_map/ppermute | solution.py:32
  186.1 35.4 %collective-permute-start.18 = (bf16[2,384,1024]{2,1,0:T(8,128)(2,1)S(1)}, bf16[2,384,1024]{2,1,0:T(8,128)(2,1)S(1)}, u32[]{:S(2)}, u32[]{:S(2)}) collective-permute-start(bf16[2,384,1024]{2,1,0:T(8,128)(2,1)S(1)} %bitcast.163), channel_id=1, source_target_pairs={{0,16},{1,3},{2,18},{3,1},{4,20},{5,7},{6,22},{7,5},{8,24},{9,11},... | collective-permute-start | bytes 4718600 | tf_op jit(solution)/shard_map/ppermute | solution.py:32
  198.0 25.1 %collective-permute-start.51 = (bf16[384,1024]{1,0:T(8,128)(2,1)}, bf16[384,1024]{1,0:T(8,128)(2,1)}, u32[]{:S(2)}, u32[]{:S(2)}) collective-permute-start(bf16[384,1024]{1,0:T(8,128)(2,1)} %fusion.19), channel_id=1, source_target_pairs={{0,2},{1,17},{2,0},{3,19},{4,6},{5,21},{6,4},{7,23},{8,10},{9,25},... | collective-permute-start | bytes 2359304 | tf_op jit(solution)/shard_map/ppermute | solution.py:32
  229.1 19.7 %collective-permute-start.56 = (bf16[384,1024]{1,0:T(8,128)(2,1)}, bf16[384,1024]{1,0:T(8,128)(2,1)}, u32[]{:S(2)}, u32[]{:S(2)}) collective-permute-start(bf16[384,1024]{1,0:T(8,128)(2,1)} %get-tuple-element.12), channel_id=1, source_target_pairs={{0,4},{1,5},{2,6},{3,7},{4,8},{5,9},{6,10},{7,11},{8,12},{9,13},{1... | collective-permute-start | bytes 2359304 | tf_op jit(solution)/shard_map/ppermute | solution.py:32
  241.6 22.9 %collective-permute-start.24 = (bf16[384,1024]{1,0:T(8,128)(2,1)}, bf16[384,1024]{1,0:T(8,128)(2,1)S(1)}, u32[]{:S(2)}, u32[]{:S(2)}) collective-permute-start(bf16[384,1024]{1,0:T(8,128)(2,1)} %get-tuple-element.8), channel_id=1, source_target_pairs={{0,4},{1,5},{2,6},{3,7},{4,8},{5,9},{6,10},{7,11},{8,12},{9,13},{1... | collective-permute-start | bytes 2359304 | tf_op jit(solution)/shard_map/ppermute | solution.py:32
  243.1 22.6 %collective-permute-start.25 = (bf16[384,1024]{1,0:T(8,128)(2,1)}, bf16[384,1024]{1,0:T(8,128)(2,1)S(1)}, u32[]{:S(2)}, u32[]{:S(2)}) collective-permute-start(bf16[384,1024]{1,0:T(8,128)(2,1)} %get-tuple-element.8), channel_id=1, source_target_pairs={{4,0},{5,1},{6,2},{7,3},{8,4},{9,5},{10,6},{11,7},{12,8},{13,9},{1... | collective-permute-start | bytes 2359304 | tf_op jit(solution)/shard_map/ppermute | solution.py:32
  244.4 38.1 %collective-permute-start.57 = (bf16[384,1024]{1,0:T(8,128)(2,1)}, bf16[384,1024]{1,0:T(8,128)(2,1)S(1)}, u32[]{:S(2)}, u32[]{:S(2)}) collective-permute-start(bf16[384,1024]{1,0:T(8,128)(2,1)} %get-tuple-element.12), channel_id=1, source_target_pairs={{4,0},{5,1},{6,2},{7,3},{8,4},{9,5},{10,6},{11,7},{12,8},{13,9},{1... | collective-permute-start | bytes 2359304 | tf_op jit(solution)/shard_map/ppermute | solution.py:32
  245.7 36.9 %collective-permute-start.52 = (bf16[384,1024]{1,0:T(8,128)(2,1)}, bf16[384,1024]{1,0:T(8,128)(2,1)}, u32[]{:S(2)}, u32[]{:S(2)}) collective-permute-start(bf16[384,1024]{1,0:T(8,128)(2,1)} %get-tuple-element.12), channel_id=1, source_target_pairs={{0,16},{1,3},{2,18},{3,1},{4,20},{5,7},{6,22},{7,5},{8,24},{9,11},... | collective-permute-start | bytes 2359304 | tf_op jit(solution)/shard_map/ppermute | solution.py:32
  248.8 35.9 %collective-permute-start.20 = (bf16[384,1024]{1,0:T(8,128)(2,1)}, bf16[384,1024]{1,0:T(8,128)(2,1)}, u32[]{:S(2)}, u32[]{:S(2)}) collective-permute-start(bf16[384,1024]{1,0:T(8,128)(2,1)} %get-tuple-element.8), channel_id=1, source_target_pairs={{0,16},{1,3},{2,18},{3,1},{4,20},{5,7},{6,22},{7,5},{8,24},{9,11},... | collective-permute-start | bytes 2359304 | tf_op jit(solution)/shard_map/ppermute | solution.py:32
  264.4 21.6 %collective-permute-start.26 = (bf16[384,1024]{1,0:T(8,128)(2,1)S(1)}, bf16[384,1024]{1,0:T(8,128)(2,1)S(1)}, u32[]{:S(2)}, u32[]{:S(2)}) collective-permute-start(bf16[384,1024]{1,0:T(8,128)(2,1)S(1)} %collective-permute-done.24), channel_id=1, source_target_pairs={{4,8},{5,9},{6,10},{7,11},{8,12},{9,13},{10,14},{11,15},{20,24},{2... | collective-permute-start | bytes 2359304 | tf_op jit(solution)/shard_map/ppermute | solution.py:32
  265.6 33.8 %collective-permute-start.27 = (bf16[384,1024]{1,0:T(8,128)(2,1)S(1)}, bf16[384,1024]{1,0:T(8,128)(2,1)}, u32[]{:S(2)}, u32[]{:S(2)}) collective-permute-start(bf16[384,1024]{1,0:T(8,128)(2,1)S(1)} %collective-permute-done.25), channel_id=1, source_target_pairs={{4,0},{5,1},{6,2},{7,3},{8,4},{9,5},{10,6},{11,7},{20,16},{21,17},... | collective-permute-start | bytes 2359304 | tf_op jit(solution)/shard_map/ppermute | solution.py:32
  282.5 20.3 %collective-permute-start.21 = (bf16[384,1024]{1,0:T(8,128)(2,1)}, bf16[384,1024]{1,0:T(8,128)(2,1)S(1)}, u32[]{:S(2)}, u32[]{:S(2)}) collective-permute-start(bf16[384,1024]{1,0:T(8,128)(2,1)} %get-tuple-element.8), channel_id=1, source_target_pairs={{0,2},{1,17},{2,0},{3,19},{4,6},{5,21},{6,4},{7,23},{8,10},{9,25},... | collective-permute-start | bytes 2359304 | tf_op jit(solution)/shard_map/ppermute | solution.py:32
  282.5 22.3 %collective-permute-start.58 = (bf16[384,1024]{1,0:T(8,128)(2,1)}, bf16[384,1024]{1,0:T(8,128)(2,1)S(1)}, u32[]{:S(2)}, u32[]{:S(2)}) collective-permute-start(bf16[384,1024]{1,0:T(8,128)(2,1)} %collective-permute-done.56), channel_id=1, source_target_pairs={{4,8},{5,9},{6,10},{7,11},{8,12},{9,13},{10,14},{11,15},{20,24},{2... | collective-permute-start | bytes 2359304 | tf_op jit(solution)/shard_map/ppermute | solution.py:32
  284.7 31.5 %collective-permute-start.59 = (bf16[384,1024]{1,0:T(8,128)(2,1)S(1)}, bf16[384,1024]{1,0:T(8,128)(2,1)S(1)}, u32[]{:S(2)}, u32[]{:S(2)}) collective-permute-start(bf16[384,1024]{1,0:T(8,128)(2,1)S(1)} %collective-permute-done.57), channel_id=1, source_target_pairs={{4,0},{5,1},{6,2},{7,3},{8,4},{9,5},{10,6},{11,7},{20,16},{21,17},... | collective-permute-start | bytes 2359304 | tf_op jit(solution)/shard_map/ppermute | solution.py:32
  286.0 30.9 %collective-permute-start.28 = (bf16[384,1024]{1,0:T(8,128)(2,1)S(1)}, bf16[384,1024]{1,0:T(8,128)(2,1)S(1)}, u32[]{:S(2)}, u32[]{:S(2)}) collective-permute-start(bf16[384,1024]{1,0:T(8,128)(2,1)S(1)} %collective-permute-done.26), channel_id=1, source_target_pairs={{8,12},{9,13},{10,14},{11,15},{24,28},{25,29},{26,30},{27,31}} | collective-permute-start | bytes 2359304 | tf_op jit(solution)/shard_map/ppermute | solution.py:32
  299.5 31.1 %collective-permute-start.29 = (bf16[384,1024]{1,0:T(8,128)(2,1)}, bf16[384,1024]{1,0:T(8,128)(2,1)S(1)}, u32[]{:S(2)}, u32[]{:S(2)}) collective-permute-start(bf16[384,1024]{1,0:T(8,128)(2,1)} %collective-permute-done.27), channel_id=1, source_target_pairs={{4,0},{5,1},{6,2},{7,3},{20,16},{21,17},{22,18},{23,19}} | collective-permute-start | bytes 2359304 | tf_op jit(solution)/shard_map/ppermute | solution.py:32
  302.8 29.4 %collective-permute-start.30 = (bf16[384,1024]{1,0:T(8,128)(2,1)S(1)}, bf16[384,1024]{1,0:T(8,128)(2,1)S(1)}, u32[]{:S(2)}, u32[]{:S(2)}) collective-permute-start(bf16[384,1024]{1,0:T(8,128)(2,1)S(1)} %get-tuple-element.26), channel_id=1, source_target_pairs={{0,2},{1,3},{6,4},{7,5},{8,10},{9,11},{22,20},{23,21},{24,26},{25,... | collective-permute-start | bytes 2359304 | tf_op jit(solution)/shard_map/ppermute | solution.py:32
  304.8 28.1 %collective-permute-start.22 = (bf16[384,1024]{1,0:T(8,128)(2,1)}, bf16[384,1024]{1,0:T(8,128)(2,1)S(1)}, u32[]{:S(2)}, u32[]{:S(2)}) collective-permute-start(bf16[384,1024]{1,0:T(8,128)(2,1)} %collective-permute-done.20), channel_id=1, source_target_pairs={{0,2},{1,17},{2,0},{3,19},{4,6},{5,21},{6,4},{7,23},{8,10},{9,25},... | collective-permute-start | bytes 2359304 | tf_op jit(solution)/shard_map/ppermute | solution.py:32
  316.2 18.6 %collective-permute-start.33 = (bf16[384,1024]{1,0:T(8,128)(2,1)S(1)}, bf16[384,1024]{1,0:T(8,128)(2,1)S(1)}, u32[]{:S(2)}, u32[]{:S(2)}) collective-permute-start(bf16[384,1024]{1,0:T(8,128)(2,1)S(1)} %get-tuple-element.25), channel_id=1, source_target_pairs={{4,20},{5,21},{10,26},{11,27},{12,28},{13,29},{18,2},{19,3},{20,4}... | collective-permute-start | bytes 2359304 | tf_op jit(solution)/shard_map/ppermute | solution.py:32
  316.9 18.6 %collective-permute-start.60 = (bf16[384,1024]{1,0:T(8,128)(2,1)S(1)}, bf16[384,1024]{1,0:T(8,128)(2,1)S(1)}, u32[]{:S(2)}, u32[]{:S(2)}) collective-permute-start(bf16[384,1024]{1,0:T(8,128)(2,1)S(1)} %collective-permute-done.58), channel_id=1, source_target_pairs={{8,12},{9,13},{10,14},{11,15},{24,28},{25,29},{26,30},{27,31}} | collective-permute-start | bytes 2359304 | tf_op jit(solution)/shard_map/ppermute | solution.py:32
  330.6 19.0 %collective-permute-start.61 = (bf16[384,1024]{1,0:T(8,128)(2,1)S(1)}, bf16[384,1024]{1,0:T(8,128)(2,1)S(1)}, u32[]{:S(2)}, u32[]{:S(2)}) collective-permute-start(bf16[384,1024]{1,0:T(8,128)(2,1)S(1)} %collective-permute-done.59), channel_id=1, source_target_pairs={{4,0},{5,1},{6,2},{7,3},{20,16},{21,17},{22,18},{23,19}} | collective-permute-start | bytes 2359304 | tf_op jit(solution)/shard_map/ppermute | solution.py:32
  332.2 20.6 %collective-permute-start.31 = (bf16[384,1024]{1,0:T(8,128)(2,1)S(1)}, bf16[384,1024]{1,0:T(8,128)(2,1)S(1)}, u32[]{:S(2)}, u32[]{:S(2)}) collective-permute-start(bf16[384,1024]{1,0:T(8,128)(2,1)S(1)} %get-tuple-element.23), channel_id=1, source_target_pairs={{10,8},{11,9},{12,14},{13,15},{18,16},{19,17},{20,22},{21,23}} | collective-permute-start | bytes 2359304 | tf_op jit(solution)/shard_map/ppermute | solution.py:32
  332.9 20.6 %collective-permute-start.32 = (bf16[384,1024]{1,0:T(8,128)(2,1)S(1)}, bf16[384,1024]{1,0:T(8,128)(2,1)S(1)}, u32[]{:S(2)}, u32[]{:S(2)}) collective-permute-start(bf16[384,1024]{1,0:T(8,128)(2,1)S(1)} %get-tuple-element.29), channel_id=1, source_target_pairs={{14,12},{15,13},{16,18},{17,19}} | collective-permute-start | bytes 2359304 | tf_op jit(solution)/shard_map/ppermute | solution.py:32
  334.8 22.8 %collective-permute-start.36 = (bf16[384,1024]{1,0:T(8,128)(2,1)S(1)}, bf16[384,1024]{1,0:T(8,128)(2,1)S(1)}, u32[]{:S(2)}, u32[]{:S(2)}) collective-permute-start(bf16[384,1024]{1,0:T(8,128)(2,1)S(1)} %get-tuple-element.24), channel_id=1, source_target_pairs={{6,20},{7,21},{8,26},{9,27},{14,28},{15,29},{16,2},{17,3},{22,4},{... | collective-permute-start | bytes 2359304 | tf_op jit(solution)/shard_map/ppermute | solution.py:32
  335.5 25.1 %collective-permute-start.34 = (bf16[384,1024]{1,0:T(8,128)(2,1)S(1)}, bf16[384,1024]{1,0:T(8,128)(2,1)S(1)}, u32[]{:S(2)}, u32[]{:S(2)}) collective-permute-start(bf16[384,1024]{1,0:T(8,128)(2,1)S(1)} %get-tuple-element.22), channel_id=1, source_target_pairs={{0,16},{1,17},{6,22},{7,23},{24,8},{25,9},{30,14},{31,15}} | collective-permute-start | bytes 2359304 | tf_op jit(solution)/shard_map/ppermute | solution.py:32
  353.6 33.4 %collective-permute-start.38 = (bf16[384,1024]{1,0:T(8,128)(2,1)S(1)}, bf16[384,1024]{1,0:T(8,128)(2,1)S(1)}, u32[]{:S(2)}, u32[]{:S(2)}) collective-permute-start(bf16[384,1024]{1,0:T(8,128)(2,1)S(1)} %get-tuple-element.27), channel_id=1, source_target_pairs={{0,18},{1,19},{30,12},{31,13}} | collective-permute-start | bytes 2359304 | tf_op jit(solution)/shard_map/ppermute | solution.py:32
  357.6 33.6 %collective-permute-start.53 = (bf16[384,1024]{1,0:T(8,128)(2,1)}, bf16[384,1024]{1,0:T(8,128)(2,1)S(1)}, u32[]{:S(2)}, u32[]{:S(2)}) collective-permute-start(bf16[384,1024]{1,0:T(8,128)(2,1)} %get-tuple-element.12), channel_id=1, source_target_pairs={{0,2},{1,17},{2,0},{3,19},{4,6},{5,21},{6,4},{7,23},{8,10},{9,25},... | collective-permute-start | bytes 2359304 | tf_op jit(solution)/shard_map/ppermute | solution.py:32
  360.6 34.3 %collective-permute-start.62 = (bf16[384,1024]{1,0:T(8,128)(2,1)S(1)}, bf16[384,1024]{1,0:T(8,128)(2,1)S(1)}, u32[]{:S(2)}, u32[]{:S(2)}) collective-permute-start(bf16[384,1024]{1,0:T(8,128)(2,1)S(1)} %get-tuple-element.37), channel_id=1, source_target_pairs={{0,2},{1,3},{6,4},{7,5},{8,10},{9,11},{22,20},{23,21},{24,26},{25,... | collective-permute-start | bytes 2359304 | tf_op jit(solution)/shard_map/ppermute | solution.py:32
  362.0 33.7 %collective-permute-start.65 = (bf16[384,1024]{1,0:T(8,128)(2,1)S(1)}, bf16[384,1024]{1,0:T(8,128)(2,1)S(1)}, u32[]{:S(2)}, u32[]{:S(2)}) collective-permute-start(bf16[384,1024]{1,0:T(8,128)(2,1)S(1)} %get-tuple-element.36), channel_id=1, source_target_pairs={{4,20},{5,21},{10,26},{11,27},{12,28},{13,29},{18,2},{19,3},{20,4}... | collective-permute-start | bytes 2359304 | tf_op jit(solution)/shard_map/ppermute | solution.py:32
  363.2 35.6 %collective-permute-start.54 = (bf16[384,1024]{1,0:T(8,128)(2,1)}, bf16[384,1024]{1,0:T(8,128)(2,1)S(1)}, u32[]{:S(2)}, u32[]{:S(2)}) collective-permute-start(bf16[384,1024]{1,0:T(8,128)(2,1)} %collective-permute-done.52), channel_id=1, source_target_pairs={{0,2},{1,17},{2,0},{3,19},{4,6},{5,21},{6,4},{7,23},{8,10},{9,25},... | collective-permute-start | bytes 2359304 | tf_op jit(solution)/shard_map/ppermute | solution.py:32
  395.6 41.6 %collective-permute-start.23 = (bf16[4,384,1024]{2,1,0:T(8,128)(2,1)S(1)}, bf16[4,384,1024]{2,1,0:T(8,128)(2,1)S(1)}, u32[]{:S(2)}, u32[]{:S(2)}) collective-permute-start(bf16[4,384,1024]{2,1,0:T(8,128)(2,1)S(1)} %get-tuple-element.6), channel_id=1, source_target_pairs={{0,1},{1,0},{2,3},{3,2},{4,5},{5,4},{6,7},{7,6},{8,9},{9,8},{10,11... | collective-permute-start | bytes 9437192 | tf_op jit(solution)/shard_map/ppermute | solution.py:32
  398.7 23.7 %collective-permute-start.67 = (bf16[384,1024]{1,0:T(8,128)(2,1)S(1)}, bf16[384,1024]{1,0:T(8,128)(2,1)S(1)}, u32[]{:S(2)}, u32[]{:S(2)}) collective-permute-start(bf16[384,1024]{1,0:T(8,128)(2,1)S(1)} %get-tuple-element.39), channel_id=1, source_target_pairs={{2,18},{3,19},{28,12},{29,13}} | collective-permute-start | bytes 2359304 | tf_op jit(solution)/shard_map/ppermute | solution.py:32
  400.4 22.5 %collective-permute-start.68 = (bf16[384,1024]{1,0:T(8,128)(2,1)S(1)}, bf16[384,1024]{1,0:T(8,128)(2,1)S(1)}, u32[]{:S(2)}, u32[]{:S(2)}) collective-permute-start(bf16[384,1024]{1,0:T(8,128)(2,1)S(1)} %get-tuple-element.35), channel_id=1, source_target_pairs={{6,20},{7,21},{8,26},{9,27},{14,28},{15,29},{16,2},{17,3},{22,4},{... | collective-permute-start | bytes 2359304 | tf_op jit(solution)/shard_map/ppermute | solution.py:32
  408.6 25.8 %collective-permute-start.70 = (bf16[384,1024]{1,0:T(8,128)(2,1)S(1)}, bf16[384,1024]{1,0:T(8,128)(2,1)S(1)}, u32[]{:S(2)}, u32[]{:S(2)}) collective-permute-start(bf16[384,1024]{1,0:T(8,128)(2,1)S(1)} %get-tuple-element.38), channel_id=1, source_target_pairs={{0,18},{1,19},{30,12},{31,13}} | collective-permute-start | bytes 2359304 | tf_op jit(solution)/shard_map/ppermute | solution.py:32
  (34 other events, 431.5 us)

commit v2 on v0

v2 whole, which is shorter than its diff:
```python
import jax
import jax.numpy as jnp
from jax import lax
from jax.experimental import pallas as pl
from jax.experimental.pallas import tpu as pltpu
from jax.sharding import PartitionSpec as P

AXES = ("sec", "row", "col")


def pick(array, index):
    return lax.dynamic_index_in_dim(array, index, 0, keepdims=False)


def make_body(shape):
    secs, rows, cols = (shape[axis] for axis in AXES)
    mates = secs * cols // rows
    lanes = cols // mates
    swaps = secs == lanes
    sizes = (secs, lanes)
    steps = [(ds, dy) for dy in range(lanes) for ds in range(secs) if ds or dy]

    def send(value, route, name):
        pairs = []
        for s in range(secs):
            for r in range(rows):
                for y in range(lanes):
                    for k in range(mates):
                        to = route(s, r, y, k)
                        if to is not None:
                            t, q, v, m = to
                            source = (s * rows + r) * cols + y * mates + k
                            pairs.append((source, (t * rows + q) * cols + v * mates + m))
        with jax.named_scope(name):
            return lax.ppermute(value, AXES, pairs)

    def to_mate(value, step, name):
        return send(value, lambda s, r, y, k: (s, r, y, (k + step) % mates), name)

    def to_plane(value, phase, step, name):
        def route(s, r, y, k):
            along_sec = phase == (1 if swaps and k % 2 else 0)
            if along_sec:
                return ((s + step) % secs, r, y, k)
            return (s, r, (y + step) % lanes, k)

        return send(value, route, name)

    free = pl.CostEstimate(flops=0, bytes_accessed=0, transcendentals=0)
    params = pltpu.CompilerParams(vmem_limit_bytes=40 * 2**20)

    def scale(factor, inverse):
        _, tile, depth = factor.shape
        full, width = inverse.shape
        chunk = tile // rows

        def kernel(factor_ref, inverse_ref, out_ref):
            out_ref[...] = jnp.dot(
                jnp.concatenate([factor_ref[i] for i in range(rows)], 1),
                inverse_ref[...],
                preferred_element_type=jnp.float32,
            ).astype(out_ref.dtype)

        return pl.pallas_call(
            kernel,
            out_shape=jax.ShapeDtypeStruct((tile, width), factor.dtype),
            grid=(tile // chunk,),
            in_specs=[
                pl.BlockSpec((rows, chunk, depth), lambda i: (0, i, 0)),
                pl.BlockSpec((full, width), lambda i: (0, 0)),
            ],
            out_specs=pl.BlockSpec((chunk, width), lambda i: (i, 0)),
            compiler_params=params,
            cost_estimate=free,
        )(factor, inverse)

    def product(held, scaleds, first, count, piece, kind):
        tile, width = scaleds[0].shape

        def kernel(*refs):
            left, right, out_ref = refs[:mates], refs[mates:-1], refs[-1]
            total = jnp.dot(left[0][...], right[0][...], preferred_element_type=jnp.float32)
            for step in range(1, mates):
                total += jnp.dot(
                    left[step][...], right[step][...], preferred_element_type=jnp.float32
                )
            out_ref[...] = total.astype(out_ref.dtype)

        offset = first // piece
        return pl.pallas_call(
            kernel,
            out_shape=jax.ShapeDtypeStruct((count, width), kind),
            grid=(count // piece,),
            in_specs=[pl.BlockSpec((piece, tile), lambda i: (i + offset, 0))] * mates
            + [pl.BlockSpec((tile, width), lambda i: (0, 0))] * mates,
            out_specs=pl.BlockSpec((piece, width), lambda i: (i, 0)),
            compiler_params=params,
            cost_estimate=free,
        )(*held, *scaleds)

    def update(meta, total, lefts, own, came):
        n1, piece, width = lefts[0].shape
        height, tile = total.shape
        n_left = len(lefts) * n1
        operands = [*lefts, own, *came]

        def kernel(meta_ref, total_ref, *refs):
            out_ref, left_buf, right_buf, left_sem, right_sem = refs[-5:]
            refs = list(refs[:-5])
            take = lambda n: [refs.pop(0) for _ in range(n)]
            left, (own_ref,) = take(len(lefts)), take(1)
            arrived = take(len(came))
            gap, mate = meta_ref[0], meta_ref[1]
            at = 2 + n_left + rows

            def left_copy(i):
                source = left[i // n1].at[i % n1]
                return pltpu.make_async_copy(source, left_buf.at[meta_ref[2 + i]], left_sem.at[i])

            def right_copy(j, source, place):
                rows_at = pl.ds(pl.multiple_of(place * piece, piece), piece)
                return pltpu.make_async_copy(source, right_buf.at[rows_at], right_sem.at[j])

            @pl.when(pl.program_id(0) == 0)
            def _():
                for j in range(rows):
                    place = meta_ref[2 + n_left + j]

                    @pl.when(gap == 0)
                    def _():
                        source = left[j // n1].at[j % n1]
                        right_copy(j, source, meta_ref[2 + j] - mate * rows).start()

                    @pl.when(gap != 0)
                    def _():
                        source = arrived[j - 1] if j else own_ref.at[meta_ref[at]]
                        right_copy(j, source, place).start()

                for i in range(n_left):
                    left_copy(i).start()
                for j in range(rows):
                    right_copy(j, left[0].at[0], 0).wait()
                for i in range(n_left):
                    left_copy(i).wait()

            out_ref[...] = total_ref[...] + lax.dot_general(
                left_buf[pl.program_id(0)],
                right_buf[...],
                (((1,), (1,)), ((), ())),
                preferred_element_type=jnp.float32,
            )

        block = pl.BlockSpec((piece, tile), lambda i, meta_ref: (i, 0))
        return pl.pallas_call(
            kernel,
            out_shape=jax.ShapeDtypeStruct(total.shape, total.dtype),
            grid_spec=pltpu.PrefetchScalarGridSpec(
                num_scalar_prefetch=1,
                grid=(n_left,),
                in_specs=[block] + [pl.BlockSpec(memory_space=pl.ANY)] * len(operands),
                out_specs=block,
                scratch_shapes=[
                    pltpu.VMEM((n_left, piece, width), jnp.bfloat16),
                    pltpu.VMEM((tile, width), jnp.bfloat16),
                    pltpu.SemaphoreType.DMA((n_left,)),
                    pltpu.SemaphoreType.DMA((rows,)),
                ],
            ),
            compiler_params=params,
            cost_estimate=pl.CostEstimate(
                flops=2 * height * tile * width,
                bytes_accessed=8 * height * tile + 2 * width * (height + tile),
                transcendentals=0,
            ),
        )(meta, total, *operands)

    def body(held_inverse, factor_panels, block_inverses, covariance):
        panels, tile, depth = factor_panels.shape
        sec, row = lax.axis_index("sec"), lax.axis_index("row")
        lane, mate = lax.axis_index("col") // mates, lax.axis_index("col") % mates
        block = sec * lanes + lane
        piece = tile // (secs * lanes)
        n1, n2 = sizes

        def first_second(mate):
            if not swaps:
                return sec, lane
            odd = mate % 2 == 1
            return jnp.where(odd, lane, sec), jnp.where(odd, sec, lane)

        def piece_of(mate, one, two):
            if not swaps:
                return one * lanes + two
            return jnp.where(mate % 2 == 1, two * lanes + one, one * lanes + two)

        def fence(*values):
            return lax.optimization_barrier(values)

        halves = held_inverse.reshape(mates, secs * lanes, piece, tile)

        def share(step):
            target = (mate + step) % mates
            half = pick(halves, target)
            one, two = first_second(target)
            return jnp.concatenate(
                [
                    pick(half, piece_of(target, (one + a) % n1, (two + b) % n2))
                    for a in range(n1)
                    for b in range(n2)
                ]
            )

        def whole_inverse(stack, name):
            part_rows = stack[None]
            for phase, size in enumerate(sizes):
                kept = part_rows
                for step in range(1, size):
                    moved = to_plane(kept, phase, step, f"{name}_plane{phase}")
                    part_rows = jnp.concatenate([part_rows, moved])
            kept = part_rows
            for step in range(1, mates):
                part_rows = jnp.concatenate([part_rows, to_mate(kept, step, f"{name}_swap")])
            ordered = []
            for q in range(rows):
                for k in range(mates):
                    one, two = first_second(k)
                    at_one, at_two = q // lanes, q % lanes
                    if swaps and k % 2:
                        at_one, at_two = at_two, at_one
                    index = (one - at_one) % n1 + (two - at_two) % n2 * n1
                    ordered.append(pick(part_rows, (mate - k) % mates * rows + index))
            return jnp.stack(ordered, 1).reshape(rows * depth, -1)

        def sum_first(panel, factor, inverse, *held):
            scaled = scale(factor, inverse)
            scaleds = [scaled]
            scaleds += [to_mate(scaled, step, f"scaled{panel}_swap") for step in range(1, mates)]
            each = n2 * piece
            sent = product(held, scaleds, each, (n1 - 1) * each, piece, jnp.bfloat16)
            sent = sent.reshape(n1 - 1, n2, piece, -1)
            received = [
                to_plane(sent[step - 1], 0, step, f"sum{panel}_first") for step in range(1, n1)
            ]
            half_sum = product(held, scaleds, 0, each, piece, jnp.float32).reshape(n2, piece, -1)
            for value in received:
                half_sum = half_sum + value
            return half_sum

        def sum_second(panel, half_sum):
            whole_sum = half_sum[0]
            for step in range(1, n2):
                part = half_sum[step].astype(jnp.bfloat16)
                whole_sum = whole_sum + to_plane(part, 1, step, f"sum{panel}_second")
            return whole_sum.astype(jnp.bfloat16)

        def ring(panel, own):
            return jnp.stack([own] + [to_plane(own, 0, a, f"ring{panel}_first") for a in range(1, n1)])

        def ring_rest(panel, pair):
            lefts = [pair] + [to_plane(pair, 1, b, f"ring{panel}_second") for b in range(1, n2)]
            return lefts + [
                to_mate(value, step, f"ring{panel}_swap")
                for step in range(1, mates)
                for value in lefts
            ]

        def to_columns(panel, gathered):
            came = []
            for ds, dy in steps:
                target = (sec + ds) % secs * lanes + (lane + dy) % lanes

                def route(s, r, y, k):
                    v, w = (s + ds) % secs, (y + dy) % lanes
                    return (v, r, w, k) if r != v * lanes + w else None

                value = pick(gathered, target)
                came.append(send(value, route, f"column{panel}_{ds}{dy}"))
            return came

        places = []
        for step in range(mates):
            source = (mate - step) % mates
            one, two = first_second(source)
            for b in range(n2):
                for a in range(n1):
                    place = piece_of(source, (one - a) % n1, (two - b) % n2)
                    places.append(source * rows + place)
        places += [
            (sec - ds) % secs * lanes + (lane - dy) % lanes for ds, dy in [(0, 0)] + steps
        ]
        meta = jnp.stack([row - block, mate, *places, block]).astype(jnp.int32)
        always = (row + rows) // rows == 1

        def together(function, *values):
            shapes = jax.eval_shape(function, *values)
            zeros = lambda *_: jax.tree.map(lambda x: jnp.zeros(x.shape, x.dtype), shapes)
            return lax.cond(always, function, zeros, *values)

        part = depth // (mates * rows)
        group = block * mates + mate
        own_rows = lax.dynamic_slice_in_dim(block_inverses, group * part, part, 1)

        def prepare(own_rows, *shares):
            stack = lax.all_gather(own_rows, "row")
            held = [to_mate(value, step + 1, "held_swap") for step, value in enumerate(shares)]
            return [whole_inverse(stack[:, p], f"inverse{p}") for p in range(panels)], held

        shares = [share(step) for step in range(mates)]
        factors = {0: lax.all_gather(factor_panels[0], "row")}
        inverses, swapped = together(prepare, own_rows, *shares[1:])
        held = [shares[0]] + swapped

        total, owns, moved, lefts = covariance, {}, {}, {}
        for now in range(panels + 2):
            state = fence(factors, inverses, held, total, owns, moved, lefts)
            factors, inverses, held, total, owns, moved, lefts = state
            if now + 1 < panels:
                ahead, factors[now] = fence(factor_panels[now + 1], factors[now])
                factors[now + 1] = lax.all_gather(ahead, "row")
            if 0 <= now - 1 < panels:
                moved[now - 1] = lax.all_gather(owns[now - 1], "row")

            def work(factor, held, inverse, own, total, lefts, moved):
                following = None
                if own is not None:
                    pair = ring(now - 1, own)
                if factor is not None:
                    following = sum_first(now, factor, inverse, *held)
                if lefts is not None:
                    came = to_columns(now - 2, moved)
                    if own is not None:
                        pair, came = fence(pair, came)
                if own is not None:
                    own = ring_rest(now - 1, pair)
                if factor is not None:
                    following = sum_second(now, following)
                if lefts is not None:
                    total = update(meta, total, lefts, moved, came)
                return following, own, total if lefts is not None else None

            operands = (
                factors.get(now),
                held if now < panels else None,
                inverses[now] if now < panels else None,
                owns.get(now - 1),
                total if now >= 2 else None,
                lefts.get(now - 2),
                moved.get(now - 2),
            )
            step = together if now < panels + 1 else lambda function, *values: function(*values)
            following, around, latest = step(work, *operands)
            if following is not None:
                owns[now] = following
            if around is not None:
                lefts[now - 1] = around
            if latest is not None:
                total = latest
        return total

    return body


def solution(mesh):
    in_specs = (
        P("row", ("sec", "col")),
        P(None, ("sec", "col"), "row"),
        P(None, "row", None),
        P("row", ("sec", "col")),
    )
    out_specs = P("row", ("sec", "col"))
    return jax.shard_map(
        make_body(dict(mesh.shape)), mesh=mesh, in_specs=in_specs, out_specs=out_specs, check_vma=False
    )
```

time: 930 us -> 386 us (0.42)
  waiting for transfers between devices: 813 us -> 185 us
  Pallas kernels: 0 us -> 84.5 us
  matrix products: 83.8 us -> 0 us
  starting transfers between devices: 0.74 us -> 35.8 us
  blocking collectives: 0 us -> 23.9 us
  local copies, waits for them, and re-layouts: 1.63 us -> 25.2 us
    reduce_scatter x4 -> x0, waiting for transfers between devices: 389 us -> none  [the longest x2 219 us: body(): lax.psum_scatter(partial_value, 'row', scatter_dimension=1, tiled=True)]
    psum x1 -> x0, waiting for transfers between devices: 223 us -> none  [from_root(): return lax.psum(jnp.where(mine, x, jnp.zeros_like(x)), axis)]
    all_gather x4, waiting for transfers between devices: 200 us -> 12.8 us  [the longest x1 12.8 us: body(): factors[now + 1] = lax.all_gather(ahead, 'row')]
    ppermute x0 -> x27, waiting for transfers between devices: none -> 173 us  [send(): return lax.ppermute(value, AXES, pairs)]
    pallas_call x0 -> x8, Pallas kernels: none -> 84.5 us  [the longest x2 46.2 us: update(): pl.pallas_call(kernel, out_shape=jax.ShapeDtypeStruct(total.shape, total....]
    dot_general x6 -> x0, matrix products: 83.8 us -> none  [the longest x2 41.6 us: body(): lax.dot_general(inverse, column_block, (((1,), (1,)), ((), ())), preferre...]
    ppermute x0 -> x27, starting transfers between devices: none -> 35.7 us  [send(): return lax.ppermute(value, AXES, pairs)]
    all_gather x0 -> x1, blocking collectives: none -> 23.9 us  [prepare(): stack = lax.all_gather(own_rows, 'row')]
  transfers between devices with their start and end apart: 9 -> 31, of which waited for: 9 -> 19; matrix products, arithmetic and copies ran while one was open for 5% -> 9% of each run, Pallas kernels for 0% -> 16%
where the time goes in v2:
time: 386 us; the launch traced here: 385 us
  waiting for transfers between devices  185 us (48%)
  Pallas kernels  84.5 us (22%)
  starting transfers between devices  35.8 us (9%)
  local copies, waits for them, and re-layouts  25.2 us (7%)
  blocking collectives  23.9 us (6%)
  other arithmetic  15.9 us (4%)
  between operations  13.9 us (4%)
    ppermute x27, waiting for transfers between devices, send(): return lax.ppermute(value, AXES, pairs)  173 us
    pallas_call x2, Pallas kernels, update(): pl.pallas_call(kernel, out_shape=jax.ShapeDtypeStruct(total.shape, total....  46.2 us
    ppermute x27, starting transfers between devices, send(): return lax.ppermute(value, AXES, pairs)  35.7 us
    pallas_call x4, Pallas kernels, product(): pl.pallas_call(kernel, out_shape=jax.ShapeDtypeStruct((count, width), kin...  26 us
    all_gather x1, blocking collectives, prepare(): stack = lax.all_gather(own_rows, 'row')  23.9 us
    all_gather x1, waiting for transfers between devices, body(): factors[now + 1] = lax.all_gather(ahead, 'row')  12.8 us
    pallas_call x2, Pallas kernels, scale(): pl.pallas_call(kernel, out_shape=jax.ShapeDtypeStruct((tile, width), fact...  12.3 us
    cond x43, local copies, waits for them, and re-layouts  9.75 us
  transfers between devices with their start and end apart: 31, of which 19 were waited for; matrix products, arithmetic and copies ran while one was open for 9% of the time, Pallas kernels for 16%

profile of v2, /device:TPU:0, one launch (start us, length us, event | category | flops | bytes accessed | tf_op | source)
XLA Modules:
  0.0 385.3 jit_solution(10499904424602144576)
XLA Ops:
  6.5 2.6 fusion.6
  9.6 5.4 %dynamic-slice_bitcast_fusion.6 = (bf16[384,1536]{1,0:T(8,128)(2,1)S(1)}, bf16[384,1536]{1,0:T(8,128)(2,1)S(1)}, bf16[384,1536]{1,0:T(8,128)(2,1)S(1)}, bf16[384...) fusion(bf16[2,4,384,1536]{3,2,1,0:T(8,128)(2,1)} %bitcast.121, ...), kind=kLoop, calls=%fused_computation.47 | loop fusion | bytes 18874408 | tf_op jit(solution)/shard_map/jit(dynamic_index_in_dim)/squeeze | solution.py:12
  14.9 2.3 pad_maximum_fusion.8
  17.3 63.5 %conditional.4 = (bf16[1024,1024]{1,0:T(8,128)(2,1)}, bf16[1024,1024]{1,0:T(8,128)(2,1)}, bf16[1536,1536]{1,0:T(8,128)(2,1)}) conditional(s32[]{:T(128)} %convert_element_type.32, () %tuple.45, (s32[]{:T(128)}, bf16[2,256,1024]{2,1,0:T(8,128)(2,1)}, s32[]{:T(128)}, s32[]{:T(128)}, s32[]{:T(128)}, /*index=5*/bf16[1536,1536]{1,0:T(8,128)(2,1)}, (), ...), branch_computations={%region_0.1_spmd, %region_1.2_spmd} | conditional | flops 8913017 | bytes 71173968 | solution.py:297
  18.6 23.9 %all-gather = bf16[8,32,1024]{2,1,0:T(8,128)(2,1)S(1)} all-gather(bf16[2,32,1024]{2,1,0:T(8,128)(2,1)S(1)} %constant_dynamic-slice_fusion), channel_id=2, replica_groups=mesh['sec'=2,'row'=4,'col'=4] {'row'}, dimensions={0}, use_global_device_ids=true | all-gather | bytes 655360 | tf_op jit(solution)/shard_map/cond/branch_1_fun/all_gather | solution.py:304
  42.6 1.6 collective-permute-start
  44.7 4.3 %collective-permute-done = bf16[1,4,32,1024]{3,2,1,0:T(8,128)(2,1)S(1)} collective-permute-done((bf16[1,4,32,1024]{3,2,1,0:T(8,128)(2,1)S(1)}, bf16[1,4,32,1024]{3,2,1,0:T(8,128)(2,1)S(1)}, u32[]{:S(2)}, u32[]{:S(2)}) %collective-permute-start) | collective-permute-done | bytes 262176 | tf_op jit(solution)/shard_map/cond/branch_1_fun/inverse0_plane0/ppermute | solution.py:35
  49.1 1.6 collective-permute-start.1
  50.7 3.1 collective-permute-done.3
  53.8 1.6 collective-permute-start.4
  55.4 2.9 collective-permute-done.1
  59.5 4.5 %collective-permute-done.4 = bf16[2,4,32,1024]{3,2,1,0:T(8,128)(2,1)S(1)} collective-permute-done((bf16[2,4,32,1024]{3,2,1,0:T(8,128)(2,1)S(1)}, bf16[2,4,32,1024]{3,2,1,0:T(8,128)(2,1)S(1)}, u32[]{:S(2)}, u32[]{:S(2)}) %collective-permute-start.4) | collective-permute-done | bytes 524320 | tf_op jit(solution)/shard_map/cond/branch_1_fun/inverse1_plane1/ppermute | solution.py:35
  65.3 1.8 pad_maximum_fusion
  80.8 3.6 pad_maximum_fusion.9
  84.5 51.9 %conditional.5 = (bf16[384,1024]{1,0:T(8,128)(2,1)S(1)}) conditional(s32[]{:T(128)} %convert_element_type.32, () %tuple.49, (bf16[4,1536,256]{2,1,0:T(8,128)(2,1)}, bf16[1024,1024]{1,0:T(8,128)(2,1)}, bf16[1536,1536]{1,0:T(8,128)(2,1)}, bf16[1536,1536]{1,0:T(8,128)(2,1)}) %tuple.50), branch_computations={%region_2.3_spmd, %region_3.4_spmd} | conditional | flops 2752512 | bytes 53477532 | solution.py:297
  84.5 6.1 %branch_1_fun.7.refs_2_ = bf16[1536,1024]{1,0:T(8,128)(2,1)S(1)} custom-call(bf16[4,1536,256]{2,1,0:T(8,128)(2,1)} %get-tuple-element.75.factor_ref, bf16[1024,1024]{1,0:T(8,128)(2,1)} %get-tuple-element.76.inverse_ref), custom_call_target="tpu_custom_call" | custom-call | tf_op jit(solution)/shard_map/cond/branch_1_fun/pallas_call | solution.py:64
  90.9 5.5 %collective-permute-done.7.refs_3_ = bf16[1536,1024]{1,0:T(8,128)(2,1)S(1)} collective-permute-done((bf16[1536,1024]{1,0:T(8,128)(2,1)S(1)}, bf16[1536,1024]{1,0:T(8,128)(2,1)S(1)}, u32[]{:S(2)}, u32[]{:S(2)}) %collective-permute-start.7) | collective-permute-done | bytes 3145760 | tf_op jit(solution)/shard_map/cond/branch_1_fun/scaled0_swap/ppermute | solution.py:35
  96.4 6.5 %branch_1_fun.9 = bf16[768,1024]{1,0:T(8,128)(2,1)S(1)} custom-call(bf16[1536,1536]{1,0:T(8,128)(2,1)S(1)} %copy-done.1, bf16[1536,1536]{1,0:T(8,128)(2,1)} %get-tuple-element.74.refs_1_, bf16[1536,1024]{1,0:T(8,128)(2,1)S(1)} %branch_1_fun.7.refs_2_, bf16[1536,1024]{1,0:T(8,128)(2,1)S(1)} %collective-permute-done.7.refs_3_), custom_call_target="tpu_custom_call" | custom-call | tf_op jit(solution)/shard_map/cond/branch_1_fun/pallas_call | solution.py:90
  104.5 6.5 %branch_1_fun.8 = f32[768,1024]{1,0:T(8,128)S(1)} custom-call(bf16[1536,1536]{1,0:T(8,128)(2,1)S(1)} %copy-done.1, bf16[1536,1536]{1,0:T(8,128)(2,1)} %get-tuple-element.74.refs_1_, bf16[1536,1024]{1,0:T(8,128)(2,1)S(1)} %branch_1_fun.7.refs_2_, bf16[1536,1024]{1,0:T(8,128)(2,1)S(1)} %collective-permute-done.7.refs_3_), custom_call_target="tpu_custom_call" | custom-call | tf_op jit(solution)/shard_map/cond/branch_1_fun/pallas_call | solution.py:90
  111.0 12.4 %collective-permute-done.8 = bf16[2,384,1024]{2,1,0:T(8,128)(2,1)S(1)} collective-permute-done((bf16[2,384,1024]{2,1,0:T(8,128)(2,1)S(1)}, bf16[2,384,1024]{2,1,0:T(8,128)(2,1)S(1)}, u32[]{:S(2)}, u32[]{:S(2)}) %collective-permute-start.8) | collective-permute-done | bytes 1572896 | tf_op jit(solution)/shard_map/cond/branch_1_fun/sum0_first/ppermute | solution.py:35
  124.0 1.6 collective-permute-start.9
  125.6 10.5 %collective-permute-done.9 = bf16[384,1024]{1,0:T(8,128)(2,1)S(1)} collective-permute-done((bf16[384,1024]{1,0:T(8,128)(2,1)S(1)}, bf16[384,1024]{1,0:T(8,128)(2,1)S(1)}, u32[]{:S(2)}, u32[]{:S(2)}) %collective-permute-start.9) | collective-permute-done | bytes 786464 | tf_op jit(solution)/shard_map/cond/branch_1_fun/sum0_second/ppermute | solution.py:35
  136.4 12.8 %all-gather.11.cloned.1.call-done = bf16[6144,256]{1,0:T(8,128)(2,1)} async-done(((bf16[1536,256]{1,0:T(8,128)(2,1)}), bf16[6144,256]{1,0:T(8,128)(2,1)}) %all-gather.11.cloned.1.call-update) | async-done | bytes 3145744 | tf_op jit(solution)/shard_map/all_gather | solution.py:319
  149.2 70.6 %conditional.6 = (bf16[384,1024]{1,0:T(8,128)(2,1)S(1)}, bf16[2,384,1024]{2,1,0:T(8,128)(2,1)}, bf16[2,384,1024]{2,1,0:T(8,128)(2,1)}, bf16[2,384,1024]{2,1,0:T(8,128)(2,1)}, bf16[2,384,1024]{2,1,0:T(8,128)(2,1)}) conditional(s32[]{:T(128)} %convert_element_type.32, () %tuple.52, (bf16[4,1536,256]{2,1,0:T(8,128)(2,1)}, bf16[1024,1024]{1,0:T(8,128)(2,1)}, ...), branch_computations={%region_4.5_spmd, %region_5.6_spmd} | conditional | flops 3538944 | bytes 77070736 | solution.py:297
  149.5 6.2 %branch_1_fun.10.refs_2_ = bf16[1536,1024]{1,0:T(8,128)(2,1)S(1)} custom-call(bf16[4,1536,256]{2,1,0:T(8,128)(2,1)} %get-tuple-element.79.factor_ref, bf16[1024,1024]{1,0:T(8,128)(2,1)} %get-tuple-element.80.inverse_ref), custom_call_target="tpu_custom_call" | custom-call | tf_op jit(solution)/shard_map/cond/branch_1_fun/pallas_call | solution.py:64
  157.3 10.5 %collective-permute-done.13 = bf16[384,1024]{1,0:T(8,128)(2,1)S(1)} collective-permute-done((bf16[384,1024]{1,0:T(8,128)(2,1)S(1)}, bf16[384,1024]{1,0:T(8,128)(2,1)S(1)}, u32[]{:S(2)}, u32[]{:S(2)}) %collective-permute-start.13) | collective-permute-done | bytes 786464 | tf_op jit(solution)/shard_map/cond/branch_1_fun/ring0_first/ppermute | solution.py:35
  170.6 6.5 %branch_1_fun.12 = bf16[768,1024]{1,0:T(8,128)(2,1)S(1)} custom-call(bf16[1536,1536]{1,0:T(8,128)(2,1)S(1)} %bitcast.119, bf16[1536,1536]{1,0:T(8,128)(2,1)} %get-tuple-element.78.refs_1_, bf16[1536,1024]{1,0:T(8,128)(2,1)S(1)} %branch_1_fun.10.refs_2_, bf16[1536,1024]{1,0:T(8,128)(2,1)S(1)} %collective-permute-done.10.refs_3_), custom_call_target="tpu_custom_call" | custom-call | tf_op jit(solution)/shard_map/cond/branch_1_fun/pallas_call | solution.py:90
  178.6 21.7 %collective-permute-done.14 = bf16[2,384,1024]{2,1,0:T(8,128)(2,1)} collective-permute-done((bf16[2,384,1024]{2,1,0:T(8,128)(2,1)}, bf16[2,384,1024]{2,1,0:T(8,128)(2,1)}, u32[]{:S(2)}, u32[]{:S(2)}) %collective-permute-start.14) | collective-permute-done | bytes 1572896 | tf_op jit(solution)/shard_map/cond/branch_1_fun/ring0_second/ppermute | solution.py:35
  200.3 6.5 %branch_1_fun.11 = f32[768,1024]{1,0:T(8,128)S(1)} custom-call(bf16[1536,1536]{1,0:T(8,128)(2,1)S(1)} %bitcast.119, bf16[1536,1536]{1,0:T(8,128)(2,1)} %get-tuple-element.78.refs_1_, bf16[1536,1024]{1,0:T(8,128)(2,1)S(1)} %branch_1_fun.10.refs_2_, bf16[1536,1024]{1,0:T(8,128)(2,1)S(1)} %collective-permute-done.10.refs_3_), custom_call_target="tpu_custom_call" | custom-call | tf_op jit(solution)/shard_map/cond/branch_1_fun/pallas_call | solution.py:90
  209.0 10.5 %collective-permute-done.12 = bf16[384,1024]{1,0:T(8,128)(2,1)S(1)} collective-permute-done((bf16[384,1024]{1,0:T(8,128)(2,1)S(1)}, bf16[384,1024]{1,0:T(8,128)(2,1)S(1)}, u32[]{:S(2)}, u32[]{:S(2)}) %collective-permute-start.12) | collective-permute-done | bytes 786464 | tf_op jit(solution)/shard_map/cond/branch_1_fun/sum1_second/ppermute | solution.py:35
  221.2 91.3 %conditional.7 = (bf16[2,384,1024]{2,1,0:T(8,128)(2,1)}, bf16[2,384,1024]{2,1,0:T(8,128)(2,1)}, bf16[2,384,1024]{2,1,0:T(8,128)(2,1)}, bf16[2,384,1024]{2,1,0:T(8,128)(2,1)}, f32[3072,1536]{1,0:T(8,128)}) conditional(s32[]{:T(128)} %convert_element_type.32, () %tuple.44, (bf16[384,1024]{1,0:T(8,128)(2,1)}, s32[]{:T(128)}, s32[]{:T(128)}, ...), branch_computations={%region_6.7_spmd, %region_7.8_spmd} | conditional | flops 9664462848 | bytes 102237144 | solution.py:297
  221.2 2.4 collective-permute-start.17
  223.6 1.9 dynamic-slice_bitcast_fusion
  225.5 2.3 collective-permute-start.18
  227.8 3.4 collective-permute-start.19
  231.2 3.3 collective-permute-start.20
  234.5 3.5 collective-permute-done.17
  239.4 15.4 %collective-permute-done.18.refs_5_ = bf16[384,1024]{1,0:T(8,128)(2,1)S(1)} collective-permute-done((bf16[384,1024]{1,0:T(8,128)(2,1)S(1)}, bf16[384,1024]{1,0:T(8,128)(2,1)S(1)}, u32[]{:S(2)}, u32[]{:S(2)}) %collective-permute-start.18) | collective-permute-done | bytes 786464 | tf_op jit(solution)/shard_map/cond/branch_1_fun/column0_10/ppermute | solution.py:35
  254.8 10.5 %collective-permute-done.19.refs_6_ = bf16[384,1024]{1,0:T(8,128)(2,1)S(1)} collective-permute-done((bf16[384,1024]{1,0:T(8,128)(2,1)S(1)}, bf16[384,1024]{1,0:T(8,128)(2,1)S(1)}, u32[]{:S(2)}, u32[]{:S(2)}) %collective-permute-start.19) | collective-permute-done | bytes 786464 | tf_op jit(solution)/shard_map/cond/branch_1_fun/column0_01/ppermute | solution.py:35
  265.3 3.3 collective-permute-done.20.refs_7_
  269.1 20.2 %collective-permute-done.21 = bf16[2,384,1024]{2,1,0:T(8,128)(2,1)} collective-permute-done((bf16[2,384,1024]{2,1,0:T(8,128)(2,1)}, bf16[2,384,1024]{2,1,0:T(8,128)(2,1)}, u32[]{:S(2)}, u32[]{:S(2)}) %collective-permute-start.21) | collective-permute-done | bytes 1572896 | tf_op jit(solution)/shard_map/cond/branch_1_fun/ring1_second/ppermute | solution.py:35
  289.3 23.1 %branch_1_fun.13 = f32[3072,1536]{1,0:T(8,128)} custom-call(s32[15]{0:T(128)S(1)} %get-tuple-element.87.meta_ref, f32[3072,1536]{1,0:T(8,128)} %get-tuple-element.88.total_ref, bf16[2,384,1024]{2,1,0:T(8,128)(2,1)} %get-tuple-element.89.refs_0_, bf16[2,384,1024]{2,1,0:T(8,128)(2,1)} %get-tuple-element.90.refs_1_, ...), custom_call_target="tpu_custom_call" | custom-call | flops 9663676416 | bytes 47185920 | tf_op jit(solution)/shard_map/cond/branch_1_fun/pallas_call | solution.py:154
  312.5 2.0 dynamic-slice_bitcast_fusion.11
  314.5 3.7 collective-permute-start.24
  318.2 3.4 collective-permute-start.25
  323.0 13.0 %collective-permute-done.24.refs_5_ = bf16[384,1024]{1,0:T(8,128)(2,1)S(1)} collective-permute-done((bf16[384,1024]{1,0:T(8,128)(2,1)S(1)}, bf16[384,1024]{1,0:T(8,128)(2,1)S(1)}, u32[]{:S(2)}, u32[]{:S(2)}) %collective-permute-start.24) | collective-permute-done | bytes 786464 | tf_op jit(solution)/shard_map/column1_10/ppermute | solution.py:35
  336.0 19.6 %collective-permute-done.25.refs_6_ = bf16[384,1024]{1,0:T(8,128)(2,1)S(1)} collective-permute-done((bf16[384,1024]{1,0:T(8,128)(2,1)S(1)}, bf16[384,1024]{1,0:T(8,128)(2,1)S(1)}, u32[]{:S(2)}, u32[]{:S(2)}) %collective-permute-start.25) | collective-permute-done | bytes 786464 | tf_op jit(solution)/shard_map/column1_01/ppermute | solution.py:35
  355.6 23.1 %shard_map.47 = f32[3072,1536]{1,0:T(8,128)} custom-call(s32[15]{0:T(128)S(1)} %stack.135.meta_ref, f32[3072,1536]{1,0:T(8,128)} %get-tuple-element.170.total_ref, bf16[2,384,1024]{2,1,0:T(8,128)(2,1)} %get-tuple-element.171.refs_0_, bf16[2,384,1024]{2,1,0:T(8,128)(2,1)} %get-tuple-element.172.refs_1_, bf16[2,384,1024]{2,1,0:T(8,128)(2,1)} %get-tuple-element.173.refs_2_, ...), custom_call_target="tpu_custom_call" | custom-call | flops 9663676416 | bytes 47185920 | tf_op jit(solution)/shard_map/pallas_call | solution.py:154
  (106 shorter events, 33.6 us)
Async XLA Ops:
  6.5 77.9 %all-gather.9.cloned.1.call-start = ((), (), s32[]{:S(2)}) async-start(), calls=%async_computation | async-start | bytes 3932160 | tf_op jit(solution)/shard_map/all_gather | solution.py:309
  9.2 140.0 %all-gather.11.cloned.1.call-start = ((), (), s32[]{:S(2)}) async-start(), calls=%async_computation.1 | async-start | bytes 3932160 | tf_op jit(solution)/shard_map/all_gather | solution.py:319
  17.3 63.5 %collective-permute-start.6 = (bf16[1536,1536]{1,0:T(8,128)(2,1)}, bf16[1536,1536]{1,0:T(8,128)(2,1)}, u32[]{:S(2)}, u32[]{:S(2)}) collective-permute-start(bf16[1536,1536]{1,0:T(8,128)(2,1)} %get-tuple-element.72), channel_id=1, source_target_pairs={{0,1},{1,0},{2,3},{3,2},{4,5},{5,4},{6,7},{7,6},{8,9},{9,8},{10,11... | collective-permute-start | bytes 14155784 | tf_op jit(solution)/shard_map/cond/branch_1_fun/held_swap/ppermute | solution.py:35
  42.6 16.9 %copy-start.9 = (bf16[1,4,32,1024]{3,2,1,0:T(8,128)(2,1)}, bf16[1,4,32,1024]{3,2,1,0:T(8,128)(2,1)S(1)}, u32[]{:S(2)}) copy-start(bf16[1,4,32,1024]{3,2,1,0:T(8,128)(2,1)S(1)} %get-tuple-element.185) | copy-start | bytes 786436 | tf_op jit(solution)/shard_map/cond
  42.6 21.4 %copy-start.7 = (bf16[1,4,32,1024]{3,2,1,0:T(8,128)(2,1)}, bf16[1,4,32,1024]{3,2,1,0:T(8,128)(2,1)S(1)}, u32[]{:S(2)}) copy-start(bf16[1,4,32,1024]{3,2,1,0:T(8,128)(2,1)S(1)} %get-tuple-element.184) | copy-start | bytes 786436 | tf_op jit(solution)/shard_map/cond
  42.6 6.4 %collective-permute-start = (bf16[1,4,32,1024]{3,2,1,0:T(8,128)(2,1)S(1)}, bf16[1,4,32,1024]{3,2,1,0:T(8,128)(2,1)S(1)}, u32[]{:S(2)}, u32[]{:S(2)}) collective-permute-start(bf16[1,4,32,1024]{3,2,1,0:T(8,128)(2,1)S(1)} %get-tuple-element.185), channel_id=1, source_target_pairs={{0,16},{1,3},{2,18},{3,1},{4,20},{5,7},{6,22},{7,5},{8,24},{9,11},... | collective-permute-start | bytes 786440 | tf_op jit(solution)/shard_map/cond/branch_1_fun/inverse0_plane0/ppermute | solution.py:35
  44.1 9.6 %collective-permute-start.3 = (bf16[1,4,32,1024]{3,2,1,0:T(8,128)(2,1)S(1)}, bf16[1,4,32,1024]{3,2,1,0:T(8,128)(2,1)S(1)}, u32[]{:S(2)}, u32[]{:S(2)}) collective-permute-start(bf16[1,4,32,1024]{3,2,1,0:T(8,128)(2,1)S(1)} %get-tuple-element.184), channel_id=1, source_target_pairs={{0,16},{1,3},{2,18},{3,1},{4,20},{5,7},{6,22},{7,5},{8,24},{9,11},... | collective-permute-start | bytes 786440 | tf_op jit(solution)/shard_map/cond/branch_1_fun/inverse1_plane0/ppermute | solution.py:35
  49.0 10.4 %copy-start.12 = (bf16[1,4,32,1024]{3,2,1,0:T(8,128)(2,1)}, bf16[1,4,32,1024]{3,2,1,0:T(8,128)(2,1)S(1)}, u32[]{:S(2)}) copy-start(bf16[1,4,32,1024]{3,2,1,0:T(8,128)(2,1)S(1)} %collective-permute-done) | copy-start | bytes 786436 | tf_op jit(solution)/shard_map/cond
  49.1 9.2 %collective-permute-start.1 = (bf16[2,4,32,1024]{3,2,1,0:T(8,128)(2,1)S(1)}, bf16[2,4,32,1024]{3,2,1,0:T(8,128)(2,1)S(1)}, u32[]{:S(2)}, u32[]{:S(2)}) collective-permute-start(bf16[2,4,32,1024]{3,2,1,0:T(8,128)(2,1)S(1)} %pad_maximum_fusion.4), channel_id=1, source_target_pairs={{0,2},{1,17},{2,0},{3,19},{4,6},{5,21},{6,4},{7,23},{8,10},{9,25},... | collective-permute-start | bytes 1572872 | tf_op jit(solution)/shard_map/cond/branch_1_fun/inverse0_plane1/ppermute | solution.py:35
  53.8 11.4 %copy-start.10 = (bf16[1,4,32,1024]{3,2,1,0:T(8,128)(2,1)}, bf16[1,4,32,1024]{3,2,1,0:T(8,128)(2,1)S(1)}, u32[]{:S(2)}) copy-start(bf16[1,4,32,1024]{3,2,1,0:T(8,128)(2,1)S(1)} %collective-permute-done.3) | copy-start | bytes 786436 | tf_op jit(solution)/shard_map/cond
  53.8 10.1 %collective-permute-start.4 = (bf16[2,4,32,1024]{3,2,1,0:T(8,128)(2,1)S(1)}, bf16[2,4,32,1024]{3,2,1,0:T(8,128)(2,1)S(1)}, u32[]{:S(2)}, u32[]{:S(2)}) collective-permute-start(bf16[2,4,32,1024]{3,2,1,0:T(8,128)(2,1)S(1)} %pad_maximum_fusion.5), channel_id=1, source_target_pairs={{0,2},{1,17},{2,0},{3,19},{4,6},{5,21},{6,4},{7,23},{8,10},{9,25},... | collective-permute-start | bytes 1572872 | tf_op jit(solution)/shard_map/cond/branch_1_fun/inverse1_plane1/ppermute | solution.py:35
  58.3 6.8 %copy-start.15 = (bf16[2,4,32,1024]{3,2,1,0:T(8,128)(2,1)}, bf16[2,4,32,1024]{3,2,1,0:T(8,128)(2,1)S(1)}, u32[]{:S(2)}) copy-start(bf16[2,4,32,1024]{3,2,1,0:T(8,128)(2,1)S(1)} %collective-permute-done.1) | copy-start | bytes 1572868 | tf_op jit(solution)/shard_map/cond
  59.5 5.9 %collective-permute-start.2 = (bf16[4,4,32,1024]{3,2,1,0:T(8,128)(2,1)}, bf16[4,4,32,1024]{3,2,1,0:T(8,128)(2,1)}, u32[]{:S(2)}, u32[]{:S(2)}) collective-permute-start(bf16[4,4,32,1024]{3,2,1,0:T(8,128)(2,1)} %pad_maximum_fusion.2), channel_id=1, source_target_pairs={{0,1},{1,0},{2,3},{3,2},{4,5},{5,4},{6,7},{7,6},{8,9},{9,8},{10,11... | collective-permute-start | bytes 3145736 | tf_op jit(solution)/shard_map/cond/branch_1_fun/inverse0_swap/ppermute | solution.py:35
  63.9 1.2 copy-start.13
  65.1 3.0 collective-permute-start.5
  65.3 2.8 copy-start.8
  65.3 2.8 copy-start.11
  65.3 2.8 copy-start.14
  84.4 135.5 %all-gather.13.cloned.1.call-start = ((), (), s32[]{:S(2)}) async-start(), calls=%async_computation.2 | async-start | bytes 3932160 | tf_op jit(solution)/shard_map/all_gather | solution.py:321
  84.5 11.9 %copy-start.1 = (bf16[1536,1536]{1,0:T(8,128)(2,1)S(1)}, bf16[1536,1536]{1,0:T(8,128)(2,1)}, u32[]{:S(2)}) copy-start(bf16[1536,1536]{1,0:T(8,128)(2,1)} %get-tuple-element.73.refs_0_) | copy-start | bytes 14155780 | tf_op jit(solution)/shard_map/cond
  90.7 5.7 %collective-permute-start.7 = (bf16[1536,1024]{1,0:T(8,128)(2,1)S(1)}, bf16[1536,1024]{1,0:T(8,128)(2,1)S(1)}, u32[]{:S(2)}, u32[]{:S(2)}) collective-permute-start(bf16[1536,1024]{1,0:T(8,128)(2,1)S(1)} %branch_1_fun.7.refs_2_), channel_id=1, source_target_pairs={{0,1},{1,0},{2,3},{3,2},{4,5},{5,4},{6,7},{7,6},{8,9},{9,8},{10,11... | collective-permute-start | bytes 9437192 | tf_op jit(solution)/shard_map/cond/branch_1_fun/scaled0_swap/ppermute | solution.py:35
  102.9 20.5 %collective-permute-start.8 = (bf16[2,384,1024]{2,1,0:T(8,128)(2,1)S(1)}, bf16[2,384,1024]{2,1,0:T(8,128)(2,1)S(1)}, u32[]{:S(2)}, u32[]{:S(2)}) collective-permute-start(bf16[2,384,1024]{2,1,0:T(8,128)(2,1)S(1)} %bitcast.117), channel_id=1, source_target_pairs={{0,16},{1,3},{2,18},{3,1},{4,20},{5,7},{6,22},{7,5},{8,24},{9,11},... | collective-permute-start | bytes 4718600 | tf_op jit(solution)/shard_map/cond/branch_1_fun/sum0_first/ppermute | solution.py:35
  124.0 12.1 %collective-permute-start.9 = (bf16[384,1024]{1,0:T(8,128)(2,1)S(1)}, bf16[384,1024]{1,0:T(8,128)(2,1)S(1)}, u32[]{:S(2)}, u32[]{:S(2)}) collective-permute-start(bf16[384,1024]{1,0:T(8,128)(2,1)S(1)} %fusion.2), channel_id=1, source_target_pairs={{0,2},{1,17},{2,0},{3,19},{4,6},{5,21},{6,4},{7,23},{8,10},{9,25},... | collective-permute-start | bytes 2359304 | tf_op jit(solution)/shard_map/cond/branch_1_fun/sum0_second/ppermute | solution.py:35
  136.4 12.8 %copy-start.5 = (bf16[384,1024]{1,0:T(8,128)(2,1)}, bf16[384,1024]{1,0:T(8,128)(2,1)S(1)}, u32[]{:S(2)}) copy-start(bf16[384,1024]{1,0:T(8,128)(2,1)S(1)} %get-tuple-element.230) | copy-start | bytes 2359300
  149.2 163.3 %all-gather.15.cloned.1.call-start = ((), (), s32[]{:S(2)}) async-start(), calls=%async_computation.3 | async-start | bytes 3932160 | tf_op jit(solution)/shard_map/all_gather | solution.py:321
  149.4 21.1 %slice-start = ((s8[4718592]{0:T(1024)(128)(4,1)}), s8[4194304]{0:T(1024)(128)(4,1)S(1)}, s32[]{:S(2)}) async-start(s8[4718592]{0:T(1024)(128)(4,1)} %bitcast.118), calls=%async_computation.4 | async-start | bytes 8388608 | tf_op jit(solution)/shard_map/cond
  149.4 6.3 %copy-start.6 = (bf16[384,1024]{1,0:T(8,128)(2,1)S(1)}, bf16[384,1024]{1,0:T(8,128)(2,1)}, u32[]{:S(2)}) copy-start(bf16[384,1024]{1,0:T(8,128)(2,1)} %get-tuple-element.81) | copy-start | bytes 2359300 | tf_op jit(solution)/shard_map/cond
  149.4 21.1 %slice-start.1 = ((s8[4718592]{0:T(1024)(128)(4,1)}), s8[524288]{0:T(1024)(128)(4,1)S(1)}, s32[]{:S(2)}) async-start(s8[4718592]{0:T(1024)(128)(4,1)} %bitcast.118), calls=%async_computation.5 | async-start | bytes 1048576 | tf_op jit(solution)/shard_map/cond
  155.6 14.9 %collective-permute-start.10 = (bf16[1536,1024]{1,0:T(8,128)(2,1)S(1)}, bf16[1536,1024]{1,0:T(8,128)(2,1)S(1)}, u32[]{:S(2)}, u32[]{:S(2)}) collective-permute-start(bf16[1536,1024]{1,0:T(8,128)(2,1)S(1)} %branch_1_fun.10.refs_2_), channel_id=1, source_target_pairs={{0,1},{1,0},{2,3},{3,2},{4,5},{5,4},{6,7},{7,6},{8,9},{9,8},{10,11... | collective-permute-start | bytes 9437192 | tf_op jit(solution)/shard_map/cond/branch_1_fun/scaled1_swap/ppermute | solution.py:35
  155.7 12.1 %collective-permute-start.13 = (bf16[384,1024]{1,0:T(8,128)(2,1)S(1)}, bf16[384,1024]{1,0:T(8,128)(2,1)S(1)}, u32[]{:S(2)}, u32[]{:S(2)}) collective-permute-start(bf16[384,1024]{1,0:T(8,128)(2,1)S(1)} %copy-done.6), channel_id=1, source_target_pairs={{0,16},{1,3},{2,18},{3,1},{4,20},{5,7},{6,22},{7,5},{8,24},{9,11},... | collective-permute-start | bytes 2359304 | tf_op jit(solution)/shard_map/cond/branch_1_fun/ring0_first/ppermute | solution.py:35
  169.1 31.2 %collective-permute-start.14 = (bf16[2,384,1024]{2,1,0:T(8,128)(2,1)}, bf16[2,384,1024]{2,1,0:T(8,128)(2,1)}, u32[]{:S(2)}, u32[]{:S(2)}) collective-permute-start(bf16[2,384,1024]{2,1,0:T(8,128)(2,1)} %pad_maximum_fusion.6), channel_id=1, source_target_pairs={{0,2},{1,17},{2,0},{3,19},{4,6},{5,21},{6,4},{7,23},{8,10},{9,25},... | collective-permute-start | bytes 4718600 | tf_op jit(solution)/shard_map/cond/branch_1_fun/ring0_second/ppermute | solution.py:35
  177.1 29.7 %collective-permute-start.11 = (bf16[2,384,1024]{2,1,0:T(8,128)(2,1)S(1)}, bf16[2,384,1024]{2,1,0:T(8,128)(2,1)S(1)}, u32[]{:S(2)}, u32[]{:S(2)}) collective-permute-start(bf16[2,384,1024]{2,1,0:T(8,128)(2,1)S(1)} %bitcast.116), channel_id=1, source_target_pairs={{0,16},{1,3},{2,18},{3,1},{4,20},{5,7},{6,22},{7,5},{8,24},{9,11},... | collective-permute-start | bytes 4718600 | tf_op jit(solution)/shard_map/cond/branch_1_fun/sum1_first/ppermute | solution.py:35
  178.6 41.2 %collective-permute-start.15 = (bf16[2,384,1024]{2,1,0:T(8,128)(2,1)}, bf16[2,384,1024]{2,1,0:T(8,128)(2,1)}, u32[]{:S(2)}, u32[]{:S(2)}) collective-permute-start(bf16[2,384,1024]{2,1,0:T(8,128)(2,1)} %pad_maximum_fusion.6), channel_id=1, source_target_pairs={{0,1},{1,0},{2,3},{3,2},{4,5},{5,4},{6,7},{7,6},{8,9},{9,8},{10,11... | collective-permute-start | bytes 4718600 | tf_op jit(solution)/shard_map/cond/branch_1_fun/ring0_swap/ppermute | solution.py:35
  200.3 19.5 %collective-permute-start.16 = (bf16[2,384,1024]{2,1,0:T(8,128)(2,1)}, bf16[2,384,1024]{2,1,0:T(8,128)(2,1)}, u32[]{:S(2)}, u32[]{:S(2)}) collective-permute-start(bf16[2,384,1024]{2,1,0:T(8,128)(2,1)} %collective-permute-done.14), channel_id=1, source_target_pairs={{0,1},{1,0},{2,3},{3,2},{4,5},{5,4},{6,7},{7,6},{8,9},{9,8},{10,11... | collective-permute-start | bytes 4718600 | tf_op jit(solution)/shard_map/cond/branch_1_fun/ring0_swap/ppermute | solution.py:35
  207.5 12.1 %collective-permute-start.12 = (bf16[384,1024]{1,0:T(8,128)(2,1)S(1)}, bf16[384,1024]{1,0:T(8,128)(2,1)S(1)}, u32[]{:S(2)}, u32[]{:S(2)}) collective-permute-start(bf16[384,1024]{1,0:T(8,128)(2,1)S(1)} %fusion.5), channel_id=1, source_target_pairs={{0,2},{1,17},{2,0},{3,19},{4,6},{5,21},{6,4},{7,23},{8,10},{9,25},... | collective-permute-start | bytes 2359304 | tf_op jit(solution)/shard_map/cond/branch_1_fun/sum1_second/ppermute | solution.py:35
  221.2 16.9 %collective-permute-start.17 = (bf16[384,1024]{1,0:T(8,128)(2,1)}, bf16[384,1024]{1,0:T(8,128)(2,1)S(1)}, u32[]{:S(2)}, u32[]{:S(2)}) collective-permute-start(bf16[384,1024]{1,0:T(8,128)(2,1)} %get-tuple-element.82), channel_id=1, source_target_pairs={{0,16},{1,3},{2,18},{3,1},{4,20},{5,7},{6,22},{7,5},{8,24},{9,11},... | collective-permute-start | bytes 2359304 | tf_op jit(solution)/shard_map/cond/branch_1_fun/ring1_first/ppermute | solution.py:35
  223.6 14.5 %copy-start.4 = (bf16[384,1024]{1,0:T(8,128)(2,1)S(1)}, bf16[384,1024]{1,0:T(8,128)(2,1)}, u32[]{:S(2)}) copy-start(bf16[384,1024]{1,0:T(8,128)(2,1)} %get-tuple-element.82) | copy-start | bytes 2359300 | tf_op jit(solution)/shard_map/cond
  225.5 63.8 %copy-start.2 = (bf16[4,384,1024]{2,1,0:T(8,128)(2,1)S(1)}, bf16[4,384,1024]{2,1,0:T(8,128)(2,1)}, u32[]{:S(2)}) copy-start(bf16[4,384,1024]{2,1,0:T(8,128)(2,1)} %get-tuple-element.83.refs_4_) | copy-start | bytes 9437188 | tf_op jit(solution)/shard_map/cond
  225.5 29.3 %collective-permute-start.18 = (bf16[384,1024]{1,0:T(8,128)(2,1)S(1)}, bf16[384,1024]{1,0:T(8,128)(2,1)S(1)}, u32[]{:S(2)}, u32[]{:S(2)}) collective-permute-start(bf16[384,1024]{1,0:T(8,128)(2,1)S(1)} %get-tuple-element.190), channel_id=1, source_target_pairs={{0,16},{1,17},{2,18},{3,19},{4,20},{5,21},{6,22},{7,23},{10,26},{1... | collective-permute-start | bytes 2359304 | tf_op jit(solution)/shard_map/cond/branch_1_fun/column0_10/ppermute | solution.py:35
  227.8 37.4 %collective-permute-start.19 = (bf16[384,1024]{1,0:T(8,128)(2,1)S(1)}, bf16[384,1024]{1,0:T(8,128)(2,1)S(1)}, u32[]{:S(2)}, u32[]{:S(2)}) collective-permute-start(bf16[384,1024]{1,0:T(8,128)(2,1)S(1)} %get-tuple-element.189), channel_id=1, source_target_pairs={{0,2},{1,3},{6,4},{7,5},{8,10},{9,11},{10,8},{11,9},{12,14},{13,15... | collective-permute-start | bytes 2359304 | tf_op jit(solution)/shard_map/cond/branch_1_fun/column0_01/ppermute | solution.py:35
  231.2 37.4 %collective-permute-start.20 = (bf16[384,1024]{1,0:T(8,128)(2,1)S(1)}, bf16[384,1024]{1,0:T(8,128)(2,1)S(1)}, u32[]{:S(2)}, u32[]{:S(2)}) collective-permute-start(bf16[384,1024]{1,0:T(8,128)(2,1)S(1)} %get-tuple-element.188), channel_id=1, source_target_pairs={{0,18},{1,19},{2,16},{3,17},{4,22},{5,23},{6,20},{7,21},{8,26},{9,... | collective-permute-start | bytes 2359304 | tf_op jit(solution)/shard_map/cond/branch_1_fun/column0_11/ppermute | solution.py:35
  268.6 20.7 %collective-permute-start.21 = (bf16[2,384,1024]{2,1,0:T(8,128)(2,1)}, bf16[2,384,1024]{2,1,0:T(8,128)(2,1)}, u32[]{:S(2)}, u32[]{:S(2)}) collective-permute-start(bf16[2,384,1024]{2,1,0:T(8,128)(2,1)} %pad_maximum_fusion.7), channel_id=1, source_target_pairs={{0,2},{1,17},{2,0},{3,19},{4,6},{5,21},{6,4},{7,23},{8,10},{9,25},... | collective-permute-start | bytes 4718600 | tf_op jit(solution)/shard_map/cond/branch_1_fun/ring1_second/ppermute | solution.py:35
  269.1 43.3 %collective-permute-start.22 = (bf16[2,384,1024]{2,1,0:T(8,128)(2,1)}, bf16[2,384,1024]{2,1,0:T(8,128)(2,1)}, u32[]{:S(2)}, u32[]{:S(2)}) collective-permute-start(bf16[2,384,1024]{2,1,0:T(8,128)(2,1)} %pad_maximum_fusion.7), channel_id=1, source_target_pairs={{0,1},{1,0},{2,3},{3,2},{4,5},{5,4},{6,7},{7,6},{8,9},{9,8},{10,11... | collective-permute-start | bytes 4718600 | tf_op jit(solution)/shard_map/cond/branch_1_fun/ring1_swap/ppermute | solution.py:35
  289.3 23.2 %collective-permute-start.23 = (bf16[2,384,1024]{2,1,0:T(8,128)(2,1)}, bf16[2,384,1024]{2,1,0:T(8,128)(2,1)}, u32[]{:S(2)}, u32[]{:S(2)}) collective-permute-start(bf16[2,384,1024]{2,1,0:T(8,128)(2,1)} %collective-permute-done.21), channel_id=1, source_target_pairs={{0,1},{1,0},{2,3},{3,2},{4,5},{5,4},{6,7},{7,6},{8,9},{9,8},{10,11... | collective-permute-start | bytes 4718600 | tf_op jit(solution)/shard_map/cond/branch_1_fun/ring1_swap/ppermute | solution.py:35
  312.5 43.1 %copy-start = (bf16[1536,1024]{1,0:T(8,128)(2,1)S(1)}, bf16[1536,1024]{1,0:T(8,128)(2,1)}, u32[]{:S(2)}) copy-start(bf16[1536,1024]{1,0:T(8,128)(2,1)} %all-gather.15.cloned.1.call-done) | copy-start | bytes 9437188
  314.5 21.5 %collective-permute-start.24 = (bf16[384,1024]{1,0:T(8,128)(2,1)S(1)}, bf16[384,1024]{1,0:T(8,128)(2,1)S(1)}, u32[]{:S(2)}, u32[]{:S(2)}) collective-permute-start(bf16[384,1024]{1,0:T(8,128)(2,1)S(1)} %get-tuple-element.201), channel_id=1, source_target_pairs={{0,16},{1,17},{2,18},{3,19},{4,20},{5,21},{6,22},{7,23},{10,26},{1... | collective-permute-start | bytes 2359304 | tf_op jit(solution)/shard_map/column1_10/ppermute | solution.py:35
  318.2 37.4 %collective-permute-start.25 = (bf16[384,1024]{1,0:T(8,128)(2,1)S(1)}, bf16[384,1024]{1,0:T(8,128)(2,1)S(1)}, u32[]{:S(2)}, u32[]{:S(2)}) collective-permute-start(bf16[384,1024]{1,0:T(8,128)(2,1)S(1)} %get-tuple-element.200), channel_id=1, source_target_pairs={{0,2},{1,3},{6,4},{7,5},{8,10},{9,11},{10,8},{11,9},{12,14},{13,15... | collective-permute-start | bytes 2359304 | tf_op jit(solution)/shard_map/column1_01/ppermute | solution.py:35
  321.6 34.0 %collective-permute-start.26 = (bf16[384,1024]{1,0:T(8,128)(2,1)S(1)}, bf16[384,1024]{1,0:T(8,128)(2,1)S(1)}, u32[]{:S(2)}, u32[]{:S(2)}) collective-permute-start(bf16[384,1024]{1,0:T(8,128)(2,1)S(1)} %get-tuple-element.199), channel_id=1, source_target_pairs={{0,18},{1,19},{2,16},{3,17},{4,22},{5,23},{6,20},{7,21},{8,26},{9,... | collective-permute-start | bytes 2359304 | tf_op jit(solution)/shard_map/column1_11/ppermute | solution.py:35
  (1 other events, 0.9 us)
Sparse Core Ops, SparseCore 0:
  9.3 74.4 all-gather.8
  85.4 63.7 all-gather.10
  150.7 62.1 all-gather.12
  220.9 63.1 all-gather.14

commit v3 on v2

v3 whole, which is shorter than its diff:
```python
import jax
import jax.numpy as jnp
from jax import lax
from jax.experimental import pallas as pl
from jax.experimental.pallas import tpu as pltpu
from jax.sharding import PartitionSpec as P

AXES = ("sec", "row", "col")
HALVES = 2


def pick(array, index):
    return lax.dynamic_index_in_dim(array, index, 0, keepdims=False)


def make_body(shape):
    secs, rows, cols = (shape[axis] for axis in AXES)
    mates = secs * cols // rows
    lanes = cols // mates
    swaps = secs == lanes
    sizes = (secs, lanes)
    steps = [(ds, dy) for dy in range(lanes) for ds in range(secs) if ds or dy]

    def send(value, route, name):
        pairs = []
        for s in range(secs):
            for r in range(rows):
                for y in range(lanes):
                    for k in range(mates):
                        to = route(s, r, y, k)
                        if to is not None:
                            t, q, v, m = to
                            source = (s * rows + r) * cols + y * mates + k
                            pairs.append((source, (t * rows + q) * cols + v * mates + m))
        with jax.named_scope(name):
            return lax.ppermute(value, AXES, pairs)

    def to_mate(value, step, name):
        return send(value, lambda s, r, y, k: (s, r, y, (k + step) % mates), name)

    def to_plane(value, phase, step, name):
        def route(s, r, y, k):
            along_sec = phase == (1 if swaps and k % 2 else 0)
            if along_sec:
                return ((s + step) % secs, r, y, k)
            return (s, r, (y + step) % lanes, k)

        return send(value, route, name)

    params = pltpu.CompilerParams(vmem_limit_bytes=40 * 2**20)

    def reorder(order, array):
        _, planes, height, width = array.shape
        count = order.shape[0]

        def kernel(order_ref, in_ref, out_ref):
            for plane in range(planes):
                out_ref[plane, 0] = in_ref[0, plane]

        return pl.pallas_call(
            kernel,
            out_shape=jax.ShapeDtypeStruct((planes, count, height, width), array.dtype),
            grid_spec=pltpu.PrefetchScalarGridSpec(
                num_scalar_prefetch=1,
                grid=(count,),
                in_specs=[
                    pl.BlockSpec((1, planes, height, width), lambda i, order_ref: (order_ref[i], 0, 0, 0))
                ],
                out_specs=pl.BlockSpec((planes, 1, height, width), lambda i, order_ref: (0, i, 0, 0)),
            ),
            compiler_params=params,
            cost_estimate=pl.CostEstimate(
                flops=0, bytes_accessed=4 * count * planes * height * width, transcendentals=0
            ),
        )(order, array)

    def scale(factor, inverse):
        _, tile, depth = factor.shape
        full, width = inverse.shape
        chunk = tile // rows

        def kernel(factor_ref, inverse_ref, out_ref):
            out_ref[...] = jnp.dot(
                jnp.concatenate([factor_ref[i] for i in range(rows)], 1),
                inverse_ref[...],
                preferred_element_type=jnp.float32,
            ).astype(out_ref.dtype)

        return pl.pallas_call(
            kernel,
            out_shape=jax.ShapeDtypeStruct((tile, width), factor.dtype),
            grid=(tile // chunk,),
            in_specs=[
                pl.BlockSpec((rows, chunk, depth), lambda i: (0, i, 0)),
                pl.BlockSpec((full, width), lambda i: (0, 0)),
            ],
            out_specs=pl.BlockSpec((chunk, width), lambda i: (i, 0)),
            compiler_params=params,
            cost_estimate=pl.CostEstimate(
                flops=2 * tile * full * width,
                bytes_accessed=2 * (tile * full + full * width + tile * width),
                transcendentals=0,
            ),
        )(factor, inverse)

    def product(held, scaleds, first, count, piece, kind):
        tile, width = scaleds[0].shape

        def kernel(*refs):
            left, right, out_ref = refs[:mates], refs[mates:-1], refs[-1]
            total = jnp.dot(left[0][...], right[0][...], preferred_element_type=jnp.float32)
            for step in range(1, mates):
                total += jnp.dot(
                    left[step][...], right[step][...], preferred_element_type=jnp.float32
                )
            out_ref[...] = total.astype(out_ref.dtype)

        offset = first // piece
        return pl.pallas_call(
            kernel,
            out_shape=jax.ShapeDtypeStruct((count, width), kind),
            grid=(count // piece,),
            in_specs=[pl.BlockSpec((piece, tile), lambda i: (i + offset, 0))] * mates
            + [pl.BlockSpec((tile, width), lambda i: (0, 0))] * mates,
            out_specs=pl.BlockSpec((piece, width), lambda i: (i, 0)),
            compiler_params=params,
            cost_estimate=pl.CostEstimate(
                flops=2 * mates * count * tile * width,
                bytes_accessed=2 * mates * tile * (count + width) + 4 * count * width,
                transcendentals=0,
            ),
        )(*held, *scaleds)

    def update(meta, total, lefts, rights):
        n1, piece, width = lefts[0].shape
        height, tile = total.shape
        n_left, sub = len(lefts) * n1, piece // HALVES
        span = tile // HALVES
        halves = list(rights)
        sources = [[gathered, *came] for gathered, _, came in rights.values()]
        operands = [*lefts, *[value for group in sources for value in group]]

        def kernel(meta_ref, total_ref, *refs):
            left, out_ref, left_buf, right_buf, left_sem, right_sem = refs[: len(lefts)], *refs[-5:]
            gap, mate, own = meta_ref[0], meta_ref[1], meta_ref[2]
            base = 3

            def left_copy(i, h):
                source = left[i // n1].at[i % n1, pl.ds(h * sub, sub)]
                start = meta_ref[base + i] + h * span
                to = pl.ds(pl.multiple_of(start, sub), sub)
                return pltpu.make_async_copy(source, left_buf.at[to], left_sem.at[start // sub])

            def right_copy(j, at, source, place):
                to = pl.ds(pl.multiple_of(place + at * span, sub), sub)
                return pltpu.make_async_copy(source, right_buf.at[to], right_sem.at[j, at])

            @pl.when(pl.program_id(0) == 0)
            def _():
                for at, h in enumerate(halves):
                    gathered, *came = refs[len(lefts) + at * rows :][:rows]
                    lines = pl.ds(rights[h][1], sub)
                    for j in range(rows):

                        @pl.when(gap == 0)
                        def _():
                            source = left[j // n1].at[j % n1, pl.ds(h * sub, sub)]
                            right_copy(j, at, source, meta_ref[base + j] - mate * tile).start()

                        @pl.when(gap != 0)
                        def _():
                            source = came[j - 1].at[lines] if j else gathered.at[own, lines]
                            right_copy(j, at, source, meta_ref[base + n_left + j]).start()

                for i in range(n_left):
                    for h in range(HALVES):
                        left_copy(i, h).start()
                for at in range(len(halves)):
                    for j in range(rows):
                        right_copy(j, at, left[0].at[0, pl.ds(0, sub)], 0).wait()

            for h in range(HALVES):
                at = pl.program_id(0) * HALVES + h
                pltpu.make_async_copy(
                    left[0].at[0, pl.ds(0, sub)], left_buf.at[pl.ds(0, sub)], left_sem.at[at]
                ).wait()
            lines = pl.ds(pl.multiple_of(pl.program_id(0) * piece, piece), piece)
            out_ref[...] = total_ref[...] + lax.dot_general(
                left_buf[lines],
                right_buf[...],
                (((1,), (1,)), ((), ())),
                preferred_element_type=jnp.float32,
            )

        first = halves[0]
        columns = span * len(halves)
        block = pl.BlockSpec((piece, columns), lambda i, meta_ref: (i, first))
        return pl.pallas_call(
            kernel,
            out_shape=jax.ShapeDtypeStruct(total.shape, total.dtype),
            grid_spec=pltpu.PrefetchScalarGridSpec(
                num_scalar_prefetch=1,
                grid=(n_left,),
                in_specs=[block] + [pl.BlockSpec(memory_space=pl.ANY)] * len(operands),
                out_specs=block,
                scratch_shapes=[
                    pltpu.VMEM((height, width), jnp.bfloat16),
                    pltpu.VMEM((columns, width), jnp.bfloat16),
                    pltpu.SemaphoreType.DMA((n_left * HALVES,)),
                    pltpu.SemaphoreType.DMA((rows, len(halves))),
                ],
            ),
            input_output_aliases={} if len(halves) == HALVES else {1: 0},
            compiler_params=params,
            cost_estimate=pl.CostEstimate(
                flops=2 * height * columns * width,
                bytes_accessed=8 * height * columns + 2 * width * (height + columns),
                transcendentals=0,
            ),
        )(meta, total, *operands)

    def body(held_inverse, factor_panels, block_inverses, covariance):
        panels, tile, depth = factor_panels.shape
        sec, row = lax.axis_index("sec"), lax.axis_index("row")
        lane, mate = lax.axis_index("col") // mates, lax.axis_index("col") % mates
        block = sec * lanes + lane
        piece = tile // (secs * lanes)
        n1, n2 = sizes

        def first_second(mate):
            if not swaps:
                return sec, lane
            odd = mate % 2 == 1
            return jnp.where(odd, lane, sec), jnp.where(odd, sec, lane)

        def piece_of(mate, one, two):
            if not swaps:
                return one * lanes + two
            return jnp.where(mate % 2 == 1, two * lanes + one, one * lanes + two)

        def fence(*values):
            return lax.optimization_barrier(values)

        sub = piece // HALVES
        blocks = held_inverse.reshape(mates * HALVES * rows, 1, sub, tile)

        def share(blocks, step):
            target = (mate + step) % mates
            one, two = first_second(target)
            order = [
                (target * HALVES + h) * rows + piece_of(target, (one + a) % n1, (two + b) % n2)
                for a in range(n1)
                for b in range(n2)
                for h in range(HALVES)
            ]
            return reorder(jnp.stack(order).astype(jnp.int32), blocks).reshape(tile, tile)

        def whole_inverse(stack, name):
            part_rows = stack[None]
            for phase, size in enumerate(sizes):
                kept = part_rows
                for step in range(1, size):
                    moved = to_plane(kept, phase, step, f"{name}_plane{phase}")
                    part_rows = jnp.concatenate([part_rows, moved])
            kept = part_rows
            for step in range(1, mates):
                part_rows = jnp.concatenate([part_rows, to_mate(kept, step, f"{name}_swap")])
            ordered = []
            for q in range(rows):
                for k in range(mates):
                    one, two = first_second(k)
                    at_one, at_two = q // lanes, q % lanes
                    if swaps and k % 2:
                        at_one, at_two = at_two, at_one
                    index = (one - at_one) % n1 + (two - at_two) % n2 * n1
                    ordered.append((mate - k) % mates * rows + index)
            order = jnp.stack(ordered).astype(jnp.int32)
            return reorder(order, part_rows).reshape(rows * depth, -1)

        def sum_first(panel, factor, inverse, around, *held):
            scaled = scale(factor, inverse)
            scaleds = [scaled]
            scaleds += [to_mate(scaled, step, f"scaled{panel}_swap") for step in range(1, mates)]
            each = n2 * piece
            sent = product(held, scaleds, each, (n1 - 1) * each, piece, jnp.bfloat16)
            sent, around = fence(sent.reshape(n1 - 1, n2, piece, -1), around)
            received = [
                to_plane(sent[step - 1], 0, step, f"sum{panel}_first") for step in range(1, n1)
            ]
            half_sum = product(held, scaleds, 0, each, piece, jnp.float32).reshape(n2, piece, -1)
            for value in received:
                half_sum = half_sum + value
            return half_sum, around

        def sum_second(panel, half_sum):
            whole_sum = half_sum[0]
            for step in range(1, n2):
                part = half_sum[step].astype(jnp.bfloat16)
                whole_sum = whole_sum + to_plane(part, 1, step, f"sum{panel}_second")
            return whole_sum.astype(jnp.bfloat16)

        def halved(own):
            return [own[h * sub : (h + 1) * sub] for h in range(HALVES)]

        def ring(panel, own):
            return jnp.stack([own] + [to_plane(own, 0, a, f"ring{panel}_first") for a in range(1, n1)])

        def ring_rest(panel, pair):
            return [pair] + [to_plane(pair, 1, b, f"ring{panel}_second") for b in range(1, n2)]

        def ring_swap(panel, lefts):
            return lefts + [
                to_mate(value, step, f"ring{panel}_swap")
                for step in range(1, mates)
                for value in lefts
            ]

        def to_columns(name, gathered):
            came = []
            for ds, dy in steps:
                target = (sec + ds) % secs * lanes + (lane + dy) % lanes

                def route(s, r, y, k):
                    return ((s + ds) % secs, r, (y + dy) % lanes, k)

                value = pick(gathered, target)
                came.append(send(value, route, f"column{name}_{ds}{dy}"))
            return came

        places = []
        for step in range(mates):
            source = (mate - step) % mates
            one, two = first_second(source)
            for b in range(n2):
                for a in range(n1):
                    place = piece_of(source, (one - a) % n1, (two - b) % n2)
                    places.append(source * tile + place * sub)
        places += [
            ((sec - ds) % secs * lanes + (lane - dy) % lanes) * sub for ds, dy in [(0, 0)] + steps
        ]
        meta = jnp.stack([row - block, mate, block, *places]).astype(jnp.int32)
        always = (row + rows) // rows == 1

        def together(function, *values):
            shapes = jax.eval_shape(function, *values)
            zeros = lambda *_: jax.tree.map(lambda x: jnp.zeros(x.shape, x.dtype), shapes)
            return lax.cond(always, function, zeros, *values)

        part = depth // (mates * rows)
        group = block * mates + mate
        own_rows = lax.dynamic_slice_in_dim(block_inverses, group * part, part, 1)

        def prepare(own_rows, blocks):
            stack, blocks = fence(lax.all_gather(own_rows, "row"), blocks)
            shares = [share(blocks, step) for step in range(mates)]
            held = [shares[0]] + [to_mate(shares[step], step, "held_swap") for step in range(1, mates)]
            return [whole_inverse(stack[:, p], f"inverse{p}") for p in range(panels)], held

        factors = {0: lax.all_gather(factor_panels[0], "row")}
        inverses, held = together(prepare, own_rows, blocks)

        def both(gathered, came):
            return {h: (gathered, h * sub, came) for h in range(HALVES)}

        total, owns, pairs, moved, lefts = covariance, {}, {}, {}, {}
        for now in range(panels):
            state = fence(factors, inverses, held, total, owns, pairs, moved, lefts)
            factors, inverses, held, total, owns, pairs, moved, lefts = state
            if now + 1 < panels:
                factor_panels, factors[now] = fence(factor_panels, factors[now])
                factors[now + 1] = lax.all_gather(factor_panels[now + 1], "row")
            if now >= 1:
                moved[now - 1] = lax.all_gather(owns[now - 1], "row")

            def work(factor, held, inverse, pair, total, lefts, moved):
                around = latest = None
                if pair is not None:
                    around = ring_rest(now - 1, pair)
                half_sum, around = sum_first(now, factor, inverse, around, *held)
                own = sum_second(now, half_sum)
                if lefts is not None:
                    latest = update(meta, total, lefts, both(moved, to_columns(now - 2, moved)))
                if pair is not None:
                    around = ring_swap(now - 1, around)
                if now + 1 < panels:
                    return own, ring(now, own), around, latest
                return own, halved(own), around, latest

            owns[now], pairs[now], around, latest = together(
                work,
                factors[now],
                held,
                inverses[now],
                pairs.get(now - 1),
                total if now >= 2 else None,
                lefts.get(now - 2),
                moved.get(now - 2),
            )
            if around is not None:
                lefts[now - 1] = around
            if latest is not None:
                total = latest

        own, parts, moved, lefts, total = fence(owns[panels - 1], pairs[panels - 1], moved, lefts, total)
        gathered = {0: lax.all_gather(parts[0], "row")}

        def first_work(own, value):
            came = to_columns(panels - 2, value) if value is not None else None
            return ring(panels - 1, own), came

        pair, came = together(first_work, own, moved.get(panels - 2))
        arrived = {}
        for h in range(HALVES):
            state = fence(parts, pair, moved, lefts, total, gathered, came, arrived)
            parts, pair, moved, lefts, total, gathered, came, arrived = state
            if h + 1 < HALVES:
                gathered[h + 1] = lax.all_gather(parts[h + 1], "row")
            if h == 0:

                def last_work(value, pair, total, lefts, moved, came):
                    steps_done = to_columns(f"{panels - 1}_half0", value)
                    around = ring_rest(panels - 1, pair)
                    if came is not None:
                        total = update(meta, total, lefts, both(moved, came))
                        around, total, steps_done = fence(around, total, steps_done)
                    return steps_done, ring_swap(panels - 1, around), total if came is not None else None

                arrived[0], around, latest = together(
                    last_work,
                    gathered[0],
                    pair,
                    total if panels > 1 else None,
                    lefts.get(panels - 2),
                    moved.get(panels - 2),
                    came,
                )
                if latest is not None:
                    total = latest
            else:
                arrived[h] = to_columns(f"{panels - 1}_half{h}", gathered[h])
                total = update(meta, total, around, {h - 1: (gathered[h - 1], 0, arrived[h - 1])})
        total = update(meta, total, around, {HALVES - 1: (gathered[HALVES - 1], 0, arrived[HALVES - 1])})
        return total

    return body


def solution(mesh):
    in_specs = (
        P("row", ("sec", "col")),
        P(None, ("sec", "col"), "row"),
        P(None, "row", None),
        P("row", ("sec", "col")),
    )
    out_specs = P("row", ("sec", "col"))
    return jax.shard_map(
        make_body(dict(mesh.shape)), mesh=mesh, in_specs=in_specs, out_specs=out_specs, check_vma=False
    )
```

time: 386 us -> 347 us (0.90)
  waiting for transfers between devices: 185 us -> 141 us
  Pallas kernels: 84.5 us -> 113 us
  local copies, waits for them, and re-layouts: 25.2 us -> 14.2 us
  starting transfers between devices: 35.8 us -> 29.2 us
  other arithmetic: 15.9 us -> 11.3 us
    ppermute x27 -> x30, waiting for transfers between devices: 173 us -> 141 us  [send(): return lax.ppermute(value, AXES, pairs)]
    pallas_call x0 -> x4, Pallas kernels: none -> 22 us  [reorder(): pl.pallas_call(kernel, out_shape=jax.ShapeDtypeStruct((planes, count, hei...]
    all_gather x1 -> x3, waiting for transfers between devices: 12.8 us -> 0.02 us  [the longest x1 0.02 us: body(): factors[now + 1] = lax.all_gather(factor_panels[now + 1], 'row')]
    cond x43 -> x2, local copies, waits for them, and re-layouts: 9.75 us -> 1.53 us
    ppermute x27 -> x30, starting transfers between devices: 35.7 us -> 29 us  [send(): return lax.ppermute(value, AXES, pairs)]
    concatenate x2 -> x0, other arithmetic: 5.97 us -> none  [share(): jnp.concatenate([pick(half, piece_of(target, (one + a) % n1, (two + b) %...]
    pallas_call x2 -> x3, Pallas kernels: 46.2 us -> 51.9 us  [update(): pl.pallas_call(kernel, out_shape=jax.ShapeDtypeStruct(total.shape, total....]
    squeeze x3, local copies, waits for them, and re-layouts: 9.23 us -> 4.56 us  [pick(): return lax.dynamic_index_in_dim(array, index, 0, keepdims=False)]
  transfers between devices with their start and end apart: 31 -> 35, of which waited for: 19 -> 20; matrix products, arithmetic and copies ran while one was open for 9% -> 6% of each run, Pallas kernels for 16% -> 29%
where the time goes in v3:
time: 347 us; the launch traced here: 345 us
  waiting for transfers between devices  141 us (41%)
  Pallas kernels  113 us (33%)
  starting transfers between devices  29.2 us (8%)
  blocking collectives  21.5 us (6%)
  local copies, waits for them, and re-layouts  14.2 us (4%)
  between operations  13.6 us (4%)
  other arithmetic  11.3 us (3%)
    ppermute x30, waiting for transfers between devices, send(): return lax.ppermute(value, AXES, pairs)  141 us
    pallas_call x3, Pallas kernels, update(): pl.pallas_call(kernel, out_shape=jax.ShapeDtypeStruct(total.shape, total....  51.9 us
    ppermute x30, starting transfers between devices, send(): return lax.ppermute(value, AXES, pairs)  29 us
    pallas_call x4, Pallas kernels, product(): pl.pallas_call(kernel, out_shape=jax.ShapeDtypeStruct((count, width), kin...  27.4 us
    pallas_call x4, Pallas kernels, reorder(): pl.pallas_call(kernel, out_shape=jax.ShapeDtypeStruct((planes, count, hei...  22 us
    all_gather x1, blocking collectives, prepare(): stack, blocks = fence(lax.all_gather(own_rows, 'row'), blocks)  21.5 us
    pallas_call x2, Pallas kernels, scale(): pl.pallas_call(kernel, out_shape=jax.ShapeDtypeStruct((tile, width), fact...  12 us
  transfers between devices with their start and end apart: 35, of which 20 were waited for; matrix products, arithmetic and copies ran while one was open for 6% of the time, Pallas kernels for 29%

profile of v3, /device:TPU:0, one launch (start us, length us, event | category | flops | bytes accessed | tf_op | source)
XLA Modules:
  0.0 345.2 jit_solution(3731086839768173021)
XLA Ops:
  6.5 2.1 slice.32
  8.7 69.5 %conditional.5 = (bf16[1024,1024]{1,0:T(8,128)(2,1)}, bf16[1024,1024]{1,0:T(8,128)(2,1)}, bf16[1536,1536]{1,0:T(8,128)(2,1)}, bf16[1536,1536]{1,0:T(8,128)(2,1)}) conditional(s32[]{:T(128)} %convert_element_type.33, () %tuple.57, (s32[]{:T(128)}, s32[]{:T(128)}, s32[]{:T(128)}, s32[]{:T(128)}, bf16[2,256,1024]{2,1,0:T(8,128)(2,1)}, ...), branch_computations={%region_0.1_spmd, %region_1.2_spmd} | conditional | flops 8913181 | bytes 77467024 | solution.py:347
  9.8 21.5 %all-gather = bf16[8,32,1024]{2,1,0:T(8,128)(2,1)S(1)} all-gather(bf16[2,32,1024]{2,1,0:T(8,128)(2,1)S(1)} %constant_dynamic-slice_fusion), channel_id=2, replica_groups=mesh['sec'=2,'row'=4,'col'=4] {'row'}, dimensions={0}, use_global_device_ids=true | all-gather | bytes 655360 | tf_op jit(solution)/shard_map/cond/branch_1_fun/all_gather | solution.py:354
  31.3 7.4 %branch_1_fun.14 = bf16[1,8,192,1536]{3,2,1,0:T(8,128)(2,1)} custom-call(s32[8]{0:T(128)S(1)} %stack.133.order_ref, bf16[16,1,192,1536]{3,2,1,0:T(8,128)(2,1)} %bitcast.102), custom_call_target="tpu_custom_call" | custom-call | bytes 9437184 | tf_op jit(solution)/shard_map/cond/branch_1_fun/pallas_call | solution.py:60
  40.9 4.3 %collective-permute-done.20 = bf16[1,4,32,1024]{3,2,1,0:T(8,128)(2,1)S(1)} collective-permute-done((bf16[1,4,32,1024]{3,2,1,0:T(8,128)(2,1)S(1)}, bf16[1,4,32,1024]{3,2,1,0:T(8,128)(2,1)S(1)}, u32[]{:S(2)}, u32[]{:S(2)}) %collective-permute-start.20) | collective-permute-done | bytes 262176 | tf_op jit(solution)/shard_map/cond/branch_1_fun/inverse0_plane0/ppermute | solution.py:36
  45.3 1.6 collective-permute-start.21
  48.3 1.6 collective-permute-start.24
  50.0 4.5 %collective-permute-done.21 = bf16[2,4,32,1024]{3,2,1,0:T(8,128)(2,1)S(1)} collective-permute-done((bf16[2,4,32,1024]{3,2,1,0:T(8,128)(2,1)S(1)}, bf16[2,4,32,1024]{3,2,1,0:T(8,128)(2,1)S(1)}, u32[]{:S(2)}, u32[]{:S(2)}) %collective-permute-start.21) | collective-permute-done | bytes 524320 | tf_op jit(solution)/shard_map/cond/branch_1_fun/inverse0_plane1/ppermute | solution.py:36
  55.6 4.5 %collective-permute-done.24 = bf16[2,4,32,1024]{3,2,1,0:T(8,128)(2,1)S(1)} collective-permute-done((bf16[2,4,32,1024]{3,2,1,0:T(8,128)(2,1)S(1)}, bf16[2,4,32,1024]{3,2,1,0:T(8,128)(2,1)S(1)}, u32[]{:S(2)}, u32[]{:S(2)}) %collective-permute-start.24) | collective-permute-done | bytes 524320 | tf_op jit(solution)/shard_map/cond/branch_1_fun/inverse1_plane1/ppermute | solution.py:36
  60.6 7.4 %branch_1_fun.13 = bf16[1,8,192,1536]{3,2,1,0:T(8,128)(2,1)} custom-call(s32[8]{0:T(128)S(1)} %stack.124.order_ref, bf16[16,1,192,1536]{3,2,1,0:T(8,128)(2,1)} %bitcast.103), custom_call_target="tpu_custom_call" | custom-call | bytes 9437184 | tf_op jit(solution)/shard_map/cond/branch_1_fun/pallas_call | solution.py:60
  69.5 3.6 %branch_1_fun.11 = bf16[4,8,32,1024]{3,2,1,0:T(8,128)(2,1)} custom-call(s32[8]{0:T(128)S(1)} %stack.42.order_ref, bf16[8,4,32,1024]{3,2,1,0:T(8,128)(2,1)S(1)} %pad_maximum_fusion.in_ref), custom_call_target="tpu_custom_call" | custom-call | bytes 4194304 | tf_op jit(solution)/shard_map/cond/branch_1_fun/pallas_call | solution.py:60
  74.6 3.6 %branch_1_fun.12 = bf16[4,8,32,1024]{3,2,1,0:T(8,128)(2,1)} custom-call(s32[8]{0:T(128)S(1)} %stack.42.order_ref, bf16[8,4,32,1024]{3,2,1,0:T(8,128)(2,1)S(1)} %pad_maximum_fusion.1.in_ref), custom_call_target="tpu_custom_call" | custom-call | bytes 4194304 | tf_op jit(solution)/shard_map/cond/branch_1_fun/pallas_call | solution.py:60
  78.2 2.1 slice.33
  80.3 66.5 %conditional.6 = (bf16[384,1024]{1,0:T(8,128)(2,1)}, bf16[2,384,1024]{2,1,0:T(8,128)(2,1)S(1)}) conditional(s32[]{:T(128)} %convert_element_type.33, () %tuple.61, (bf16[4,1536,256]{2,1,0:T(8,128)(2,1)}, bf16[1024,1024]{1,0:T(8,128)(2,1)}, bf16[1536,1536]{1,0:T(8,128)(2,1)}, bf16[1536,1536]{1,0:T(8,128)(2,1)}) %tuple.62), branch_computations={%region_2.3_spmd, %region_3.4_spmd} | conditional | flops 12888440832 | bytes 77594800 | solution.py:347
  80.3 6.0 %branch_1_fun.15.refs_2_ = bf16[1536,1024]{1,0:T(8,128)(2,1)S(1)} custom-call(bf16[4,1536,256]{2,1,0:T(8,128)(2,1)} %get-tuple-element.91.factor_ref, bf16[1024,1024]{1,0:T(8,128)(2,1)} %get-tuple-element.92.inverse_ref), custom_call_target="tpu_custom_call" | custom-call | flops 3221225472 | bytes 8388608 | tf_op jit(solution)/shard_map/cond/branch_1_fun/pallas_call | solution.py:89
  86.7 5.4 %collective-permute-done.refs_3_ = bf16[1536,1024]{1,0:T(8,128)(2,1)S(1)} collective-permute-done((bf16[1536,1024]{1,0:T(8,128)(2,1)S(1)}, bf16[1536,1024]{1,0:T(8,128)(2,1)S(1)}, u32[]{:S(2)}, u32[]{:S(2)}) %collective-permute-start) | collective-permute-done | bytes 3145760 | tf_op jit(solution)/shard_map/cond/branch_1_fun/scaled0_swap/ppermute | solution.py:36
  92.1 6.9 %branch_1_fun.17 = bf16[768,1024]{1,0:T(8,128)(2,1)S(1)} custom-call(bf16[1536,1536]{1,0:T(8,128)(2,1)} %get-tuple-element.89.refs_0_, bf16[1536,1536]{1,0:T(8,128)(2,1)} %get-tuple-element.90.refs_1_, bf16[1536,1024]{1,0:T(8,128)(2,1)S(1)} %branch_1_fun.15.refs_2_, bf16[1536,1024]{1,0:T(8,128)(2,1)S(1)} %collective-permute-done.refs_3_), custom_call_target="tpu_custom_call" | custom-call | flops 4831838208 | bytes 14155776 | tf_op jit(solution)/shard_map/cond/branch_1_fun/pallas_call | solution.py:119
  100.5 6.8 %branch_1_fun.16 = f32[768,1024]{1,0:T(8,128)S(1)} custom-call(bf16[1536,1536]{1,0:T(8,128)(2,1)} %get-tuple-element.89.refs_0_, bf16[1536,1536]{1,0:T(8,128)(2,1)} %get-tuple-element.90.refs_1_, bf16[1536,1024]{1,0:T(8,128)(2,1)S(1)} %branch_1_fun.15.refs_2_, bf16[1536,1024]{1,0:T(8,128)(2,1)S(1)} %collective-permute-done.refs_3_), custom_call_target="tpu_custom_call" | custom-call | flops 4831838208 | bytes 14155776 | tf_op jit(solution)/shard_map/cond/branch_1_fun/pallas_call | solution.py:119
  107.4 12.1 %collective-permute-done.1 = bf16[2,384,1024]{2,1,0:T(8,128)(2,1)S(1)} collective-permute-done((bf16[2,384,1024]{2,1,0:T(8,128)(2,1)S(1)}, bf16[2,384,1024]{2,1,0:T(8,128)(2,1)S(1)}, u32[]{:S(2)}, u32[]{:S(2)}) %collective-permute-start.1) | collective-permute-done | bytes 1572896 | tf_op jit(solution)/shard_map/cond/branch_1_fun/sum0_first/ppermute | solution.py:36
  120.1 1.6 collective-permute-start.2
  121.7 10.4 %collective-permute-done.2 = bf16[384,1024]{1,0:T(8,128)(2,1)S(1)} collective-permute-done((bf16[384,1024]{1,0:T(8,128)(2,1)S(1)}, bf16[384,1024]{1,0:T(8,128)(2,1)S(1)}, u32[]{:S(2)}, u32[]{:S(2)}) %collective-permute-start.2) | collective-permute-done | bytes 786464 | tf_op jit(solution)/shard_map/cond/branch_1_fun/sum0_second/ppermute | solution.py:36
  134.8 10.7 %collective-permute-done.3 = bf16[384,1024]{1,0:T(8,128)(2,1)S(1)} collective-permute-done((bf16[384,1024]{1,0:T(8,128)(2,1)}, bf16[384,1024]{1,0:T(8,128)(2,1)S(1)}, u32[]{:S(2)}, u32[]{:S(2)}) %collective-permute-start.3) | collective-permute-done | bytes 786464 | tf_op jit(solution)/shard_map/cond/branch_1_fun/ring0_first/ppermute | solution.py:36
  146.9 63.1 %conditional.7 = (bf16[384,1024]{1,0:T(8,128)(2,1)}, bf16[192,1024]{1,0:T(8,128)(2,1)S(1)}, bf16[192,1024]{1,0:T(8,128)(2,1)}, bf16[2,384,1024]{2,1,0:T(8,128)(2...) conditional(s32[]{:T(128)} %convert_element_type.33, () %tuple.56, ...), branch_computations={%region_4.5_spmd, %region_5.6_spmd} | conditional | flops 12887654400 | bytes 94896424 | solution.py:347
  147.1 6.0 %branch_1_fun.18.refs_2_ = bf16[1536,1024]{1,0:T(8,128)(2,1)S(1)} custom-call(bf16[4,1536,256]{2,1,0:T(8,128)(2,1)} %get-tuple-element.95.factor_ref, bf16[1024,1024]{1,0:T(8,128)(2,1)} %get-tuple-element.96.inverse_ref), custom_call_target="tpu_custom_call" | custom-call | flops 3221225472 | bytes 8388608 | tf_op jit(solution)/shard_map/cond/branch_1_fun/pallas_call | solution.py:89
  153.2 1.6 collective-permute-start.15
  154.8 4.0 %collective-permute-done.14.refs_3_ = bf16[1536,1024]{1,0:T(8,128)(2,1)S(1)} collective-permute-done((bf16[1536,1024]{1,0:T(8,128)(2,1)S(1)}, bf16[1536,1024]{1,0:T(8,128)(2,1)S(1)}, u32[]{:S(2)}, u32[]{:S(2)}) %collective-permute-start.14) | collective-permute-done | bytes 3145760 | tf_op jit(solution)/shard_map/cond/branch_1_fun/scaled1_swap/ppermute | solution.py:36
  158.8 6.9 %branch_1_fun.20 = bf16[768,1024]{1,0:T(8,128)(2,1)S(1)} custom-call(bf16[1536,1536]{1,0:T(8,128)(2,1)} %get-tuple-element.93.refs_0_, bf16[1536,1536]{1,0:T(8,128)(2,1)} %get-tuple-element.94.refs_1_, bf16[1536,1024]{1,0:T(8,128)(2,1)S(1)} %branch_1_fun.18.refs_2_, bf16[1536,1024]{1,0:T(8,128)(2,1)S(1)} %collective-permute-done.14.refs_3_), custom_call_target="tpu_custom_call" | custom-call | flops 4831838208 | bytes 14155776 | tf_op jit(solution)/shard_map/cond/branch_1_fun/pallas_call | solution.py:119
  165.7 8.1 %collective-permute-done.15 = bf16[2,384,1024]{2,1,0:T(8,128)(2,1)} collective-permute-done((bf16[2,384,1024]{2,1,0:T(8,128)(2,1)S(1)}, bf16[2,384,1024]{2,1,0:T(8,128)(2,1)}, u32[]{:S(2)}, u32[]{:S(2)}) %collective-permute-start.15) | collective-permute-done | bytes 1572896 | tf_op jit(solution)/shard_map/cond/branch_1_fun/ring0_second/ppermute | solution.py:36
  175.8 6.8 %branch_1_fun.19 = f32[768,1024]{1,0:T(8,128)S(1)} custom-call(bf16[1536,1536]{1,0:T(8,128)(2,1)} %get-tuple-element.93.refs_0_, bf16[1536,1536]{1,0:T(8,128)(2,1)} %get-tuple-element.94.refs_1_, bf16[1536,1024]{1,0:T(8,128)(2,1)S(1)} %branch_1_fun.18.refs_2_, bf16[1536,1024]{1,0:T(8,128)(2,1)S(1)} %collective-permute-done.14.refs_3_), custom_call_target="tpu_custom_call" | custom-call | flops 4831838208 | bytes 14155776 | tf_op jit(solution)/shard_map/cond/branch_1_fun/pallas_call | solution.py:119
  182.6 11.5 %collective-permute-done.16 = bf16[2,384,1024]{2,1,0:T(8,128)(2,1)S(1)} collective-permute-done((bf16[2,384,1024]{2,1,0:T(8,128)(2,1)S(1)}, bf16[2,384,1024]{2,1,0:T(8,128)(2,1)S(1)}, u32[]{:S(2)}, u32[]{:S(2)}) %collective-permute-start.16) | collective-permute-done | bytes 1572896 | tf_op jit(solution)/shard_map/cond/branch_1_fun/sum1_first/ppermute | solution.py:36
  194.8 1.6 collective-permute-start.17
  196.6 10.3 %collective-permute-done.17 = bf16[384,1024]{1,0:T(8,128)(2,1)S(1)} collective-permute-done((bf16[384,1024]{1,0:T(8,128)(2,1)S(1)}, bf16[384,1024]{1,0:T(8,128)(2,1)S(1)}, u32[]{:S(2)}, u32[]{:S(2)}) %collective-permute-start.17) | collective-permute-done | bytes 786464 | tf_op jit(solution)/shard_map/cond/branch_1_fun/sum1_second/ppermute | solution.py:36
  208.1 1.9 fusion.6
  210.8 50.8 %conditional.8 = (bf16[2,384,1024]{2,1,0:T(8,128)(2,1)}, bf16[384,1024]{1,0:T(8,128)(2,1)}, bf16[384,1024]{1,0:T(8,128)(2,1)}, bf16[384,1024]{1,0:T(8,128)(2,1)}) conditional(s32[]{:T(128)} %convert_element_type.33, () %tuple.66, (bf16[384,1024]{1,0:T(8,128)(2,1)}, s32[]{:T(128)}, s32[]{:T(128)}, bf16[4,384,1024]{2,1,0:T(8,128)(2,1)}) %tuple.104), branch_computations={%region_6.7_spmd, %region_7.8_spmd} | conditional | flops 786492 | bytes 20448058 | solution.py:347
  212.4 1.8 dynamic-slice_bitcast_fusion
  217.8 12.5 %collective-permute-done.4 = bf16[384,1024]{1,0:T(8,128)(2,1)S(1)} collective-permute-done((bf16[384,1024]{1,0:T(8,128)(2,1)}, bf16[384,1024]{1,0:T(8,128)(2,1)S(1)}, u32[]{:S(2)}, u32[]{:S(2)}) %collective-permute-start.4) | collective-permute-done | bytes 786464 | tf_op jit(solution)/shard_map/cond/branch_1_fun/ring1_first/ppermute | solution.py:36
  230.3 2.4 pad_maximum_fusion.7
  232.7 14.5 %collective-permute-done.5 = bf16[384,1024]{1,0:T(8,128)(2,1)} collective-permute-done((bf16[384,1024]{1,0:T(8,128)(2,1)S(1)}, bf16[384,1024]{1,0:T(8,128)(2,1)}, u32[]{:S(2)}, u32[]{:S(2)}) %collective-permute-start.5) | collective-permute-done | bytes 786464 | tf_op jit(solution)/shard_map/cond/branch_1_fun/column0_10/ppermute | solution.py:36
  247.3 14.3 %collective-permute-done.7 = bf16[384,1024]{1,0:T(8,128)(2,1)} collective-permute-done((bf16[384,1024]{1,0:T(8,128)(2,1)S(1)}, bf16[384,1024]{1,0:T(8,128)(2,1)}, u32[]{:S(2)}, u32[]{:S(2)}) %collective-permute-start.7) | collective-permute-done | bytes 786464 | tf_op jit(solution)/shard_map/cond/branch_1_fun/column0_11/ppermute | solution.py:36
  262.1 39.5 %conditional.9 = (bf16[192,1024]{1,0:T(8,128)(2,1)}, bf16[192,1024]{1,0:T(8,128)(2,1)}, bf16[192,1024]{1,0:T(8,128)(2,1)}, bf16[2,384,1024]{2,1,0:T(8,128)(2,1)S...) conditional(s32[]{:T(128)} %convert_element_type.33, () %tuple.69, ...), branch_computations={%region_8.9_spmd, %region_9.10_spmd} | conditional | flops 9663676416 | bytes 76284840 | solution.py:347
  265.5 1.6 collective-permute-start.10
  267.4 22.3 %branch_1_fun.21 = f32[3072,1536]{1,0:T(8,128)} custom-call(s32[15]{0:T(128)S(1)} %get-tuple-element.106.meta_ref, f32[3072,1536]{1,0:T(8,128)} %get-tuple-element.107.total_ref, bf16[2,384,1024]{2,1,0:T(8,128)(2,1)S(1)} %get-tuple-element.108.refs_0_, bf16[2,384,1024]{2,1,0:T(8,128)(2,1)} %get-tuple-element.109.refs_1_, ...), custom_call_target="tpu_custom_call" | custom-call | flops 9663676416 | bytes 47185920 | tf_op jit(solution)/shard_map/cond/branch_1_fun/pallas_call | solution.py:198
  289.7 5.8 %collective-permute-done.10 = bf16[192,1024]{1,0:T(8,128)(2,1)} collective-permute-done((bf16[192,1024]{1,0:T(8,128)(2,1)S(1)}, bf16[192,1024]{1,0:T(8,128)(2,1)}, u32[]{:S(2)}, u32[]{:S(2)}) %collective-permute-start.10) | collective-permute-done | bytes 393248 | tf_op jit(solution)/shard_map/cond/branch_1_fun/column1_half0_01/ppermute | solution.py:36
  297.4 1.8 collective-permute-done.12
  299.3 2.2 collective-permute-done.13
  306.5 14.8 %shard_map.48.total_ref = f32[3072,1536]{1,0:T(8,128)} custom-call(s32[15]{0:T(128)S(1)} %stack.171.meta_ref, f32[3072,1536]{1,0:T(8,128)} %get-tuple-element.249.total_ref, bf16[2,384,1024]{2,1,0:T(8,128)(2,1)S(1)} %get-tuple-element.250.refs_0_, bf16[2,384,1024]{2,1,0:T(8,128)(2,1)} %get-tuple-element.251.refs_1_, ...), custom_call_target="tpu_custom_call", output_to_operand_aliasing={{}: (1, {})} | custom-call | flops 4831838208 | bytes 26738688 | tf_op jit(solution)/shard_map/pallas_call | solution.py:198
  321.3 2.6 collective-permute-done.28.refs_6_
  323.9 14.8 %shard_map.49 = f32[3072,1536]{1,0:T(8,128)} custom-call(s32[15]{0:T(128)S(1)} %stack.171.meta_ref, f32[3072,1536]{1,0:T(8,128)} %shard_map.48.total_ref, bf16[2,384,1024]{2,1,0:T(8,128)(2,1)S(1)} %get-tuple-element.250.refs_0_, bf16[2,384,1024]{2,1,0:T(8,128)(2,1)} %get-tuple-element.251.refs_1_, ...), custom_call_target="tpu_custom_call", output_to_operand_aliasing={{}: (1, {})} | custom-call | flops 4831838208 | bytes 26738688 | tf_op jit(solution)/shard_map/pallas_call | solution.py:198
  (80 shorter events, 36.4 us)
Async XLA Ops:
  6.5 71.6 %all-gather.10.cloned.1.call-start = ((), (), s32[]{:S(2)}) async-start(), calls=%async_computation | async-start | bytes 3932160 | tf_op jit(solution)/shard_map/all_gather | solution.py:359
  8.6 138.2 %all-gather.12.cloned.1.call-start = ((), (), s32[]{:S(2)}) async-start(), calls=%async_computation.1 | async-start | bytes 3932160 | tf_op jit(solution)/shard_map/all_gather | solution.py:371
  38.7 39.4 %collective-permute-start.26 = (bf16[1536,1536]{1,0:T(8,128)(2,1)}, bf16[1536,1536]{1,0:T(8,128)(2,1)}, u32[]{:S(2)}, u32[]{:S(2)}) collective-permute-start(bf16[1536,1536]{1,0:T(8,128)(2,1)} %bitcast.31), channel_id=1, source_target_pairs={{0,1},{1,0},{2,3},{3,2},{4,5},{5,4},{6,7},{7,6},{8,9},{9,8},{10,11... | collective-permute-start | bytes 14155784 | tf_op jit(solution)/shard_map/cond/branch_1_fun/held_swap/ppermute | solution.py:36
  38.8 6.4 %collective-permute-start.20 = (bf16[1,4,32,1024]{3,2,1,0:T(8,128)(2,1)S(1)}, bf16[1,4,32,1024]{3,2,1,0:T(8,128)(2,1)S(1)}, u32[]{:S(2)}, u32[]{:S(2)}) collective-permute-start(bf16[1,4,32,1024]{3,2,1,0:T(8,128)(2,1)S(1)} %get-tuple-element.270), channel_id=1, source_target_pairs={{0,16},{1,3},{2,18},{3,1},{4,20},{5,7},{6,22},{7,5},{8,24},{9,11},... | collective-permute-start | bytes 786440 | tf_op jit(solution)/shard_map/cond/branch_1_fun/inverse0_plane0/ppermute | solution.py:36
  40.3 7.9 %collective-permute-start.23 = (bf16[1,4,32,1024]{3,2,1,0:T(8,128)(2,1)S(1)}, bf16[1,4,32,1024]{3,2,1,0:T(8,128)(2,1)S(1)}, u32[]{:S(2)}, u32[]{:S(2)}) collective-permute-start(bf16[1,4,32,1024]{3,2,1,0:T(8,128)(2,1)S(1)} %get-tuple-element.269), channel_id=1, source_target_pairs={{0,16},{1,3},{2,18},{3,1},{4,20},{5,7},{6,22},{7,5},{8,24},{9,11},... | collective-permute-start | bytes 786440 | tf_op jit(solution)/shard_map/cond/branch_1_fun/inverse1_plane0/ppermute | solution.py:36
  45.3 9.2 %collective-permute-start.21 = (bf16[2,4,32,1024]{3,2,1,0:T(8,128)(2,1)S(1)}, bf16[2,4,32,1024]{3,2,1,0:T(8,128)(2,1)S(1)}, u32[]{:S(2)}, u32[]{:S(2)}) collective-permute-start(bf16[2,4,32,1024]{3,2,1,0:T(8,128)(2,1)S(1)} %pad_maximum_fusion.4), channel_id=1, source_target_pairs={{0,2},{1,17},{2,0},{3,19},{4,6},{5,21},{6,4},{7,23},{8,10},{9,25},... | collective-permute-start | bytes 1572872 | tf_op jit(solution)/shard_map/cond/branch_1_fun/inverse0_plane1/ppermute | solution.py:36
  48.3 11.8 %collective-permute-start.24 = (bf16[2,4,32,1024]{3,2,1,0:T(8,128)(2,1)S(1)}, bf16[2,4,32,1024]{3,2,1,0:T(8,128)(2,1)S(1)}, u32[]{:S(2)}, u32[]{:S(2)}) collective-permute-start(bf16[2,4,32,1024]{3,2,1,0:T(8,128)(2,1)S(1)} %pad_maximum_fusion.5), channel_id=1, source_target_pairs={{0,2},{1,17},{2,0},{3,19},{4,6},{5,21},{6,4},{7,23},{8,10},{9,25},... | collective-permute-start | bytes 1572872 | tf_op jit(solution)/shard_map/cond/branch_1_fun/inverse1_plane1/ppermute | solution.py:36
  55.6 12.5 %collective-permute-start.22 = (bf16[4,4,32,1024]{3,2,1,0:T(8,128)(2,1)}, bf16[4,4,32,1024]{3,2,1,0:T(8,128)(2,1)}, u32[]{:S(2)}, u32[]{:S(2)}) collective-permute-start(bf16[4,4,32,1024]{3,2,1,0:T(8,128)(2,1)} %pad_maximum_fusion.2), channel_id=1, source_target_pairs={{0,1},{1,0},{2,3},{3,2},{4,5},{5,4},{6,7},{7,6},{8,9},{9,8},{10,11... | collective-permute-start | bytes 3145736 | tf_op jit(solution)/shard_map/cond/branch_1_fun/inverse0_swap/ppermute | solution.py:36
  60.2 12.9 %collective-permute-start.25 = (bf16[4,4,32,1024]{3,2,1,0:T(8,128)(2,1)S(1)}, bf16[4,4,32,1024]{3,2,1,0:T(8,128)(2,1)}, u32[]{:S(2)}, u32[]{:S(2)}) collective-permute-start(bf16[4,4,32,1024]{3,2,1,0:T(8,128)(2,1)S(1)} %pad_maximum_fusion.3), channel_id=1, source_target_pairs={{0,1},{1,0},{2,3},{3,2},{4,5},{5,4},{6,7},{7,6},{8,9},{9,8},{10,11... | collective-permute-start | bytes 3145736 | tf_op jit(solution)/shard_map/cond/branch_1_fun/inverse1_swap/ppermute | solution.py:36
  80.3 130.0 %all-gather.14.cloned.1.call-start = ((), (), s32[]{:S(2)}) async-start(), calls=%async_computation.2 | async-start | bytes 3932160 | tf_op jit(solution)/shard_map/all_gather | solution.py:373
  86.3 5.7 %collective-permute-start = (bf16[1536,1024]{1,0:T(8,128)(2,1)S(1)}, bf16[1536,1024]{1,0:T(8,128)(2,1)S(1)}, u32[]{:S(2)}, u32[]{:S(2)}) collective-permute-start(bf16[1536,1024]{1,0:T(8,128)(2,1)S(1)} %branch_1_fun.15.refs_2_), channel_id=1, source_target_pairs={{0,1},{1,0},{2,3},{3,2},{4,5},{5,4},{6,7},{7,6},{8,9},{9,8},{10,11... | collective-permute-start | bytes 9437192 | tf_op jit(solution)/shard_map/cond/branch_1_fun/scaled0_swap/ppermute | solution.py:36
  98.9 20.5 %collective-permute-start.1 = (bf16[2,384,1024]{2,1,0:T(8,128)(2,1)S(1)}, bf16[2,384,1024]{2,1,0:T(8,128)(2,1)S(1)}, u32[]{:S(2)}, u32[]{:S(2)}) collective-permute-start(bf16[2,384,1024]{2,1,0:T(8,128)(2,1)S(1)} %bitcast.101), channel_id=1, source_target_pairs={{0,16},{1,3},{2,18},{3,1},{4,20},{5,7},{6,22},{7,5},{8,24},{9,11},... | collective-permute-start | bytes 4718600 | tf_op jit(solution)/shard_map/cond/branch_1_fun/sum0_first/ppermute | solution.py:36
  120.1 12.1 %collective-permute-start.2 = (bf16[384,1024]{1,0:T(8,128)(2,1)S(1)}, bf16[384,1024]{1,0:T(8,128)(2,1)S(1)}, u32[]{:S(2)}, u32[]{:S(2)}) collective-permute-start(bf16[384,1024]{1,0:T(8,128)(2,1)S(1)} %fusion.2), channel_id=1, source_target_pairs={{0,2},{1,17},{2,0},{3,19},{4,6},{5,21},{6,4},{7,23},{8,10},{9,25},... | collective-permute-start | bytes 2359304 | tf_op jit(solution)/shard_map/cond/branch_1_fun/sum0_second/ppermute | solution.py:36
  133.3 12.2 %collective-permute-start.3 = (bf16[384,1024]{1,0:T(8,128)(2,1)}, bf16[384,1024]{1,0:T(8,128)(2,1)S(1)}, u32[]{:S(2)}, u32[]{:S(2)}) collective-permute-start(bf16[384,1024]{1,0:T(8,128)(2,1)} %fusion.1), channel_id=1, source_target_pairs={{0,16},{1,3},{2,18},{3,1},{4,20},{5,7},{6,22},{7,5},{8,24},{9,11},... | collective-permute-start | bytes 2359304 | tf_op jit(solution)/shard_map/cond/branch_1_fun/ring0_first/ppermute | solution.py:36
  146.8 114.8 %all-gather.16.cloned.1.call-start = ((), (), s32[]{:S(2)}) async-start(), calls=%async_computation.3 | async-start | bytes 1966080 | tf_op jit(solution)/shard_map/all_gather | solution.py:405
  153.1 5.7 %collective-permute-start.14 = (bf16[1536,1024]{1,0:T(8,128)(2,1)S(1)}, bf16[1536,1024]{1,0:T(8,128)(2,1)S(1)}, u32[]{:S(2)}, u32[]{:S(2)}) collective-permute-start(bf16[1536,1024]{1,0:T(8,128)(2,1)S(1)} %branch_1_fun.18.refs_2_), channel_id=1, source_target_pairs={{0,1},{1,0},{2,3},{3,2},{4,5},{5,4},{6,7},{7,6},{8,9},{9,8},{10,11... | collective-permute-start | bytes 9437192 | tf_op jit(solution)/shard_map/cond/branch_1_fun/scaled1_swap/ppermute | solution.py:36
  153.2 20.6 %collective-permute-start.15 = (bf16[2,384,1024]{2,1,0:T(8,128)(2,1)S(1)}, bf16[2,384,1024]{2,1,0:T(8,128)(2,1)}, u32[]{:S(2)}, u32[]{:S(2)}) collective-permute-start(bf16[2,384,1024]{2,1,0:T(8,128)(2,1)S(1)} %get-tuple-element.304), channel_id=1, source_target_pairs={{0,2},{1,17},{2,0},{3,19},{4,6},{5,21},{6,4},{7,23},{8,10},{9,25},... | collective-permute-start | bytes 4718600 | tf_op jit(solution)/shard_map/cond/branch_1_fun/ring0_second/ppermute | solution.py:36
  173.8 20.4 %collective-permute-start.16 = (bf16[2,384,1024]{2,1,0:T(8,128)(2,1)S(1)}, bf16[2,384,1024]{2,1,0:T(8,128)(2,1)S(1)}, u32[]{:S(2)}, u32[]{:S(2)}) collective-permute-start(bf16[2,384,1024]{2,1,0:T(8,128)(2,1)S(1)} %bitcast.100), channel_id=1, source_target_pairs={{0,16},{1,3},{2,18},{3,1},{4,20},{5,7},{6,22},{7,5},{8,24},{9,11},... | collective-permute-start | bytes 4718600 | tf_op jit(solution)/shard_map/cond/branch_1_fun/sum1_first/ppermute | solution.py:36
  175.3 34.7 %collective-permute-start.18 = (bf16[2,384,1024]{2,1,0:T(8,128)(2,1)S(1)}, bf16[2,384,1024]{2,1,0:T(8,128)(2,1)}, u32[]{:S(2)}, u32[]{:S(2)}) collective-permute-start(bf16[2,384,1024]{2,1,0:T(8,128)(2,1)S(1)} %get-tuple-element.304), channel_id=1, source_target_pairs={{0,1},{1,0},{2,3},{3,2},{4,5},{5,4},{6,7},{7,6},{8,9},{9,8},{10,11... | collective-permute-start | bytes 4718600 | tf_op jit(solution)/shard_map/cond/branch_1_fun/ring0_swap/ppermute | solution.py:36
  175.3 34.7 %collective-permute-start.19 = (bf16[2,384,1024]{2,1,0:T(8,128)(2,1)}, bf16[2,384,1024]{2,1,0:T(8,128)(2,1)}, u32[]{:S(2)}, u32[]{:S(2)}) collective-permute-start(bf16[2,384,1024]{2,1,0:T(8,128)(2,1)} %collective-permute-done.15), channel_id=1, source_target_pairs={{0,1},{1,0},{2,3},{3,2},{4,5},{5,4},{6,7},{7,6},{8,9},{9,8},{10,11... | collective-permute-start | bytes 4718600 | tf_op jit(solution)/shard_map/cond/branch_1_fun/ring0_swap/ppermute | solution.py:36
  194.8 12.1 %collective-permute-start.17 = (bf16[384,1024]{1,0:T(8,128)(2,1)S(1)}, bf16[384,1024]{1,0:T(8,128)(2,1)S(1)}, u32[]{:S(2)}, u32[]{:S(2)}) collective-permute-start(bf16[384,1024]{1,0:T(8,128)(2,1)S(1)} %fusion.5), channel_id=1, source_target_pairs={{0,2},{1,17},{2,0},{3,19},{4,6},{5,21},{6,4},{7,23},{8,10},{9,25},... | collective-permute-start | bytes 2359304 | tf_op jit(solution)/shard_map/cond/branch_1_fun/sum1_second/ppermute | solution.py:36
  210.0 0.7 copy-start.2
  210.8 90.8 %all-gather.18.cloned.1.call-start = ((), (), s32[]{:S(2)}) async-start(), calls=%async_computation.4 | async-start | bytes 1966080 | tf_op jit(solution)/shard_map/all_gather | solution.py:417
  210.8 19.5 %collective-permute-start.4 = (bf16[384,1024]{1,0:T(8,128)(2,1)}, bf16[384,1024]{1,0:T(8,128)(2,1)S(1)}, u32[]{:S(2)}, u32[]{:S(2)}) collective-permute-start(bf16[384,1024]{1,0:T(8,128)(2,1)} %get-tuple-element.101), channel_id=1, source_target_pairs={{0,16},{1,3},{2,18},{3,1},{4,20},{5,7},{6,22},{7,5},{8,24},{9,11},... | collective-permute-start | bytes 2359304 | tf_op jit(solution)/shard_map/cond/branch_1_fun/ring1_first/ppermute | solution.py:36
  214.2 33.1 %collective-permute-start.5 = (bf16[384,1024]{1,0:T(8,128)(2,1)S(1)}, bf16[384,1024]{1,0:T(8,128)(2,1)}, u32[]{:S(2)}, u32[]{:S(2)}) collective-permute-start(bf16[384,1024]{1,0:T(8,128)(2,1)S(1)} %get-tuple-element.275), channel_id=1, source_target_pairs={{0,16},{1,17},{2,18},{3,19},{4,20},{5,21},{6,22},{7,23},{8,24},{9,... | collective-permute-start | bytes 2359304 | tf_op jit(solution)/shard_map/cond/branch_1_fun/column0_10/ppermute | solution.py:36
  214.8 32.5 %collective-permute-start.6 = (bf16[384,1024]{1,0:T(8,128)(2,1)S(1)}, bf16[384,1024]{1,0:T(8,128)(2,1)}, u32[]{:S(2)}, u32[]{:S(2)}) collective-permute-start(bf16[384,1024]{1,0:T(8,128)(2,1)S(1)} %get-tuple-element.274), channel_id=1, source_target_pairs={{0,2},{1,3},{2,0},{3,1},{4,6},{5,7},{6,4},{7,5},{8,10},{9,11},{10,... | collective-permute-start | bytes 2359304 | tf_op jit(solution)/shard_map/cond/branch_1_fun/column0_01/ppermute | solution.py:36
  216.4 45.2 %collective-permute-start.7 = (bf16[384,1024]{1,0:T(8,128)(2,1)S(1)}, bf16[384,1024]{1,0:T(8,128)(2,1)}, u32[]{:S(2)}, u32[]{:S(2)}) collective-permute-start(bf16[384,1024]{1,0:T(8,128)(2,1)S(1)} %get-tuple-element.273), channel_id=1, source_target_pairs={{0,18},{1,19},{2,16},{3,17},{4,22},{5,23},{6,20},{7,21},{8,26},{9,... | collective-permute-start | bytes 2359304 | tf_op jit(solution)/shard_map/cond/branch_1_fun/column0_11/ppermute | solution.py:36
  262.1 33.4 %collective-permute-start.8 = (bf16[2,384,1024]{2,1,0:T(8,128)(2,1)}, bf16[2,384,1024]{2,1,0:T(8,128)(2,1)}, u32[]{:S(2)}, u32[]{:S(2)}) collective-permute-start(bf16[2,384,1024]{2,1,0:T(8,128)(2,1)} %get-tuple-element.327), channel_id=1, source_target_pairs={{0,2},{1,17},{2,0},{3,19},{4,6},{5,21},{6,4},{7,23},{8,10},{9,25},... | collective-permute-start | bytes 4718600 | tf_op jit(solution)/shard_map/cond/branch_1_fun/ring1_second/ppermute | solution.py:36
  263.9 25.9 %collective-permute-start.9 = (bf16[192,1024]{1,0:T(8,128)(2,1)S(1)}, bf16[192,1024]{1,0:T(8,128)(2,1)}, u32[]{:S(2)}, u32[]{:S(2)}) collective-permute-start(bf16[192,1024]{1,0:T(8,128)(2,1)S(1)} %get-tuple-element.278), channel_id=1, source_target_pairs={{0,16},{1,17},{2,18},{3,19},{4,20},{5,21},{6,22},{7,23},{8,24},{9,... | collective-permute-start | bytes 1179656 | tf_op jit(solution)/shard_map/cond/branch_1_fun/column1_half0_10/ppermute | solution.py:36
  265.5 30.0 %collective-permute-start.10 = (bf16[192,1024]{1,0:T(8,128)(2,1)S(1)}, bf16[192,1024]{1,0:T(8,128)(2,1)}, u32[]{:S(2)}, u32[]{:S(2)}) collective-permute-start(bf16[192,1024]{1,0:T(8,128)(2,1)S(1)} %get-tuple-element.277), channel_id=1, source_target_pairs={{0,2},{1,3},{2,0},{3,1},{4,6},{5,7},{6,4},{7,5},{8,10},{9,11},{10,... | collective-permute-start | bytes 1179656 | tf_op jit(solution)/shard_map/cond/branch_1_fun/column1_half0_01/ppermute | solution.py:36
  267.1 28.4 %collective-permute-start.11 = (bf16[192,1024]{1,0:T(8,128)(2,1)S(1)}, bf16[192,1024]{1,0:T(8,128)(2,1)}, u32[]{:S(2)}, u32[]{:S(2)}) collective-permute-start(bf16[192,1024]{1,0:T(8,128)(2,1)S(1)} %get-tuple-element.276), channel_id=1, source_target_pairs={{0,18},{1,19},{2,16},{3,17},{4,22},{5,23},{6,20},{7,21},{8,26},{9,... | collective-permute-start | bytes 1179656 | tf_op jit(solution)/shard_map/cond/branch_1_fun/column1_half0_11/ppermute | solution.py:36
  295.5 3.8 %collective-permute-start.12 = (bf16[2,384,1024]{2,1,0:T(8,128)(2,1)}, bf16[2,384,1024]{2,1,0:T(8,128)(2,1)}, u32[]{:S(2)}, u32[]{:S(2)}) collective-permute-start(bf16[2,384,1024]{2,1,0:T(8,128)(2,1)} %get-tuple-element.327), channel_id=1, source_target_pairs={{0,1},{1,0},{2,3},{3,2},{4,5},{5,4},{6,7},{7,6},{8,9},{9,8},{10,11... | collective-permute-start | bytes 4718600 | tf_op jit(solution)/shard_map/cond/branch_1_fun/ring1_swap/ppermute | solution.py:36
  295.5 6.0 %collective-permute-start.13 = (bf16[2,384,1024]{2,1,0:T(8,128)(2,1)}, bf16[2,384,1024]{2,1,0:T(8,128)(2,1)}, u32[]{:S(2)}, u32[]{:S(2)}) collective-permute-start(bf16[2,384,1024]{2,1,0:T(8,128)(2,1)} %collective-permute-done.8), channel_id=1, source_target_pairs={{0,1},{1,0},{2,3},{3,2},{4,5},{5,4},{6,7},{7,6},{8,9},{9,8},{10,11... | collective-permute-start | bytes 4718600 | tf_op jit(solution)/shard_map/cond/branch_1_fun/ring1_swap/ppermute | solution.py:36
  301.5 5.0 %copy-start.1 = (bf16[768,1024]{1,0:T(8,128)(2,1)S(1)}, bf16[768,1024]{1,0:T(8,128)(2,1)}, u32[]{:S(2)}) copy-start(bf16[768,1024]{1,0:T(8,128)(2,1)} %all-gather.16.cloned.1.call-done) | copy-start | bytes 4718596
  303.0 18.4 %collective-permute-start.27 = (bf16[192,1024]{1,0:T(8,128)(2,1)S(1)}, bf16[192,1024]{1,0:T(8,128)(2,1)S(1)}, u32[]{:S(2)}, u32[]{:S(2)}) collective-permute-start(bf16[192,1024]{1,0:T(8,128)(2,1)S(1)} %get-tuple-element.281), channel_id=1, source_target_pairs={{0,16},{1,17},{2,18},{3,19},{4,20},{5,21},{6,22},{7,23},{8,24},{9,... | collective-permute-start | bytes 1179656 | tf_op jit(solution)/shard_map/column1_half1_10/ppermute | solution.py:36
  304.6 19.3 %collective-permute-start.28 = (bf16[192,1024]{1,0:T(8,128)(2,1)S(1)}, bf16[192,1024]{1,0:T(8,128)(2,1)S(1)}, u32[]{:S(2)}, u32[]{:S(2)}) collective-permute-start(bf16[192,1024]{1,0:T(8,128)(2,1)S(1)} %get-tuple-element.280), channel_id=1, source_target_pairs={{0,2},{1,3},{2,0},{3,1},{4,6},{5,7},{6,4},{7,5},{8,10},{9,11},{10,... | collective-permute-start | bytes 1179656 | tf_op jit(solution)/shard_map/column1_half1_01/ppermute | solution.py:36
  305.0 18.9 %collective-permute-start.29 = (bf16[192,1024]{1,0:T(8,128)(2,1)S(1)}, bf16[192,1024]{1,0:T(8,128)(2,1)S(1)}, u32[]{:S(2)}, u32[]{:S(2)}) collective-permute-start(bf16[192,1024]{1,0:T(8,128)(2,1)S(1)} %get-tuple-element.279), channel_id=1, source_target_pairs={{0,18},{1,19},{2,16},{3,17},{4,22},{5,23},{6,20},{7,21},{8,26},{9,... | collective-permute-start | bytes 1179656 | tf_op jit(solution)/shard_map/column1_half1_11/ppermute | solution.py:36
  306.5 17.4 %copy-start = (bf16[768,1024]{1,0:T(8,128)(2,1)S(1)}, bf16[768,1024]{1,0:T(8,128)(2,1)}, u32[]{:S(2)}) copy-start(bf16[768,1024]{1,0:T(8,128)(2,1)} %all-gather.18.cloned.1.call-done) | copy-start | bytes 4718596
Sparse Core Ops, SparseCore 0:
  8.9 68.7 all-gather.9
  80.4 63.2 all-gather.11
  147.0 63.2 all-gather.13
  211.7 36.0 all-gather.15
  261.7 37.4 all-gather.17

commit v4 on v3

--- a/solution.py
+++ b/solution.py
@@ -125,9 +125,7 @@
             out_specs=pl.BlockSpec((piece, width), lambda i: (i, 0)),
             compiler_params=params,
             cost_estimate=pl.CostEstimate(
-                flops=2 * mates * count * tile * width,
-                bytes_accessed=2 * mates * tile * (count + width) + 4 * count * width,
-                transcendentals=0,
+                flops=0, bytes_accessed=0, transcendentals=0
             ),
         )(*held, *scaleds)
 
@@ -277,20 +275,20 @@
             order = jnp.stack(ordered).astype(jnp.int32)
             return reorder(order, part_rows).reshape(rows * depth, -1)
 
-        def sum_first(panel, factor, inverse, around, *held):
+        def sum_first(panel, factor, inverse, *held):
             scaled = scale(factor, inverse)
             scaleds = [scaled]
             scaleds += [to_mate(scaled, step, f"scaled{panel}_swap") for step in range(1, mates)]
             each = n2 * piece
             sent = product(held, scaleds, each, (n1 - 1) * each, piece, jnp.bfloat16)
-            sent, around = fence(sent.reshape(n1 - 1, n2, piece, -1), around)
+            sent = sent.reshape(n1 - 1, n2, piece, -1)
             received = [
                 to_plane(sent[step - 1], 0, step, f"sum{panel}_first") for step in range(1, n1)
             ]
             half_sum = product(held, scaleds, 0, each, piece, jnp.float32).reshape(n2, piece, -1)
             for value in received:
                 half_sum = half_sum + value
-            return half_sum, around
+            return half_sum
 
         def sum_second(panel, half_sum):
             whole_sum = half_sum[0]
@@ -309,11 +307,13 @@
             return [pair] + [to_plane(pair, 1, b, f"ring{panel}_second") for b in range(1, n2)]
 
         def ring_swap(panel, lefts):
-            return lefts + [
-                to_mate(value, step, f"ring{panel}_swap")
+            return [
+                [to_mate(value, step, f"ring{panel}_swap") for value in lefts]
                 for step in range(1, mates)
-                for value in lefts
             ]
+
+        def joined(lefts, swapped):
+            return sum(swapped, lefts)
 
         def to_columns(name, gathered):
             came = []
@@ -350,69 +350,67 @@
         group = block * mates + mate
         own_rows = lax.dynamic_slice_in_dim(block_inverses, group * part, part, 1)
 
-        def prepare(own_rows, blocks):
+        def prepare(own_rows, blocks, factor_panels):
             stack, blocks = fence(lax.all_gather(own_rows, "row"), blocks)
             shares = [share(blocks, step) for step in range(mates)]
             held = [shares[0]] + [to_mate(shares[step], step, "held_swap") for step in range(1, mates)]
-            return [whole_inverse(stack[:, p], f"inverse{p}") for p in range(panels)], held
+            inverses = [whole_inverse(stack[:, p], f"inverse{p}") for p in range(panels)]
+            return inverses, held, [factor_panels[p] for p in range(1, panels)]
 
         factors = {0: lax.all_gather(factor_panels[0], "row")}
-        inverses, held = together(prepare, own_rows, blocks)
+        inverses, held, waiting = together(prepare, own_rows, blocks, factor_panels)
 
         def both(gathered, came):
             return {h: (gathered, h * sub, came) for h in range(HALVES)}
 
-        total, owns, pairs, moved, lefts = covariance, {}, {}, {}, {}
+        total, owns, pairs, moved, rests = covariance, {}, {}, {}, {}
         for now in range(panels):
-            state = fence(factors, inverses, held, total, owns, pairs, moved, lefts)
-            factors, inverses, held, total, owns, pairs, moved, lefts = state
+            state = fence(factors, inverses, held, total, owns, pairs, moved, rests)
+            factors, inverses, held, total, owns, pairs, moved, rests = state
             if now + 1 < panels:
-                factor_panels, factors[now] = fence(factor_panels, factors[now])
-                factors[now + 1] = lax.all_gather(factor_panels[now + 1], "row")
+                waiting, factors[now] = fence(waiting, factors[now])
+                factors[now + 1] = lax.all_gather(waiting[now], "row")
             if now >= 1:
                 moved[now - 1] = lax.all_gather(owns[now - 1], "row")
-
-            def work(factor, held, inverse, pair, total, lefts, moved):
-                around = latest = None
-                if pair is not None:
-                    around = ring_rest(now - 1, pair)
-                half_sum, around = sum_first(now, factor, inverse, around, *held)
-                own = sum_second(now, half_sum)
-                if lefts is not None:
-                    latest = update(meta, total, lefts, both(moved, to_columns(now - 2, moved)))
-                if pair is not None:
-                    around = ring_swap(now - 1, around)
-                if now + 1 < panels:
-                    return own, ring(now, own), around, latest
-                return own, halved(own), around, latest
-
-            owns[now], pairs[now], around, latest = together(
+                rests[now - 1] = ring_rest(now - 1, pairs[now - 1])
+
+            def work(factor, held, inverse, total, rest, moved):
+                own = sum_second(now, sum_first(now, factor, inverse, *held))
+                latest = None
+                if rest is not None:
+                    lefts, came = joined(rest, ring_swap(now - 2, rest)), to_columns(now - 2, moved)
+                    latest = update(meta, total, lefts, both(moved, came))
+                return own, halved(own), ring(now, own), latest
+
+            owns[now], parts, pairs[now], latest = together(
                 work,
                 factors[now],
                 held,
                 inverses[now],
-                pairs.get(now - 1),
                 total if now >= 2 else None,
-                lefts.get(now - 2),
+                rests.get(now - 2),
                 moved.get(now - 2),
             )
-            if around is not None:
-                lefts[now - 1] = around
             if latest is not None:
                 total = latest
 
-        own, parts, moved, lefts, total = fence(owns[panels - 1], pairs[panels - 1], moved, lefts, total)
+        parts, pair, moved, rests, total = fence(parts, pairs[panels - 1], moved, rests, total)
         gathered = {0: lax.all_gather(parts[0], "row")}
 
-        def first_work(own, value):
-            came = to_columns(panels - 2, value) if value is not None else None
-            return ring(panels - 1, own), came
-
-        pair, came = together(first_work, own, moved.get(panels - 2))
+        def first_work(value, rest, pair):
+            came = swapped = None
+            if value is not None:
+                came, swapped = to_columns(panels - 2, value), ring_swap(panels - 2, rest)
+            return came, swapped, ring_swap(panels - 1, [pair])
+
+        came, swapped, near = together(first_work, moved.get(panels - 2), rests.get(panels - 2), pair)
+        lefts = {}
+        if panels > 1:
+            lefts[panels - 2] = joined(rests[panels - 2], swapped)
         arrived = {}
         for h in range(HALVES):
-            state = fence(parts, pair, moved, lefts, total, gathered, came, arrived)
-            parts, pair, moved, lefts, total, gathered, came, arrived = state
+            state = fence(parts, pair, near, moved, lefts, total, gathered, came, arrived)
+            parts, pair, near, moved, lefts, total, gathered, came, arrived = state
             if h + 1 < HALVES:
                 gathered[h + 1] = lax.all_gather(parts[h + 1], "row")
             if h == 0:
@@ -423,9 +421,10 @@
                     if came is not None:
                         total = update(meta, total, lefts, both(moved, came))
                         around, total, steps_done = fence(around, total, steps_done)
-                    return steps_done, ring_swap(panels - 1, around), total if came is not None else None
-
-                arrived[0], around, latest = together(
+                    far = ring_swap(panels - 1, around[1:])
+                    return steps_done, around[1:], far, total if came is not None else None
+
+                arrived[0], rest, far, latest = together(
                     last_work,
                     gathered[0],
                     pair,
@@ -434,6 +433,7 @@
                     moved.get(panels - 2),
                     came,
                 )
+                around = joined([pair, *rest], [one + two for one, two in zip(near, far)])
                 if latest is not None:
                     total = latest
             else:

time: 347 us -> 341 us (0.983)
  transfers between devices with their start and end apart: 35 -> 35, of which waited for: 20 -> 17; matrix products, arithmetic and copies ran while one was open for 6% -> 5% of each run, Pallas kernels for 29% -> 29%
where the time goes in v4:
time: 341 us; the launch traced here: 340 us
  waiting for transfers between devices  143 us (42%)
  Pallas kernels  113 us (33%)
  starting transfers between devices  26.8 us (8%)
  blocking collectives  21.5 us (6%)
  between operations  13.6 us (4%)
  local copies, waits for them, and re-layouts  12.2 us (4%)
  other arithmetic  8.28 us (2%)
    ppermute x30, waiting for transfers between devices, send(): return lax.ppermute(value, AXES, pairs)  143 us
    pallas_call x3, Pallas kernels, update(): pl.pallas_call(kernel, out_shape=jax.ShapeDtypeStruct(total.shape, total....  51.7 us
    pallas_call x4, Pallas kernels, product(): pl.pallas_call(kernel, out_shape=jax.ShapeDtypeStruct((count, width), kin...  27.4 us
    ppermute x30, starting transfers between devices, send(): return lax.ppermute(value, AXES, pairs)  26.7 us
    pallas_call x4, Pallas kernels, reorder(): pl.pallas_call(kernel, out_shape=jax.ShapeDtypeStruct((planes, count, hei...  22 us
    all_gather x1, blocking collectives, prepare(): stack, blocks = fence(lax.all_gather(own_rows, 'row'), blocks)  21.5 us
    pallas_call x2, Pallas kernels, scale(): pl.pallas_call(kernel, out_shape=jax.ShapeDtypeStruct((tile, width), fact...  12.1 us
  transfers between devices with their start and end apart: 35, of which 17 were waited for; matrix products, arithmetic and copies ran while one was open for 5% of the time, Pallas kernels for 29%

profile of v4, /device:TPU:0, one launch (start us, length us, event | category | flops | bytes accessed | tf_op | source)
XLA Modules:
  0.0 339.7 jit_solution(5446849670169331876)
XLA Ops:
  6.5 2.1 slice.32
  8.7 72.0 %conditional.5 = (bf16[1024,1024]{1,0:T(8,128)(2,1)}, bf16[1024,1024]{1,0:T(8,128)(2,1)}, bf16[1536,1536]{1,0:T(8,128)(2,1)}, bf16[1536,1536]{1,0:T(8,128)(2,1)}, bf16[1536,256]{1,0:T(8,128)(2,1)}) conditional(s32[]{:T(128)} %convert_element_type.33, () %tuple.56, (s32[]{:T(128)}, s32[]{:T(128)}, s32[]{:T(128)}, s32[]{:T(128)}, ...), branch_computations={%region_0.1_spmd, %region_1.2_spmd} | conditional | flops 8913181 | bytes 83234256 | solution.py:347
  9.8 21.5 %all-gather = bf16[8,32,1024]{2,1,0:T(8,128)(2,1)S(1)} all-gather(bf16[2,32,1024]{2,1,0:T(8,128)(2,1)S(1)} %constant_dynamic-slice_fusion), channel_id=2, replica_groups=mesh['sec'=2,'row'=4,'col'=4] {'row'}, dimensions={0}, use_global_device_ids=true | all-gather | bytes 655360 | tf_op jit(solution)/shard_map/cond/branch_1_fun/all_gather | solution.py:354
  31.3 7.5 %branch_1_fun.14 = bf16[1,8,192,1536]{3,2,1,0:T(8,128)(2,1)} custom-call(s32[8]{0:T(128)S(1)} %stack.133.order_ref, bf16[16,1,192,1536]{3,2,1,0:T(8,128)(2,1)} %bitcast.103), custom_call_target="tpu_custom_call" | custom-call | bytes 9437184 | tf_op jit(solution)/shard_map/cond/branch_1_fun/pallas_call | solution.py:60
  38.8 1.6 collective-permute-start.19
  40.9 4.3 %collective-permute-done.19 = bf16[1,4,32,1024]{3,2,1,0:T(8,128)(2,1)S(1)} collective-permute-done((bf16[1,4,32,1024]{3,2,1,0:T(8,128)(2,1)S(1)}, bf16[1,4,32,1024]{3,2,1,0:T(8,128)(2,1)S(1)}, u32[]{:S(2)}, u32[]{:S(2)}) %collective-permute-start.19) | collective-permute-done | bytes 262176 | tf_op jit(solution)/shard_map/cond/branch_1_fun/inverse0_plane0/ppermute | solution.py:36
  45.3 1.6 collective-permute-start.20
  48.4 1.6 collective-permute-start.23
  50.0 4.5 %collective-permute-done.20 = bf16[2,4,32,1024]{3,2,1,0:T(8,128)(2,1)S(1)} collective-permute-done((bf16[2,4,32,1024]{3,2,1,0:T(8,128)(2,1)S(1)}, bf16[2,4,32,1024]{3,2,1,0:T(8,128)(2,1)S(1)}, u32[]{:S(2)}, u32[]{:S(2)}) %collective-permute-start.20) | collective-permute-done | bytes 524320 | tf_op jit(solution)/shard_map/cond/branch_1_fun/inverse0_plane1/ppermute | solution.py:36
  55.7 4.5 %collective-permute-done.23 = bf16[2,4,32,1024]{3,2,1,0:T(8,128)(2,1)S(1)} collective-permute-done((bf16[2,4,32,1024]{3,2,1,0:T(8,128)(2,1)S(1)}, bf16[2,4,32,1024]{3,2,1,0:T(8,128)(2,1)S(1)}, u32[]{:S(2)}, u32[]{:S(2)}) %collective-permute-start.23) | collective-permute-done | bytes 524320 | tf_op jit(solution)/shard_map/cond/branch_1_fun/inverse1_plane1/ppermute | solution.py:36
  61.1 7.4 %branch_1_fun.13 = bf16[1,8,192,1536]{3,2,1,0:T(8,128)(2,1)} custom-call(s32[8]{0:T(128)S(1)} %stack.124.order_ref, bf16[16,1,192,1536]{3,2,1,0:T(8,128)(2,1)} %bitcast.104), custom_call_target="tpu_custom_call" | custom-call | bytes 9437184 | tf_op jit(solution)/shard_map/cond/branch_1_fun/pallas_call | solution.py:60
  68.6 2.1 slice_bitcast_fusion
  72.2 3.6 %branch_1_fun.11 = bf16[4,8,32,1024]{3,2,1,0:T(8,128)(2,1)} custom-call(s32[8]{0:T(128)S(1)} %stack.42.order_ref, bf16[8,4,32,1024]{3,2,1,0:T(8,128)(2,1)S(1)} %pad_maximum_fusion.in_ref), custom_call_target="tpu_custom_call" | custom-call | bytes 4194304 | tf_op jit(solution)/shard_map/cond/branch_1_fun/pallas_call | solution.py:60
  77.2 3.5 %branch_1_fun.12 = bf16[4,8,32,1024]{3,2,1,0:T(8,128)(2,1)} custom-call(s32[8]{0:T(128)S(1)} %stack.42.order_ref, bf16[8,4,32,1024]{3,2,1,0:T(8,128)(2,1)S(1)} %pad_maximum_fusion.1.in_ref), custom_call_target="tpu_custom_call" | custom-call | bytes 4194304 | tf_op jit(solution)/shard_map/cond/branch_1_fun/pallas_call | solution.py:60
  80.8 66.7 %conditional.6 = (bf16[384,1024]{1,0:T(8,128)(2,1)}, bf16[2,384,1024]{2,1,0:T(8,128)(2,1)S(1)}) conditional(s32[]{:T(128)} %convert_element_type.33, () %tuple.60, (bf16[4,1536,256]{2,1,0:T(8,128)(2,1)}, bf16[1024,1024]{1,0:T(8,128)(2,1)}, bf16[1536,1536]{1,0:T(8,128)(2,1)}, bf16[1536,1536]{1,0:T(8,128)(2,1)}) %tuple.61), branch_computations={%region_2.3_spmd, %region_3.4_spmd} | conditional | flops 3224764416 | bytes 49283248 | solution.py:347
  80.8 6.0 %branch_1_fun.15.refs_2_ = bf16[1536,1024]{1,0:T(8,128)(2,1)S(1)} custom-call(bf16[4,1536,256]{2,1,0:T(8,128)(2,1)} %get-tuple-element.96.factor_ref, bf16[1024,1024]{1,0:T(8,128)(2,1)} %get-tuple-element.97.inverse_ref), custom_call_target="tpu_custom_call" | custom-call | flops 3221225472 | bytes 8388608 | tf_op jit(solution)/shard_map/cond/branch_1_fun/pallas_call | solution.py:89
  86.9 5.6 %collective-permute-done.refs_3_ = bf16[1536,1024]{1,0:T(8,128)(2,1)S(1)} collective-permute-done((bf16[1536,1024]{1,0:T(8,128)(2,1)S(1)}, bf16[1536,1024]{1,0:T(8,128)(2,1)S(1)}, u32[]{:S(2)}, u32[]{:S(2)}) %collective-permute-start) | collective-permute-done | bytes 3145760 | tf_op jit(solution)/shard_map/cond/branch_1_fun/scaled0_swap/ppermute | solution.py:36
  92.6 6.9 %branch_1_fun.17 = bf16[768,1024]{1,0:T(8,128)(2,1)S(1)} custom-call(bf16[1536,1536]{1,0:T(8,128)(2,1)} %get-tuple-element.94.refs_0_, bf16[1536,1536]{1,0:T(8,128)(2,1)} %get-tuple-element.95.refs_1_, bf16[1536,1024]{1,0:T(8,128)(2,1)S(1)} %branch_1_fun.15.refs_2_, bf16[1536,1024]{1,0:T(8,128)(2,1)S(1)} %collective-permute-done.refs_3_), custom_call_target="tpu_custom_call" | custom-call | tf_op jit(solution)/shard_map/cond/branch_1_fun/pallas_call | solution.py:119
  99.4 1.6 collective-permute-start.1
  101.0 6.8 %branch_1_fun.16 = f32[768,1024]{1,0:T(8,128)S(1)} custom-call(bf16[1536,1536]{1,0:T(8,128)(2,1)} %get-tuple-element.94.refs_0_, bf16[1536,1536]{1,0:T(8,128)(2,1)} %get-tuple-element.95.refs_1_, bf16[1536,1024]{1,0:T(8,128)(2,1)S(1)} %branch_1_fun.15.refs_2_, bf16[1536,1024]{1,0:T(8,128)(2,1)S(1)} %collective-permute-done.refs_3_), custom_call_target="tpu_custom_call" | custom-call | tf_op jit(solution)/shard_map/cond/branch_1_fun/pallas_call | solution.py:119
  107.8 12.1 %collective-permute-done.1 = bf16[2,384,1024]{2,1,0:T(8,128)(2,1)S(1)} collective-permute-done((bf16[2,384,1024]{2,1,0:T(8,128)(2,1)S(1)}, bf16[2,384,1024]{2,1,0:T(8,128)(2,1)S(1)}, u32[]{:S(2)}, u32[]{:S(2)}) %collective-permute-start.1) | collective-permute-done | bytes 1572896 | tf_op jit(solution)/shard_map/cond/branch_1_fun/sum0_first/ppermute | solution.py:36
  120.8 1.6 collective-permute-start.2
  122.4 10.4 %collective-permute-done.2 = bf16[384,1024]{1,0:T(8,128)(2,1)S(1)} collective-permute-done((bf16[384,1024]{1,0:T(8,128)(2,1)S(1)}, bf16[384,1024]{1,0:T(8,128)(2,1)S(1)}, u32[]{:S(2)}, u32[]{:S(2)}) %collective-permute-start.2) | collective-permute-done | bytes 786464 | tf_op jit(solution)/shard_map/cond/branch_1_fun/sum0_second/ppermute | solution.py:36
  135.5 10.7 %collective-permute-done.3 = bf16[384,1024]{1,0:T(8,128)(2,1)S(1)} collective-permute-done((bf16[384,1024]{1,0:T(8,128)(2,1)}, bf16[384,1024]{1,0:T(8,128)(2,1)S(1)}, u32[]{:S(2)}, u32[]{:S(2)}) %collective-permute-start.3) | collective-permute-done | bytes 786464 | tf_op jit(solution)/shard_map/cond/branch_1_fun/ring0_first/ppermute | solution.py:36
  147.6 1.6 collective-permute-start.26
  149.2 64.3 %conditional.7 = (bf16[192,1024]{1,0:T(8,128)(2,1)S(1)}, bf16[192,1024]{1,0:T(8,128)(2,1)}, bf16[2,384,1024]{2,1,0:T(8,128)(2,1)S(1)}) conditional(s32[]{:T(128)} %convert_element_type.33, () %tuple.55, (bf16[4,1536,256]{2,1,0:T(8,128)(2,1)}, bf16[1024,1024]{1,0:T(8,128)(2,1)}, bf16[1536,1536]{1,0:T(8,128)(2,1)}, bf16[1536,1536]{1,0:T(8,128)(2,1)}) %tuple.106), branch_computations={%region_4.5_spmd, %region_5.6_spmd} | conditional | flops 3224764416 | bytes 50856120 | solution.py:347
  149.2 6.0 %branch_1_fun.18.refs_2_ = bf16[1536,1024]{1,0:T(8,128)(2,1)S(1)} custom-call(bf16[4,1536,256]{2,1,0:T(8,128)(2,1)} %get-tuple-element.100.factor_ref, bf16[1024,1024]{1,0:T(8,128)(2,1)} %get-tuple-element.101.inverse_ref), custom_call_target="tpu_custom_call" | custom-call | flops 3221225472 | bytes 8388608 | tf_op jit(solution)/shard_map/cond/branch_1_fun/pallas_call | solution.py:89
  155.3 5.6 %collective-permute-done.15.refs_3_ = bf16[1536,1024]{1,0:T(8,128)(2,1)S(1)} collective-permute-done((bf16[1536,1024]{1,0:T(8,128)(2,1)S(1)}, bf16[1536,1024]{1,0:T(8,128)(2,1)S(1)}, u32[]{:S(2)}, u32[]{:S(2)}) %collective-permute-start.15) | collective-permute-done | bytes 3145760 | tf_op jit(solution)/shard_map/cond/branch_1_fun/scaled1_swap/ppermute | solution.py:36
  161.0 6.9 %branch_1_fun.20 = bf16[768,1024]{1,0:T(8,128)(2,1)S(1)} custom-call(bf16[1536,1536]{1,0:T(8,128)(2,1)} %get-tuple-element.98.refs_0_, bf16[1536,1536]{1,0:T(8,128)(2,1)} %get-tuple-element.99.refs_1_, bf16[1536,1024]{1,0:T(8,128)(2,1)S(1)} %branch_1_fun.18.refs_2_, bf16[1536,1024]{1,0:T(8,128)(2,1)S(1)} %collective-permute-done.15.refs_3_), custom_call_target="tpu_custom_call" | custom-call | tf_op jit(solution)/shard_map/cond/branch_1_fun/pallas_call | solution.py:119
  167.8 1.6 collective-permute-start.16
  169.4 6.9 %branch_1_fun.19 = f32[768,1024]{1,0:T(8,128)S(1)} custom-call(bf16[1536,1536]{1,0:T(8,128)(2,1)} %get-tuple-element.98.refs_0_, bf16[1536,1536]{1,0:T(8,128)(2,1)} %get-tuple-element.99.refs_1_, bf16[1536,1024]{1,0:T(8,128)(2,1)S(1)} %branch_1_fun.18.refs_2_, bf16[1536,1024]{1,0:T(8,128)(2,1)S(1)} %collective-permute-done.15.refs_3_), custom_call_target="tpu_custom_call" | custom-call | tf_op jit(solution)/shard_map/cond/branch_1_fun/pallas_call | solution.py:119
  176.3 12.1 %collective-permute-done.16 = bf16[2,384,1024]{2,1,0:T(8,128)(2,1)S(1)} collective-permute-done((bf16[2,384,1024]{2,1,0:T(8,128)(2,1)S(1)}, bf16[2,384,1024]{2,1,0:T(8,128)(2,1)S(1)}, u32[]{:S(2)}, u32[]{:S(2)}) %collective-permute-start.16) | collective-permute-done | bytes 1572896 | tf_op jit(solution)/shard_map/cond/branch_1_fun/sum1_first/ppermute | solution.py:36
  189.4 11.6 %collective-permute-done.17 = bf16[384,1024]{1,0:T(8,128)(2,1)S(1)} collective-permute-done((bf16[384,1024]{1,0:T(8,128)(2,1)S(1)}, bf16[384,1024]{1,0:T(8,128)(2,1)S(1)}, u32[]{:S(2)}, u32[]{:S(2)}) %collective-permute-start.17) | collective-permute-done | bytes 786464 | tf_op jit(solution)/shard_map/cond/branch_1_fun/sum1_second/ppermute | solution.py:36
  201.3 1.6 collective-permute-start.18
  203.7 9.7 %collective-permute-done.18 = bf16[384,1024]{1,0:T(8,128)(2,1)S(1)} collective-permute-done((bf16[384,1024]{1,0:T(8,128)(2,1)S(1)}, bf16[384,1024]{1,0:T(8,128)(2,1)S(1)}, u32[]{:S(2)}, u32[]{:S(2)}) %collective-permute-start.18) | collective-permute-done | bytes 786464 | tf_op jit(solution)/shard_map/cond/branch_1_fun/ring1_first/ppermute | solution.py:36
  214.3 40.9 %conditional.8 = (bf16[384,1024]{1,0:T(8,128)(2,1)}, bf16[384,1024]{1,0:T(8,128)(2,1)}, bf16[384,1024]{1,0:T(8,128)(2,1)}, bf16[2,384,1024]{2,1,0:T(8,128)(2,1)}...) conditional(s32[]{:T(128)} %convert_element_type.33, () %tuple.65, (s32[]{:T(128)}, s32[]{:T(128)}, ...), branch_computations={%region_6.7_spmd, %region_7.8_spmd} | conditional | flops 60 | bytes 33031066 | solution.py:347
  214.4 1.8 dynamic-slice_bitcast_fusion
  216.2 1.6 collective-permute-start.4
  218.7 15.3 %collective-permute-done.4 = bf16[384,1024]{1,0:T(8,128)(2,1)} collective-permute-done((bf16[384,1024]{1,0:T(8,128)(2,1)S(1)}, bf16[384,1024]{1,0:T(8,128)(2,1)}, u32[]{:S(2)}, u32[]{:S(2)}) %collective-permute-start.4) | collective-permute-done | bytes 786464 | tf_op jit(solution)/shard_map/cond/branch_1_fun/column0_10/ppermute | solution.py:36
  235.1 20.2 %collective-permute-done.5 = bf16[384,1024]{1,0:T(8,128)(2,1)} collective-permute-done((bf16[384,1024]{1,0:T(8,128)(2,1)S(1)}, bf16[384,1024]{1,0:T(8,128)(2,1)}, u32[]{:S(2)}, u32[]{:S(2)}) %collective-permute-start.5) | collective-permute-done | bytes 786464 | tf_op jit(solution)/shard_map/cond/branch_1_fun/column0_01/ppermute | solution.py:36
  255.8 41.2 %conditional.9 = (bf16[192,1024]{1,0:T(8,128)(2,1)}, bf16[192,1024]{1,0:T(8,128)(2,1)}, bf16[192,1024]{1,0:T(8,128)(2,1)}, bf16[2,384,1024]{2,1,0:T(8,128)(2,1)}...) conditional(s32[]{:T(128)} %convert_element_type.33, () %tuple.68, (bf16[2,384,1024]{2,1,0:T(8,128)(2,1)S(1)}, ...), branch_computations={%region_8.9_spmd, %region_9.10_spmd} | conditional | flops 9663676416 | bytes 66847600 | solution.py:347
  258.2 1.6 collective-permute-start.12
  261.1 22.1 %branch_1_fun.21 = f32[3072,1536]{1,0:T(8,128)} custom-call(s32[15]{0:T(128)S(1)} %get-tuple-element.109.meta_ref, f32[3072,1536]{1,0:T(8,128)} %get-tuple-element.110.total_ref, bf16[2,384,1024]{2,1,0:T(8,128)(2,1)S(1)} %get-tuple-element.111.refs_0_, bf16[2,384,1024]{2,1,0:T(8,128)(2,1)} %get-tuple-element.112.refs_1_, ...), custom_call_target="tpu_custom_call" | custom-call | flops 9663676416 | bytes 47185920 | tf_op jit(solution)/shard_map/cond/branch_1_fun/pallas_call | solution.py:196
  283.2 10.0 %collective-permute-done.12 = bf16[192,1024]{1,0:T(8,128)(2,1)} collective-permute-done((bf16[192,1024]{1,0:T(8,128)(2,1)S(1)}, bf16[192,1024]{1,0:T(8,128)(2,1)}, u32[]{:S(2)}, u32[]{:S(2)}) %collective-permute-start.12) | collective-permute-done | bytes 393248 | tf_op jit(solution)/shard_map/cond/branch_1_fun/column1_half0_01/ppermute | solution.py:36
  293.3 3.7 %collective-permute-done.14 = bf16[2,384,1024]{2,1,0:T(8,128)(2,1)} collective-permute-done((bf16[2,384,1024]{2,1,0:T(8,128)(2,1)}, bf16[2,384,1024]{2,1,0:T(8,128)(2,1)}, u32[]{:S(2)}, u32[]{:S(2)}) %collective-permute-start.14) | collective-permute-done | bytes 1572896 | tf_op jit(solution)/shard_map/cond/branch_1_fun/ring1_swap/ppermute | solution.py:36
  299.4 2.6 collective-permute-start.29
  302.0 14.8 %shard_map.48.total_ref = f32[3072,1536]{1,0:T(8,128)} custom-call(s32[15]{0:T(128)S(1)} %stack.171.meta_ref, f32[3072,1536]{1,0:T(8,128)} %get-tuple-element.245.total_ref, bf16[2,384,1024]{2,1,0:T(8,128)(2,1)S(1)} %get-tuple-element.229.refs_0_, bf16[2,384,1024]{2,1,0:T(8,128)(2,1)} %get-tuple-element.246.refs_1_, ...), custom_call_target="tpu_custom_call", output_to_operand_aliasing={{}: (1, {})} | custom-call | flops 4831838208 | bytes 26738688 | tf_op jit(solution)/shard_map/pallas_call | solution.py:196
  318.3 14.8 %shard_map.49 = f32[3072,1536]{1,0:T(8,128)} custom-call(s32[15]{0:T(128)S(1)} %stack.171.meta_ref, f32[3072,1536]{1,0:T(8,128)} %shard_map.48.total_ref, bf16[2,384,1024]{2,1,0:T(8,128)(2,1)S(1)} %get-tuple-element.229.refs_0_, bf16[2,384,1024]{2,1,0:T(8,128)(2,1)} %get-tuple-element.246.refs_1_, ...), custom_call_target="tpu_custom_call", output_to_operand_aliasing={{}: (1, {})} | custom-call | flops 4831838208 | bytes 26738688 | tf_op jit(solution)/shard_map/pallas_call | solution.py:196
  (82 shorter events, 25.9 us)
Async XLA Ops:
  6.5 74.2 %all-gather.11.cloned.1.call-start = ((), (), s32[]{:S(2)}) async-start(), calls=%async_computation | async-start | bytes 3932160 | tf_op jit(solution)/shard_map/all_gather | solution.py:360
  8.6 138.9 %all-gather.13.cloned.1.call-start = ((), (), s32[]{:S(2)}) async-start(), calls=%async_computation.1 | async-start | bytes 3932160 | tf_op jit(solution)/shard_map/all_gather | solution.py:372
  38.8 41.9 %collective-permute-start.25 = (bf16[1536,1536]{1,0:T(8,128)(2,1)}, bf16[1536,1536]{1,0:T(8,128)(2,1)}, u32[]{:S(2)}, u32[]{:S(2)}) collective-permute-start(bf16[1536,1536]{1,0:T(8,128)(2,1)} %bitcast.31), channel_id=1, source_target_pairs={{0,1},{1,0},{2,3},{3,2},{4,5},{5,4},{6,7},{7,6},{8,9},{9,8},{10,11... | collective-permute-start | bytes 14155784 | tf_op jit(solution)/shard_map/cond/branch_1_fun/held_swap/ppermute | solution.py:36
  38.8 6.4 %collective-permute-start.19 = (bf16[1,4,32,1024]{3,2,1,0:T(8,128)(2,1)S(1)}, bf16[1,4,32,1024]{3,2,1,0:T(8,128)(2,1)S(1)}, u32[]{:S(2)}, u32[]{:S(2)}) collective-permute-start(bf16[1,4,32,1024]{3,2,1,0:T(8,128)(2,1)S(1)} %get-tuple-element.264), channel_id=1, source_target_pairs={{0,16},{1,3},{2,18},{3,1},{4,20},{5,7},{6,22},{7,5},{8,24},{9,11},... | collective-permute-start | bytes 786440 | tf_op jit(solution)/shard_map/cond/branch_1_fun/inverse0_plane0/ppermute | solution.py:36
  40.4 7.9 %collective-permute-start.22 = (bf16[1,4,32,1024]{3,2,1,0:T(8,128)(2,1)S(1)}, bf16[1,4,32,1024]{3,2,1,0:T(8,128)(2,1)S(1)}, u32[]{:S(2)}, u32[]{:S(2)}) collective-permute-start(bf16[1,4,32,1024]{3,2,1,0:T(8,128)(2,1)S(1)} %get-tuple-element.263), channel_id=1, source_target_pairs={{0,16},{1,3},{2,18},{3,1},{4,20},{5,7},{6,22},{7,5},{8,24},{9,11},... | collective-permute-start | bytes 786440 | tf_op jit(solution)/shard_map/cond/branch_1_fun/inverse1_plane0/ppermute | solution.py:36
  45.3 9.2 %collective-permute-start.20 = (bf16[2,4,32,1024]{3,2,1,0:T(8,128)(2,1)S(1)}, bf16[2,4,32,1024]{3,2,1,0:T(8,128)(2,1)S(1)}, u32[]{:S(2)}, u32[]{:S(2)}) collective-permute-start(bf16[2,4,32,1024]{3,2,1,0:T(8,128)(2,1)S(1)} %pad_maximum_fusion.4), channel_id=1, source_target_pairs={{0,2},{1,17},{2,0},{3,19},{4,6},{5,21},{6,4},{7,23},{8,10},{9,25},... | collective-permute-start | bytes 1572872 | tf_op jit(solution)/shard_map/cond/branch_1_fun/inverse0_plane1/ppermute | solution.py:36
  48.4 11.8 %collective-permute-start.23 = (bf16[2,4,32,1024]{3,2,1,0:T(8,128)(2,1)S(1)}, bf16[2,4,32,1024]{3,2,1,0:T(8,128)(2,1)S(1)}, u32[]{:S(2)}, u32[]{:S(2)}) collective-permute-start(bf16[2,4,32,1024]{3,2,1,0:T(8,128)(2,1)S(1)} %pad_maximum_fusion.5), channel_id=1, source_target_pairs={{0,2},{1,17},{2,0},{3,19},{4,6},{5,21},{6,4},{7,23},{8,10},{9,25},... | collective-permute-start | bytes 1572872 | tf_op jit(solution)/shard_map/cond/branch_1_fun/inverse1_plane1/ppermute | solution.py:36
  55.7 15.1 %collective-permute-start.21 = (bf16[4,4,32,1024]{3,2,1,0:T(8,128)(2,1)}, bf16[4,4,32,1024]{3,2,1,0:T(8,128)(2,1)}, u32[]{:S(2)}, u32[]{:S(2)}) collective-permute-start(bf16[4,4,32,1024]{3,2,1,0:T(8,128)(2,1)} %pad_maximum_fusion.2), channel_id=1, source_target_pairs={{0,1},{1,0},{2,3},{3,2},{4,5},{5,4},{6,7},{7,6},{8,9},{9,8},{10,11... | collective-permute-start | bytes 3145736 | tf_op jit(solution)/shard_map/cond/branch_1_fun/inverse0_swap/ppermute | solution.py:36
  60.2 0.9 copy-start.2
  60.3 15.4 %collective-permute-start.24 = (bf16[4,4,32,1024]{3,2,1,0:T(8,128)(2,1)S(1)}, bf16[4,4,32,1024]{3,2,1,0:T(8,128)(2,1)}, u32[]{:S(2)}, u32[]{:S(2)}) collective-permute-start(bf16[4,4,32,1024]{3,2,1,0:T(8,128)(2,1)S(1)} %pad_maximum_fusion.3), channel_id=1, source_target_pairs={{0,1},{1,0},{2,3},{3,2},{4,5},{5,4},{6,7},{7,6},{8,9},{9,8},{10,11... | collective-permute-start | bytes 3145736 | tf_op jit(solution)/shard_map/cond/branch_1_fun/inverse1_swap/ppermute | solution.py:36
  72.2 3.6 %copy-start.3 = (bf16[2,4,32,1024]{3,2,1,0:T(8,128)(2,1)S(1)}, bf16[2,4,32,1024]{3,2,1,0:T(8,128)(2,1)}, u32[]{:S(2)}) copy-start(bf16[2,4,32,1024]{3,2,1,0:T(8,128)(2,1)} %copy-done.2) | copy-start | bytes 1572868 | tf_op jit(solution)/shard_map/cond
  80.7 132.8 %all-gather.15.cloned.1.call-start = ((), (), s32[]{:S(2)}) async-start(), calls=%async_computation.2 | async-start | bytes 3932160 | tf_op jit(solution)/shard_map/all_gather | solution.py:374
  86.8 5.7 %collective-permute-start = (bf16[1536,1024]{1,0:T(8,128)(2,1)S(1)}, bf16[1536,1024]{1,0:T(8,128)(2,1)S(1)}, u32[]{:S(2)}, u32[]{:S(2)}) collective-permute-start(bf16[1536,1024]{1,0:T(8,128)(2,1)S(1)} %branch_1_fun.15.refs_2_), channel_id=1, source_target_pairs={{0,1},{1,0},{2,3},{3,2},{4,5},{5,4},{6,7},{7,6},{8,9},{9,8},{10,11... | collective-permute-start | bytes 9437192 | tf_op jit(solution)/shard_map/cond/branch_1_fun/scaled0_swap/ppermute | solution.py:36
  99.4 20.5 %collective-permute-start.1 = (bf16[2,384,1024]{2,1,0:T(8,128)(2,1)S(1)}, bf16[2,384,1024]{2,1,0:T(8,128)(2,1)S(1)}, u32[]{:S(2)}, u32[]{:S(2)}) collective-permute-start(bf16[2,384,1024]{2,1,0:T(8,128)(2,1)S(1)} %bitcast.101), channel_id=1, source_target_pairs={{0,16},{1,3},{2,18},{3,1},{4,20},{5,7},{6,22},{7,5},{8,24},{9,11},... | collective-permute-start | bytes 4718600 | tf_op jit(solution)/shard_map/cond/branch_1_fun/sum0_first/ppermute | solution.py:36
  120.8 12.1 %collective-permute-start.2 = (bf16[384,1024]{1,0:T(8,128)(2,1)S(1)}, bf16[384,1024]{1,0:T(8,128)(2,1)S(1)}, u32[]{:S(2)}, u32[]{:S(2)}) collective-permute-start(bf16[384,1024]{1,0:T(8,128)(2,1)S(1)} %fusion.2), channel_id=1, source_target_pairs={{0,2},{1,17},{2,0},{3,19},{4,6},{5,21},{6,4},{7,23},{8,10},{9,25},... | collective-permute-start | bytes 2359304 | tf_op jit(solution)/shard_map/cond/branch_1_fun/sum0_second/ppermute | solution.py:36
  134.0 12.2 %collective-permute-start.3 = (bf16[384,1024]{1,0:T(8,128)(2,1)}, bf16[384,1024]{1,0:T(8,128)(2,1)S(1)}, u32[]{:S(2)}, u32[]{:S(2)}) collective-permute-start(bf16[384,1024]{1,0:T(8,128)(2,1)} %fusion.1), channel_id=1, source_target_pairs={{0,16},{1,3},{2,18},{3,1},{4,20},{5,7},{6,22},{7,5},{8,24},{9,11},... | collective-permute-start | bytes 2359304 | tf_op jit(solution)/shard_map/cond/branch_1_fun/ring0_first/ppermute | solution.py:36
  147.5 107.8 %all-gather.17.cloned.1.call-start = ((), (), s32[]{:S(2)}) async-start(), calls=%async_computation.3 | async-start | bytes 1966080 | tf_op jit(solution)/shard_map/all_gather | solution.py:398
  147.6 66.0 %collective-permute-start.26 = (bf16[2,384,1024]{2,1,0:T(8,128)(2,1)S(1)}, bf16[2,384,1024]{2,1,0:T(8,128)(2,1)}, u32[]{:S(2)}, u32[]{:S(2)}) collective-permute-start(bf16[2,384,1024]{2,1,0:T(8,128)(2,1)S(1)} %get-tuple-element.232), channel_id=1, source_target_pairs={{0,2},{1,17},{2,0},{3,19},{4,6},{5,21},{6,4},{7,23},{8,10},{9,25},... | collective-permute-start | bytes 4718600 | tf_op jit(solution)/shard_map/ring0_second/ppermute | solution.py:36
  155.2 5.7 %collective-permute-start.15 = (bf16[1536,1024]{1,0:T(8,128)(2,1)S(1)}, bf16[1536,1024]{1,0:T(8,128)(2,1)S(1)}, u32[]{:S(2)}, u32[]{:S(2)}) collective-permute-start(bf16[1536,1024]{1,0:T(8,128)(2,1)S(1)} %branch_1_fun.18.refs_2_), channel_id=1, source_target_pairs={{0,1},{1,0},{2,3},{3,2},{4,5},{5,4},{6,7},{7,6},{8,9},{9,8},{10,11... | collective-permute-start | bytes 9437192 | tf_op jit(solution)/shard_map/cond/branch_1_fun/scaled1_swap/ppermute | solution.py:36
  167.8 20.5 %collective-permute-start.16 = (bf16[2,384,1024]{2,1,0:T(8,128)(2,1)S(1)}, bf16[2,384,1024]{2,1,0:T(8,128)(2,1)S(1)}, u32[]{:S(2)}, u32[]{:S(2)}) collective-permute-start(bf16[2,384,1024]{2,1,0:T(8,128)(2,1)S(1)} %bitcast.102), channel_id=1, source_target_pairs={{0,16},{1,3},{2,18},{3,1},{4,20},{5,7},{6,22},{7,5},{8,24},{9,11},... | collective-permute-start | bytes 4718600 | tf_op jit(solution)/shard_map/cond/branch_1_fun/sum1_first/ppermute | solution.py:36
  189.0 12.1 %collective-permute-start.17 = (bf16[384,1024]{1,0:T(8,128)(2,1)S(1)}, bf16[384,1024]{1,0:T(8,128)(2,1)S(1)}, u32[]{:S(2)}, u32[]{:S(2)}) collective-permute-start(bf16[384,1024]{1,0:T(8,128)(2,1)S(1)} %fusion.5), channel_id=1, source_target_pairs={{0,2},{1,17},{2,0},{3,19},{4,6},{5,21},{6,4},{7,23},{8,10},{9,25},... | collective-permute-start | bytes 2359304 | tf_op jit(solution)/shard_map/cond/branch_1_fun/sum1_second/ppermute | solution.py:36
  201.3 12.1 %collective-permute-start.18 = (bf16[384,1024]{1,0:T(8,128)(2,1)S(1)}, bf16[384,1024]{1,0:T(8,128)(2,1)S(1)}, u32[]{:S(2)}, u32[]{:S(2)}) collective-permute-start(bf16[384,1024]{1,0:T(8,128)(2,1)S(1)} %fusion.4), channel_id=1, source_target_pairs={{0,16},{1,3},{2,18},{3,1},{4,20},{5,7},{6,22},{7,5},{8,24},{9,11},... | collective-permute-start | bytes 2359304 | tf_op jit(solution)/shard_map/cond/branch_1_fun/ring1_first/ppermute | solution.py:36
  213.5 0.7 copy-start.4
  214.3 82.7 %all-gather.19.cloned.1.call-start = ((), (), s32[]{:S(2)}) async-start(), calls=%async_computation.4 | async-start | bytes 1966080 | tf_op jit(solution)/shard_map/all_gather | solution.py:415
  216.2 17.8 %collective-permute-start.4 = (bf16[384,1024]{1,0:T(8,128)(2,1)S(1)}, bf16[384,1024]{1,0:T(8,128)(2,1)}, u32[]{:S(2)}, u32[]{:S(2)}) collective-permute-start(bf16[384,1024]{1,0:T(8,128)(2,1)S(1)} %get-tuple-element.269), channel_id=1, source_target_pairs={{0,16},{1,17},{2,18},{3,19},{4,20},{5,21},{6,22},{7,23},{8,24},{9,... | collective-permute-start | bytes 2359304 | tf_op jit(solution)/shard_map/cond/branch_1_fun/column0_10/ppermute | solution.py:36
  217.8 37.5 %collective-permute-start.7 = (bf16[2,384,1024]{2,1,0:T(8,128)(2,1)S(1)}, bf16[2,384,1024]{2,1,0:T(8,128)(2,1)}, u32[]{:S(2)}, u32[]{:S(2)}) collective-permute-start(bf16[2,384,1024]{2,1,0:T(8,128)(2,1)S(1)} %get-tuple-element.105), channel_id=1, source_target_pairs={{0,1},{1,0},{2,3},{3,2},{4,5},{5,4},{6,7},{7,6},{8,9},{9,8},{10,11... | collective-permute-start | bytes 4718600 | tf_op jit(solution)/shard_map/cond/branch_1_fun/ring0_swap/ppermute | solution.py:36
  217.8 37.5 %collective-permute-start.8 = (bf16[2,384,1024]{2,1,0:T(8,128)(2,1)}, bf16[2,384,1024]{2,1,0:T(8,128)(2,1)}, u32[]{:S(2)}, u32[]{:S(2)}) collective-permute-start(bf16[2,384,1024]{2,1,0:T(8,128)(2,1)} %get-tuple-element.106), channel_id=1, source_target_pairs={{0,1},{1,0},{2,3},{3,2},{4,5},{5,4},{6,7},{7,6},{8,9},{9,8},{10,11... | collective-permute-start | bytes 4718600 | tf_op jit(solution)/shard_map/cond/branch_1_fun/ring0_swap/ppermute | solution.py:36
  218.3 37.0 %collective-permute-start.9 = (bf16[2,384,1024]{2,1,0:T(8,128)(2,1)S(1)}, bf16[2,384,1024]{2,1,0:T(8,128)(2,1)}, u32[]{:S(2)}, u32[]{:S(2)}) collective-permute-start(bf16[2,384,1024]{2,1,0:T(8,128)(2,1)S(1)} %get-tuple-element.107), channel_id=1, source_target_pairs={{0,1},{1,0},{2,3},{3,2},{4,5},{5,4},{6,7},{7,6},{8,9},{9,8},{10,11... | collective-permute-start | bytes 4718600 | tf_op jit(solution)/shard_map/cond/branch_1_fun/ring1_swap/ppermute | solution.py:36
  218.3 36.9 %collective-permute-start.5 = (bf16[384,1024]{1,0:T(8,128)(2,1)S(1)}, bf16[384,1024]{1,0:T(8,128)(2,1)}, u32[]{:S(2)}, u32[]{:S(2)}) collective-permute-start(bf16[384,1024]{1,0:T(8,128)(2,1)S(1)} %get-tuple-element.268), channel_id=1, source_target_pairs={{0,2},{1,3},{2,0},{3,1},{4,6},{5,7},{6,4},{7,5},{8,10},{9,11},{10,... | collective-permute-start | bytes 2359304 | tf_op jit(solution)/shard_map/cond/branch_1_fun/column0_01/ppermute | solution.py:36
  234.0 21.3 %collective-permute-start.6 = (bf16[384,1024]{1,0:T(8,128)(2,1)S(1)}, bf16[384,1024]{1,0:T(8,128)(2,1)}, u32[]{:S(2)}, u32[]{:S(2)}) collective-permute-start(bf16[384,1024]{1,0:T(8,128)(2,1)S(1)} %get-tuple-element.267), channel_id=1, source_target_pairs={{0,18},{1,19},{2,16},{3,17},{4,22},{5,23},{6,20},{7,21},{8,26},{9,... | collective-permute-start | bytes 2359304 | tf_op jit(solution)/shard_map/cond/branch_1_fun/column0_11/ppermute | solution.py:36
  255.8 37.4 %collective-permute-start.10 = (bf16[2,384,1024]{2,1,0:T(8,128)(2,1)S(1)}, bf16[2,384,1024]{2,1,0:T(8,128)(2,1)}, u32[]{:S(2)}, u32[]{:S(2)}) collective-permute-start(bf16[2,384,1024]{2,1,0:T(8,128)(2,1)S(1)} %get-tuple-element.108), channel_id=1, source_target_pairs={{0,2},{1,17},{2,0},{3,19},{4,6},{5,21},{6,4},{7,23},{8,10},{9,25},... | collective-permute-start | bytes 4718600 | tf_op jit(solution)/shard_map/cond/branch_1_fun/ring1_second/ppermute | solution.py:36
  257.6 25.7 %collective-permute-start.11 = (bf16[192,1024]{1,0:T(8,128)(2,1)S(1)}, bf16[192,1024]{1,0:T(8,128)(2,1)}, u32[]{:S(2)}, u32[]{:S(2)}) collective-permute-start(bf16[192,1024]{1,0:T(8,128)(2,1)S(1)} %get-tuple-element.272), channel_id=1, source_target_pairs={{0,16},{1,17},{2,18},{3,19},{4,20},{5,21},{6,22},{7,23},{8,24},{9,... | collective-permute-start | bytes 1179656 | tf_op jit(solution)/shard_map/cond/branch_1_fun/column1_half0_10/ppermute | solution.py:36
  258.2 35.1 %collective-permute-start.12 = (bf16[192,1024]{1,0:T(8,128)(2,1)S(1)}, bf16[192,1024]{1,0:T(8,128)(2,1)}, u32[]{:S(2)}, u32[]{:S(2)}) collective-permute-start(bf16[192,1024]{1,0:T(8,128)(2,1)S(1)} %get-tuple-element.271), channel_id=1, source_target_pairs={{0,2},{1,3},{2,0},{3,1},{4,6},{5,7},{6,4},{7,5},{8,10},{9,11},{10,... | collective-permute-start | bytes 1179656 | tf_op jit(solution)/shard_map/cond/branch_1_fun/column1_half0_01/ppermute | solution.py:36
  259.8 33.5 %collective-permute-start.13 = (bf16[192,1024]{1,0:T(8,128)(2,1)S(1)}, bf16[192,1024]{1,0:T(8,128)(2,1)}, u32[]{:S(2)}, u32[]{:S(2)}) collective-permute-start(bf16[192,1024]{1,0:T(8,128)(2,1)S(1)} %get-tuple-element.270), channel_id=1, source_target_pairs={{0,18},{1,19},{2,16},{3,17},{4,22},{5,23},{6,20},{7,21},{8,26},{9,... | collective-permute-start | bytes 1179656 | tf_op jit(solution)/shard_map/cond/branch_1_fun/column1_half0_11/ppermute | solution.py:36
  293.2 3.8 %collective-permute-start.14 = (bf16[2,384,1024]{2,1,0:T(8,128)(2,1)}, bf16[2,384,1024]{2,1,0:T(8,128)(2,1)}, u32[]{:S(2)}, u32[]{:S(2)}) collective-permute-start(bf16[2,384,1024]{2,1,0:T(8,128)(2,1)} %collective-permute-done.10), channel_id=1, source_target_pairs={{0,1},{1,0},{2,3},{3,2},{4,5},{5,4},{6,7},{7,6},{8,9},{9,8},{10,11... | collective-permute-start | bytes 4718600 | tf_op jit(solution)/shard_map/cond/branch_1_fun/ring1_swap/ppermute | solution.py:36
  297.0 5.0 %copy-start.1 = (bf16[768,1024]{1,0:T(8,128)(2,1)S(1)}, bf16[768,1024]{1,0:T(8,128)(2,1)}, u32[]{:S(2)}) copy-start(bf16[768,1024]{1,0:T(8,128)(2,1)} %all-gather.17.cloned.1.call-done) | copy-start | bytes 4718596
  298.4 18.4 %collective-permute-start.27 = (bf16[192,1024]{1,0:T(8,128)(2,1)S(1)}, bf16[192,1024]{1,0:T(8,128)(2,1)S(1)}, u32[]{:S(2)}, u32[]{:S(2)}) collective-permute-start(bf16[192,1024]{1,0:T(8,128)(2,1)S(1)} %get-tuple-element.275), channel_id=1, source_target_pairs={{0,16},{1,17},{2,18},{3,19},{4,20},{5,21},{6,22},{7,23},{8,24},{9,... | collective-permute-start | bytes 1179656 | tf_op jit(solution)/shard_map/column1_half1_10/ppermute | solution.py:36
  299.0 19.3 %collective-permute-start.28 = (bf16[192,1024]{1,0:T(8,128)(2,1)S(1)}, bf16[192,1024]{1,0:T(8,128)(2,1)S(1)}, u32[]{:S(2)}, u32[]{:S(2)}) collective-permute-start(bf16[192,1024]{1,0:T(8,128)(2,1)S(1)} %get-tuple-element.274), channel_id=1, source_target_pairs={{0,2},{1,3},{2,0},{3,1},{4,6},{5,7},{6,4},{7,5},{8,10},{9,11},{10,... | collective-permute-start | bytes 1179656 | tf_op jit(solution)/shard_map/column1_half1_01/ppermute | solution.py:36
  299.4 18.9 %collective-permute-start.29 = (bf16[192,1024]{1,0:T(8,128)(2,1)S(1)}, bf16[192,1024]{1,0:T(8,128)(2,1)S(1)}, u32[]{:S(2)}, u32[]{:S(2)}) collective-permute-start(bf16[192,1024]{1,0:T(8,128)(2,1)S(1)} %get-tuple-element.273), channel_id=1, source_target_pairs={{0,18},{1,19},{2,16},{3,17},{4,22},{5,23},{6,20},{7,21},{8,26},{9,... | collective-permute-start | bytes 1179656 | tf_op jit(solution)/shard_map/column1_half1_11/ppermute | solution.py:36
  302.0 16.3 %copy-start = (bf16[768,1024]{1,0:T(8,128)(2,1)S(1)}, bf16[768,1024]{1,0:T(8,128)(2,1)}, u32[]{:S(2)}) copy-start(bf16[768,1024]{1,0:T(8,128)(2,1)} %all-gather.19.cloned.1.call-done) | copy-start | bytes 4718596
Sparse Core Ops, SparseCore 0:
  8.9 68.7 all-gather.10
  80.9 63.2 all-gather.12
  147.6 63.2 all-gather.14
  214.4 35.7 all-gather.16
  255.5 34.8 all-gather.18

commit v5 on v4

--- a/solution.py
+++ b/solution.py
@@ -397,20 +397,17 @@
         parts, pair, moved, rests, total = fence(parts, pairs[panels - 1], moved, rests, total)
         gathered = {0: lax.all_gather(parts[0], "row")}
 
-        def first_work(value, rest, pair):
-            came = swapped = None
-            if value is not None:
-                came, swapped = to_columns(panels - 2, value), ring_swap(panels - 2, rest)
-            return came, swapped, ring_swap(panels - 1, [pair])
-
-        came, swapped, near = together(first_work, moved.get(panels - 2), rests.get(panels - 2), pair)
+        came = swapped = None
+        if panels > 1:
+            swapped = ring_swap(panels - 2, rests[panels - 2])
+            came = together(lambda value: to_columns(panels - 2, value), moved[panels - 2])
         lefts = {}
         if panels > 1:
             lefts[panels - 2] = joined(rests[panels - 2], swapped)
         arrived = {}
         for h in range(HALVES):
-            state = fence(parts, pair, near, moved, lefts, total, gathered, came, arrived)
-            parts, pair, near, moved, lefts, total, gathered, came, arrived = state
+            state = fence(parts, pair, moved, lefts, total, gathered, came, arrived)
+            parts, pair, moved, lefts, total, gathered, came, arrived = state
             if h + 1 < HALVES:
                 gathered[h + 1] = lax.all_gather(parts[h + 1], "row")
             if h == 0:
@@ -418,13 +415,14 @@
                 def last_work(value, pair, total, lefts, moved, came):
                     steps_done = to_columns(f"{panels - 1}_half0", value)
                     around = ring_rest(panels - 1, pair)
+                    near = ring_swap(panels - 1, [pair])
                     if came is not None:
                         total = update(meta, total, lefts, both(moved, came))
                         around, total, steps_done = fence(around, total, steps_done)
                     far = ring_swap(panels - 1, around[1:])
-                    return steps_done, around[1:], far, total if came is not None else None
-
-                arrived[0], rest, far, latest = together(
+                    return steps_done, around[1:], near, far, total if came is not None else None
+
+                arrived[0], rest, near, far, latest = together(
                     last_work,
                     gathered[0],
                     pair,

time: 341 us -> 340 us (level)
  no operation moved by 1% of the time
where the time goes in v5:
time: 340 us; the launch traced here: 339 us
  waiting for transfers between devices  142 us (42%)
  Pallas kernels  113 us (33%)
  starting transfers between devices  27.5 us (8%)
  blocking collectives  21.5 us (6%)
  between operations  13.6 us (4%)
  local copies, waits for them, and re-layouts  12.2 us (4%)
  other arithmetic  8.29 us (2%)
    ppermute x30, waiting for transfers between devices, send(): return lax.ppermute(value, AXES, pairs)  142 us
    pallas_call x3, Pallas kernels, update(): pl.pallas_call(kernel, out_shape=jax.ShapeDtypeStruct(total.shape, total....  51.9 us
    pallas_call x4, Pallas kernels, product(): pl.pallas_call(kernel, out_shape=jax.ShapeDtypeStruct((count, width), kin...  27.4 us
    ppermute x30, starting transfers between devices, send(): return lax.ppermute(value, AXES, pairs)  27.3 us
    pallas_call x4, Pallas kernels, reorder(): pl.pallas_call(kernel, out_shape=jax.ShapeDtypeStruct((planes, count, hei...  22 us
    all_gather x1, blocking collectives, prepare(): stack, blocks = fence(lax.all_gather(own_rows, 'row'), blocks)  21.5 us
    pallas_call x2, Pallas kernels, scale(): pl.pallas_call(kernel, out_shape=jax.ShapeDtypeStruct((tile, width), fact...  12.1 us
  transfers between devices with their start and end apart: 35, of which 17 were waited for; matrix products, arithmetic and copies ran while one was open for 5% of the time, Pallas kernels for 29%

profile of v5, /device:TPU:0, one launch (start us, length us, event | category | flops | bytes accessed | tf_op | source)
XLA Modules:
  0.0 338.9 jit_solution(18252622592959028153)
XLA Ops:
  6.5 2.1 slice.32
  8.7 72.0 %conditional.5 = (bf16[1024,1024]{1,0:T(8,128)(2,1)}, bf16[1024,1024]{1,0:T(8,128)(2,1)}, bf16[1536,1536]{1,0:T(8,128)(2,1)}, bf16[1536,1536]{1,0:T(8,128)(2,1)}, bf16[1536,256]{1,0:T(8,128)(2,1)}) conditional(s32[]{:T(128)} %convert_element_type.33, () %tuple.56, (s32[]{:T(128)}, s32[]{:T(128)}, s32[]{:T(128)}, s32[]{:T(128)}, ...), branch_computations={%region_0.1_spmd, %region_1.2_spmd} | conditional | flops 8913181 | bytes 83234256 | solution.py:347
  9.8 21.5 %all-gather = bf16[8,32,1024]{2,1,0:T(8,128)(2,1)S(1)} all-gather(bf16[2,32,1024]{2,1,0:T(8,128)(2,1)S(1)} %constant_dynamic-slice_fusion), channel_id=2, replica_groups=mesh['sec'=2,'row'=4,'col'=4] {'row'}, dimensions={0}, use_global_device_ids=true | all-gather | bytes 655360 | tf_op jit(solution)/shard_map/cond/branch_1_fun/all_gather | solution.py:354
  31.4 7.4 %branch_1_fun.14 = bf16[1,8,192,1536]{3,2,1,0:T(8,128)(2,1)} custom-call(s32[8]{0:T(128)S(1)} %stack.133.order_ref, bf16[16,1,192,1536]{3,2,1,0:T(8,128)(2,1)} %bitcast.103), custom_call_target="tpu_custom_call" | custom-call | bytes 9437184 | tf_op jit(solution)/shard_map/cond/branch_1_fun/pallas_call | solution.py:60
  38.8 1.6 collective-permute-start.17
  40.9 4.3 %collective-permute-done.17 = bf16[1,4,32,1024]{3,2,1,0:T(8,128)(2,1)S(1)} collective-permute-done((bf16[1,4,32,1024]{3,2,1,0:T(8,128)(2,1)S(1)}, bf16[1,4,32,1024]{3,2,1,0:T(8,128)(2,1)S(1)}, u32[]{:S(2)}, u32[]{:S(2)}) %collective-permute-start.17) | collective-permute-done | bytes 262176 | tf_op jit(solution)/shard_map/cond/branch_1_fun/inverse0_plane0/ppermute | solution.py:36
  45.3 1.6 collective-permute-start.18
  48.4 1.6 collective-permute-start.21
  50.0 4.5 %collective-permute-done.18 = bf16[2,4,32,1024]{3,2,1,0:T(8,128)(2,1)S(1)} collective-permute-done((bf16[2,4,32,1024]{3,2,1,0:T(8,128)(2,1)S(1)}, bf16[2,4,32,1024]{3,2,1,0:T(8,128)(2,1)S(1)}, u32[]{:S(2)}, u32[]{:S(2)}) %collective-permute-start.18) | collective-permute-done | bytes 524320 | tf_op jit(solution)/shard_map/cond/branch_1_fun/inverse0_plane1/ppermute | solution.py:36
  55.7 4.5 %collective-permute-done.21 = bf16[2,4,32,1024]{3,2,1,0:T(8,128)(2,1)S(1)} collective-permute-done((bf16[2,4,32,1024]{3,2,1,0:T(8,128)(2,1)S(1)}, bf16[2,4,32,1024]{3,2,1,0:T(8,128)(2,1)S(1)}, u32[]{:S(2)}, u32[]{:S(2)}) %collective-permute-start.21) | collective-permute-done | bytes 524320 | tf_op jit(solution)/shard_map/cond/branch_1_fun/inverse1_plane1/ppermute | solution.py:36
  61.1 7.4 %branch_1_fun.13 = bf16[1,8,192,1536]{3,2,1,0:T(8,128)(2,1)} custom-call(s32[8]{0:T(128)S(1)} %stack.124.order_ref, bf16[16,1,192,1536]{3,2,1,0:T(8,128)(2,1)} %bitcast.104), custom_call_target="tpu_custom_call" | custom-call | bytes 9437184 | tf_op jit(solution)/shard_map/cond/branch_1_fun/pallas_call | solution.py:60
  68.6 2.1 slice_bitcast_fusion
  72.1 3.6 %branch_1_fun.11 = bf16[4,8,32,1024]{3,2,1,0:T(8,128)(2,1)} custom-call(s32[8]{0:T(128)S(1)} %stack.42.order_ref, bf16[8,4,32,1024]{3,2,1,0:T(8,128)(2,1)S(1)} %pad_maximum_fusion.in_ref), custom_call_target="tpu_custom_call" | custom-call | bytes 4194304 | tf_op jit(solution)/shard_map/cond/branch_1_fun/pallas_call | solution.py:60
  77.1 3.6 %branch_1_fun.12 = bf16[4,8,32,1024]{3,2,1,0:T(8,128)(2,1)} custom-call(s32[8]{0:T(128)S(1)} %stack.42.order_ref, bf16[8,4,32,1024]{3,2,1,0:T(8,128)(2,1)S(1)} %pad_maximum_fusion.1.in_ref), custom_call_target="tpu_custom_call" | custom-call | bytes 4194304 | tf_op jit(solution)/shard_map/cond/branch_1_fun/pallas_call | solution.py:60
  80.8 66.7 %conditional.6 = (bf16[384,1024]{1,0:T(8,128)(2,1)}, bf16[2,384,1024]{2,1,0:T(8,128)(2,1)S(1)}) conditional(s32[]{:T(128)} %convert_element_type.33, () %tuple.60, (bf16[4,1536,256]{2,1,0:T(8,128)(2,1)}, bf16[1024,1024]{1,0:T(8,128)(2,1)}, bf16[1536,1536]{1,0:T(8,128)(2,1)}, bf16[1536,1536]{1,0:T(8,128)(2,1)}) %tuple.61), branch_computations={%region_2.3_spmd, %region_3.4_spmd} | conditional | flops 3224764416 | bytes 49283248 | solution.py:347
  80.8 6.0 %branch_1_fun.15.refs_2_ = bf16[1536,1024]{1,0:T(8,128)(2,1)S(1)} custom-call(bf16[4,1536,256]{2,1,0:T(8,128)(2,1)} %get-tuple-element.90.factor_ref, bf16[1024,1024]{1,0:T(8,128)(2,1)} %get-tuple-element.91.inverse_ref), custom_call_target="tpu_custom_call" | custom-call | flops 3221225472 | bytes 8388608 | tf_op jit(solution)/shard_map/cond/branch_1_fun/pallas_call | solution.py:89
  86.9 5.6 %collective-permute-done.refs_3_ = bf16[1536,1024]{1,0:T(8,128)(2,1)S(1)} collective-permute-done((bf16[1536,1024]{1,0:T(8,128)(2,1)S(1)}, bf16[1536,1024]{1,0:T(8,128)(2,1)S(1)}, u32[]{:S(2)}, u32[]{:S(2)}) %collective-permute-start) | collective-permute-done | bytes 3145760 | tf_op jit(solution)/shard_map/cond/branch_1_fun/scaled0_swap/ppermute | solution.py:36
  92.5 6.9 %branch_1_fun.17 = bf16[768,1024]{1,0:T(8,128)(2,1)S(1)} custom-call(bf16[1536,1536]{1,0:T(8,128)(2,1)} %get-tuple-element.88.refs_0_, bf16[1536,1536]{1,0:T(8,128)(2,1)} %get-tuple-element.89.refs_1_, bf16[1536,1024]{1,0:T(8,128)(2,1)S(1)} %branch_1_fun.15.refs_2_, bf16[1536,1024]{1,0:T(8,128)(2,1)S(1)} %collective-permute-done.refs_3_), custom_call_target="tpu_custom_call" | custom-call | tf_op jit(solution)/shard_map/cond/branch_1_fun/pallas_call | solution.py:119
  99.4 1.6 collective-permute-start.1
  101.0 6.8 %branch_1_fun.16 = f32[768,1024]{1,0:T(8,128)S(1)} custom-call(bf16[1536,1536]{1,0:T(8,128)(2,1)} %get-tuple-element.88.refs_0_, bf16[1536,1536]{1,0:T(8,128)(2,1)} %get-tuple-element.89.refs_1_, bf16[1536,1024]{1,0:T(8,128)(2,1)S(1)} %branch_1_fun.15.refs_2_, bf16[1536,1024]{1,0:T(8,128)(2,1)S(1)} %collective-permute-done.refs_3_), custom_call_target="tpu_custom_call" | custom-call | tf_op jit(solution)/shard_map/cond/branch_1_fun/pallas_call | solution.py:119
  107.8 12.1 %collective-permute-done.1 = bf16[2,384,1024]{2,1,0:T(8,128)(2,1)S(1)} collective-permute-done((bf16[2,384,1024]{2,1,0:T(8,128)(2,1)S(1)}, bf16[2,384,1024]{2,1,0:T(8,128)(2,1)S(1)}, u32[]{:S(2)}, u32[]{:S(2)}) %collective-permute-start.1) | collective-permute-done | bytes 1572896 | tf_op jit(solution)/shard_map/cond/branch_1_fun/sum0_first/ppermute | solution.py:36
  120.7 1.6 collective-permute-start.2
  122.4 10.4 %collective-permute-done.2 = bf16[384,1024]{1,0:T(8,128)(2,1)S(1)} collective-permute-done((bf16[384,1024]{1,0:T(8,128)(2,1)S(1)}, bf16[384,1024]{1,0:T(8,128)(2,1)S(1)}, u32[]{:S(2)}, u32[]{:S(2)}) %collective-permute-start.2) | collective-permute-done | bytes 786464 | tf_op jit(solution)/shard_map/cond/branch_1_fun/sum0_second/ppermute | solution.py:36
  135.5 10.7 %collective-permute-done.3 = bf16[384,1024]{1,0:T(8,128)(2,1)S(1)} collective-permute-done((bf16[384,1024]{1,0:T(8,128)(2,1)}, bf16[384,1024]{1,0:T(8,128)(2,1)S(1)}, u32[]{:S(2)}, u32[]{:S(2)}) %collective-permute-start.3) | collective-permute-done | bytes 786464 | tf_op jit(solution)/shard_map/cond/branch_1_fun/ring0_first/ppermute | solution.py:36
  147.6 1.6 collective-permute-start.24
  149.2 64.3 %conditional.7 = (bf16[192,1024]{1,0:T(8,128)(2,1)S(1)}, bf16[192,1024]{1,0:T(8,128)(2,1)}, bf16[2,384,1024]{2,1,0:T(8,128)(2,1)S(1)}) conditional(s32[]{:T(128)} %convert_element_type.33, () %tuple.55, (bf16[4,1536,256]{2,1,0:T(8,128)(2,1)}, bf16[1024,1024]{1,0:T(8,128)(2,1)}, bf16[1536,1536]{1,0:T(8,128)(2,1)}, bf16[1536,1536]{1,0:T(8,128)(2,1)}) %tuple.106), branch_computations={%region_4.5_spmd, %region_5.6_spmd} | conditional | flops 3224764416 | bytes 50856120 | solution.py:347
  149.2 6.0 %branch_1_fun.18.refs_2_ = bf16[1536,1024]{1,0:T(8,128)(2,1)S(1)} custom-call(bf16[4,1536,256]{2,1,0:T(8,128)(2,1)} %get-tuple-element.94.factor_ref, bf16[1024,1024]{1,0:T(8,128)(2,1)} %get-tuple-element.95.inverse_ref), custom_call_target="tpu_custom_call" | custom-call | flops 3221225472 | bytes 8388608 | tf_op jit(solution)/shard_map/cond/branch_1_fun/pallas_call | solution.py:89
  155.3 5.6 %collective-permute-done.13.refs_3_ = bf16[1536,1024]{1,0:T(8,128)(2,1)S(1)} collective-permute-done((bf16[1536,1024]{1,0:T(8,128)(2,1)S(1)}, bf16[1536,1024]{1,0:T(8,128)(2,1)S(1)}, u32[]{:S(2)}, u32[]{:S(2)}) %collective-permute-start.13) | collective-permute-done | bytes 3145760 | tf_op jit(solution)/shard_map/cond/branch_1_fun/scaled1_swap/ppermute | solution.py:36
  161.0 6.9 %branch_1_fun.20 = bf16[768,1024]{1,0:T(8,128)(2,1)S(1)} custom-call(bf16[1536,1536]{1,0:T(8,128)(2,1)} %get-tuple-element.92.refs_0_, bf16[1536,1536]{1,0:T(8,128)(2,1)} %get-tuple-element.93.refs_1_, bf16[1536,1024]{1,0:T(8,128)(2,1)S(1)} %branch_1_fun.18.refs_2_, bf16[1536,1024]{1,0:T(8,128)(2,1)S(1)} %collective-permute-done.13.refs_3_), custom_call_target="tpu_custom_call" | custom-call | tf_op jit(solution)/shard_map/cond/branch_1_fun/pallas_call | solution.py:119
  167.8 1.7 collective-permute-start.14
  169.5 6.9 %branch_1_fun.19 = f32[768,1024]{1,0:T(8,128)S(1)} custom-call(bf16[1536,1536]{1,0:T(8,128)(2,1)} %get-tuple-element.92.refs_0_, bf16[1536,1536]{1,0:T(8,128)(2,1)} %get-tuple-element.93.refs_1_, bf16[1536,1024]{1,0:T(8,128)(2,1)S(1)} %branch_1_fun.18.refs_2_, bf16[1536,1024]{1,0:T(8,128)(2,1)S(1)} %collective-permute-done.13.refs_3_), custom_call_target="tpu_custom_call" | custom-call | tf_op jit(solution)/shard_map/cond/branch_1_fun/pallas_call | solution.py:119
  176.4 11.9 %collective-permute-done.14 = bf16[2,384,1024]{2,1,0:T(8,128)(2,1)S(1)} collective-permute-done((bf16[2,384,1024]{2,1,0:T(8,128)(2,1)S(1)}, bf16[2,384,1024]{2,1,0:T(8,128)(2,1)S(1)}, u32[]{:S(2)}, u32[]{:S(2)}) %collective-permute-start.14) | collective-permute-done | bytes 1572896 | tf_op jit(solution)/shard_map/cond/branch_1_fun/sum1_first/ppermute | solution.py:36
  189.4 11.6 %collective-permute-done.15 = bf16[384,1024]{1,0:T(8,128)(2,1)S(1)} collective-permute-done((bf16[384,1024]{1,0:T(8,128)(2,1)S(1)}, bf16[384,1024]{1,0:T(8,128)(2,1)S(1)}, u32[]{:S(2)}, u32[]{:S(2)}) %collective-permute-start.15) | collective-permute-done | bytes 786464 | tf_op jit(solution)/shard_map/cond/branch_1_fun/sum1_second/ppermute | solution.py:36
  201.3 1.7 collective-permute-start.16
  203.8 9.6 %collective-permute-done.16 = bf16[384,1024]{1,0:T(8,128)(2,1)S(1)} collective-permute-done((bf16[384,1024]{1,0:T(8,128)(2,1)S(1)}, bf16[384,1024]{1,0:T(8,128)(2,1)S(1)}, u32[]{:S(2)}, u32[]{:S(2)}) %collective-permute-start.16) | collective-permute-done | bytes 786464 | tf_op jit(solution)/shard_map/cond/branch_1_fun/ring1_first/ppermute | solution.py:36
  214.9 39.7 %conditional.8 = (bf16[384,1024]{1,0:T(8,128)(2,1)}, bf16[384,1024]{1,0:T(8,128)(2,1)}, bf16[384,1024]{1,0:T(8,128)(2,1)}) conditional(s32[]{:T(128)} %convert_element_type.33, () %tuple.65, (s32[]{:T(128)}, s32[]{:T(128)}, bf16[4,384,1024]{2,1,0:T(8,128)(2,1)}) %tuple.103), branch_computations={%region_6.7_spmd, %region_7.8_spmd} | conditional | flops 60 | bytes 14156554 | solution.py:347
  214.9 1.8 dynamic-slice_bitcast_fusion
  216.7 1.7 collective-permute-start.4
  218.7 1.6 collective-permute-start.6
  220.3 17.0 %collective-permute-done.4 = bf16[384,1024]{1,0:T(8,128)(2,1)} collective-permute-done((bf16[384,1024]{1,0:T(8,128)(2,1)S(1)}, bf16[384,1024]{1,0:T(8,128)(2,1)}, u32[]{:S(2)}, u32[]{:S(2)}) %collective-permute-start.4) | collective-permute-done | bytes 786464 | tf_op jit(solution)/shard_map/cond/branch_1_fun/column0_10/ppermute | solution.py:36
  237.3 17.3 %collective-permute-done.5 = bf16[384,1024]{1,0:T(8,128)(2,1)} collective-permute-done((bf16[384,1024]{1,0:T(8,128)(2,1)S(1)}, bf16[384,1024]{1,0:T(8,128)(2,1)}, u32[]{:S(2)}, u32[]{:S(2)}) %collective-permute-start.5) | collective-permute-done | bytes 786464 | tf_op jit(solution)/shard_map/cond/branch_1_fun/column0_01/ppermute | solution.py:36
  255.1 41.2 %conditional.9 = (bf16[192,1024]{1,0:T(8,128)(2,1)}, bf16[192,1024]{1,0:T(8,128)(2,1)}, bf16[192,1024]{1,0:T(8,128)(2,1)}, bf16[2,384,1024]{2,1,0:T(8,128)(2,1)}...) conditional(s32[]{:T(128)} %convert_element_type.33, () %tuple.68, ...), branch_computations={%region_8.9_spmd, %region_9.10_spmd} | conditional | flops 9663676416 | bytes 73139104 | solution.py:347
  260.4 22.3 %branch_1_fun.21 = f32[3072,1536]{1,0:T(8,128)} custom-call(s32[15]{0:T(128)S(1)} %get-tuple-element.100.meta_ref, f32[3072,1536]{1,0:T(8,128)} %get-tuple-element.101.total_ref, bf16[2,384,1024]{2,1,0:T(8,128)(2,1)S(1)} %get-tuple-element.102.refs_0_, bf16[2,384,1024]{2,1,0:T(8,128)(2,1)} %get-tuple-element.103.refs_1_, ...), custom_call_target="tpu_custom_call" | custom-call | flops 9663676416 | bytes 47185920 | tf_op jit(solution)/shard_map/cond/branch_1_fun/pallas_call | solution.py:196
  282.7 9.9 %collective-permute-done.9 = bf16[192,1024]{1,0:T(8,128)(2,1)} collective-permute-done((bf16[192,1024]{1,0:T(8,128)(2,1)S(1)}, bf16[192,1024]{1,0:T(8,128)(2,1)}, u32[]{:S(2)}, u32[]{:S(2)}) %collective-permute-start.9) | collective-permute-done | bytes 393248 | tf_op jit(solution)/shard_map/cond/branch_1_fun/column1_half0_01/ppermute | solution.py:36
  292.6 3.7 %collective-permute-done.12 = bf16[2,384,1024]{2,1,0:T(8,128)(2,1)} collective-permute-done((bf16[2,384,1024]{2,1,0:T(8,128)(2,1)}, bf16[2,384,1024]{2,1,0:T(8,128)(2,1)}, u32[]{:S(2)}, u32[]{:S(2)}) %collective-permute-start.12) | collective-permute-done | bytes 1572896 | tf_op jit(solution)/shard_map/cond/branch_1_fun/ring1_swap/ppermute | solution.py:36
  299.6 1.8 collective-permute-start.29
  301.3 14.8 %shard_map.48.total_ref = f32[3072,1536]{1,0:T(8,128)} custom-call(s32[15]{0:T(128)S(1)} %stack.171.meta_ref, f32[3072,1536]{1,0:T(8,128)} %get-tuple-element.229.total_ref, bf16[2,384,1024]{2,1,0:T(8,128)(2,1)S(1)} %get-tuple-element.214.refs_0_, bf16[2,384,1024]{2,1,0:T(8,128)(2,1)} %get-tuple-element.230.refs_1_, ...), custom_call_target="tpu_custom_call", output_to_operand_aliasing={{}: (1, {})} | custom-call | flops 4831838208 | bytes 26738688 | tf_op jit(solution)/shard_map/pallas_call | solution.py:196
  317.6 14.8 %shard_map.49 = f32[3072,1536]{1,0:T(8,128)} custom-call(s32[15]{0:T(128)S(1)} %stack.171.meta_ref, f32[3072,1536]{1,0:T(8,128)} %shard_map.48.total_ref, bf16[2,384,1024]{2,1,0:T(8,128)(2,1)S(1)} %get-tuple-element.214.refs_0_, bf16[2,384,1024]{2,1,0:T(8,128)(2,1)} %get-tuple-element.230.refs_1_, ...), custom_call_target="tpu_custom_call", output_to_operand_aliasing={{}: (1, {})} | custom-call | flops 4831838208 | bytes 26738688 | tf_op jit(solution)/shard_map/pallas_call | solution.py:196
  (82 shorter events, 26.9 us)
Async XLA Ops:
  6.5 74.2 %all-gather.11.cloned.1.call-start = ((), (), s32[]{:S(2)}) async-start(), calls=%async_computation | async-start | bytes 3932160 | tf_op jit(solution)/shard_map/all_gather | solution.py:360
  8.6 138.8 %all-gather.13.cloned.1.call-start = ((), (), s32[]{:S(2)}) async-start(), calls=%async_computation.1 | async-start | bytes 3932160 | tf_op jit(solution)/shard_map/all_gather | solution.py:372
  38.8 41.9 %collective-permute-start.23 = (bf16[1536,1536]{1,0:T(8,128)(2,1)}, bf16[1536,1536]{1,0:T(8,128)(2,1)}, u32[]{:S(2)}, u32[]{:S(2)}) collective-permute-start(bf16[1536,1536]{1,0:T(8,128)(2,1)} %bitcast.31), channel_id=1, source_target_pairs={{0,1},{1,0},{2,3},{3,2},{4,5},{5,4},{6,7},{7,6},{8,9},{9,8},{10,11... | collective-permute-start | bytes 14155784 | tf_op jit(solution)/shard_map/cond/branch_1_fun/held_swap/ppermute | solution.py:36
  38.8 6.4 %collective-permute-start.17 = (bf16[1,4,32,1024]{3,2,1,0:T(8,128)(2,1)S(1)}, bf16[1,4,32,1024]{3,2,1,0:T(8,128)(2,1)S(1)}, u32[]{:S(2)}, u32[]{:S(2)}) collective-permute-start(bf16[1,4,32,1024]{3,2,1,0:T(8,128)(2,1)S(1)} %get-tuple-element.249), channel_id=1, source_target_pairs={{0,16},{1,3},{2,18},{3,1},{4,20},{5,7},{6,22},{7,5},{8,24},{9,11},... | collective-permute-start | bytes 786440 | tf_op jit(solution)/shard_map/cond/branch_1_fun/inverse0_plane0/ppermute | solution.py:36
  40.4 7.9 %collective-permute-start.20 = (bf16[1,4,32,1024]{3,2,1,0:T(8,128)(2,1)S(1)}, bf16[1,4,32,1024]{3,2,1,0:T(8,128)(2,1)S(1)}, u32[]{:S(2)}, u32[]{:S(2)}) collective-permute-start(bf16[1,4,32,1024]{3,2,1,0:T(8,128)(2,1)S(1)} %get-tuple-element.248), channel_id=1, source_target_pairs={{0,16},{1,3},{2,18},{3,1},{4,20},{5,7},{6,22},{7,5},{8,24},{9,11},... | collective-permute-start | bytes 786440 | tf_op jit(solution)/shard_map/cond/branch_1_fun/inverse1_plane0/ppermute | solution.py:36
  45.3 9.2 %collective-permute-start.18 = (bf16[2,4,32,1024]{3,2,1,0:T(8,128)(2,1)S(1)}, bf16[2,4,32,1024]{3,2,1,0:T(8,128)(2,1)S(1)}, u32[]{:S(2)}, u32[]{:S(2)}) collective-permute-start(bf16[2,4,32,1024]{3,2,1,0:T(8,128)(2,1)S(1)} %pad_maximum_fusion.4), channel_id=1, source_target_pairs={{0,2},{1,17},{2,0},{3,19},{4,6},{5,21},{6,4},{7,23},{8,10},{9,25},... | collective-permute-start | bytes 1572872 | tf_op jit(solution)/shard_map/cond/branch_1_fun/inverse0_plane1/ppermute | solution.py:36
  48.4 11.8 %collective-permute-start.21 = (bf16[2,4,32,1024]{3,2,1,0:T(8,128)(2,1)S(1)}, bf16[2,4,32,1024]{3,2,1,0:T(8,128)(2,1)S(1)}, u32[]{:S(2)}, u32[]{:S(2)}) collective-permute-start(bf16[2,4,32,1024]{3,2,1,0:T(8,128)(2,1)S(1)} %pad_maximum_fusion.5), channel_id=1, source_target_pairs={{0,2},{1,17},{2,0},{3,19},{4,6},{5,21},{6,4},{7,23},{8,10},{9,25},... | collective-permute-start | bytes 1572872 | tf_op jit(solution)/shard_map/cond/branch_1_fun/inverse1_plane1/ppermute | solution.py:36
  55.7 15.0 %collective-permute-start.19 = (bf16[4,4,32,1024]{3,2,1,0:T(8,128)(2,1)}, bf16[4,4,32,1024]{3,2,1,0:T(8,128)(2,1)}, u32[]{:S(2)}, u32[]{:S(2)}) collective-permute-start(bf16[4,4,32,1024]{3,2,1,0:T(8,128)(2,1)} %pad_maximum_fusion.2), channel_id=1, source_target_pairs={{0,1},{1,0},{2,3},{3,2},{4,5},{5,4},{6,7},{7,6},{8,9},{9,8},{10,11... | collective-permute-start | bytes 3145736 | tf_op jit(solution)/shard_map/cond/branch_1_fun/inverse0_swap/ppermute | solution.py:36
  60.2 0.8 copy-start.2
  60.3 15.4 %collective-permute-start.22 = (bf16[4,4,32,1024]{3,2,1,0:T(8,128)(2,1)S(1)}, bf16[4,4,32,1024]{3,2,1,0:T(8,128)(2,1)}, u32[]{:S(2)}, u32[]{:S(2)}) collective-permute-start(bf16[4,4,32,1024]{3,2,1,0:T(8,128)(2,1)S(1)} %pad_maximum_fusion.3), channel_id=1, source_target_pairs={{0,1},{1,0},{2,3},{3,2},{4,5},{5,4},{6,7},{7,6},{8,9},{9,8},{10,11... | collective-permute-start | bytes 3145736 | tf_op jit(solution)/shard_map/cond/branch_1_fun/inverse1_swap/ppermute | solution.py:36
  72.1 3.6 %copy-start.3 = (bf16[2,4,32,1024]{3,2,1,0:T(8,128)(2,1)S(1)}, bf16[2,4,32,1024]{3,2,1,0:T(8,128)(2,1)}, u32[]{:S(2)}) copy-start(bf16[2,4,32,1024]{3,2,1,0:T(8,128)(2,1)} %copy-done.2) | copy-start | bytes 1572868 | tf_op jit(solution)/shard_map/cond
  80.7 132.8 %all-gather.15.cloned.1.call-start = ((), (), s32[]{:S(2)}) async-start(), calls=%async_computation.2 | async-start | bytes 3932160 | tf_op jit(solution)/shard_map/all_gather | solution.py:374
  86.8 5.7 %collective-permute-start = (bf16[1536,1024]{1,0:T(8,128)(2,1)S(1)}, bf16[1536,1024]{1,0:T(8,128)(2,1)S(1)}, u32[]{:S(2)}, u32[]{:S(2)}) collective-permute-start(bf16[1536,1024]{1,0:T(8,128)(2,1)S(1)} %branch_1_fun.15.refs_2_), channel_id=1, source_target_pairs={{0,1},{1,0},{2,3},{3,2},{4,5},{5,4},{6,7},{7,6},{8,9},{9,8},{10,11... | collective-permute-start | bytes 9437192 | tf_op jit(solution)/shard_map/cond/branch_1_fun/scaled0_swap/ppermute | solution.py:36
  99.4 20.5 %collective-permute-start.1 = (bf16[2,384,1024]{2,1,0:T(8,128)(2,1)S(1)}, bf16[2,384,1024]{2,1,0:T(8,128)(2,1)S(1)}, u32[]{:S(2)}, u32[]{:S(2)}) collective-permute-start(bf16[2,384,1024]{2,1,0:T(8,128)(2,1)S(1)} %bitcast.101), channel_id=1, source_target_pairs={{0,16},{1,3},{2,18},{3,1},{4,20},{5,7},{6,22},{7,5},{8,24},{9,11},... | collective-permute-start | bytes 4718600 | tf_op jit(solution)/shard_map/cond/branch_1_fun/sum0_first/ppermute | solution.py:36
  120.7 12.1 %collective-permute-start.2 = (bf16[384,1024]{1,0:T(8,128)(2,1)S(1)}, bf16[384,1024]{1,0:T(8,128)(2,1)S(1)}, u32[]{:S(2)}, u32[]{:S(2)}) collective-permute-start(bf16[384,1024]{1,0:T(8,128)(2,1)S(1)} %fusion.2), channel_id=1, source_target_pairs={{0,2},{1,17},{2,0},{3,19},{4,6},{5,21},{6,4},{7,23},{8,10},{9,25},... | collective-permute-start | bytes 2359304 | tf_op jit(solution)/shard_map/cond/branch_1_fun/sum0_second/ppermute | solution.py:36
  134.0 12.2 %collective-permute-start.3 = (bf16[384,1024]{1,0:T(8,128)(2,1)}, bf16[384,1024]{1,0:T(8,128)(2,1)S(1)}, u32[]{:S(2)}, u32[]{:S(2)}) collective-permute-start(bf16[384,1024]{1,0:T(8,128)(2,1)} %fusion.1), channel_id=1, source_target_pairs={{0,16},{1,3},{2,18},{3,1},{4,20},{5,7},{6,22},{7,5},{8,24},{9,11},... | collective-permute-start | bytes 2359304 | tf_op jit(solution)/shard_map/cond/branch_1_fun/ring0_first/ppermute | solution.py:36
  147.5 107.1 %all-gather.17.cloned.1.call-start = ((), (), s32[]{:S(2)}) async-start(), calls=%async_computation.3 | async-start | bytes 1966080 | tf_op jit(solution)/shard_map/all_gather | solution.py:398
  147.6 66.0 %collective-permute-start.24 = (bf16[2,384,1024]{2,1,0:T(8,128)(2,1)S(1)}, bf16[2,384,1024]{2,1,0:T(8,128)(2,1)}, u32[]{:S(2)}, u32[]{:S(2)}) collective-permute-start(bf16[2,384,1024]{2,1,0:T(8,128)(2,1)S(1)} %get-tuple-element.216), channel_id=1, source_target_pairs={{0,2},{1,17},{2,0},{3,19},{4,6},{5,21},{6,4},{7,23},{8,10},{9,25},... | collective-permute-start | bytes 4718600 | tf_op jit(solution)/shard_map/ring0_second/ppermute | solution.py:36
  155.2 5.7 %collective-permute-start.13 = (bf16[1536,1024]{1,0:T(8,128)(2,1)S(1)}, bf16[1536,1024]{1,0:T(8,128)(2,1)S(1)}, u32[]{:S(2)}, u32[]{:S(2)}) collective-permute-start(bf16[1536,1024]{1,0:T(8,128)(2,1)S(1)} %branch_1_fun.18.refs_2_), channel_id=1, source_target_pairs={{0,1},{1,0},{2,3},{3,2},{4,5},{5,4},{6,7},{7,6},{8,9},{9,8},{10,11... | collective-permute-start | bytes 9437192 | tf_op jit(solution)/shard_map/cond/branch_1_fun/scaled1_swap/ppermute | solution.py:36
  167.8 20.5 %collective-permute-start.14 = (bf16[2,384,1024]{2,1,0:T(8,128)(2,1)S(1)}, bf16[2,384,1024]{2,1,0:T(8,128)(2,1)S(1)}, u32[]{:S(2)}, u32[]{:S(2)}) collective-permute-start(bf16[2,384,1024]{2,1,0:T(8,128)(2,1)S(1)} %bitcast.102), channel_id=1, source_target_pairs={{0,16},{1,3},{2,18},{3,1},{4,20},{5,7},{6,22},{7,5},{8,24},{9,11},... | collective-permute-start | bytes 4718600 | tf_op jit(solution)/shard_map/cond/branch_1_fun/sum1_first/ppermute | solution.py:36
  189.0 12.1 %collective-permute-start.15 = (bf16[384,1024]{1,0:T(8,128)(2,1)S(1)}, bf16[384,1024]{1,0:T(8,128)(2,1)S(1)}, u32[]{:S(2)}, u32[]{:S(2)}) collective-permute-start(bf16[384,1024]{1,0:T(8,128)(2,1)S(1)} %fusion.5), channel_id=1, source_target_pairs={{0,2},{1,17},{2,0},{3,19},{4,6},{5,21},{6,4},{7,23},{8,10},{9,25},... | collective-permute-start | bytes 2359304 | tf_op jit(solution)/shard_map/cond/branch_1_fun/sum1_second/ppermute | solution.py:36
  201.3 12.1 %collective-permute-start.16 = (bf16[384,1024]{1,0:T(8,128)(2,1)S(1)}, bf16[384,1024]{1,0:T(8,128)(2,1)S(1)}, u32[]{:S(2)}, u32[]{:S(2)}) collective-permute-start(bf16[384,1024]{1,0:T(8,128)(2,1)S(1)} %fusion.4), channel_id=1, source_target_pairs={{0,16},{1,3},{2,18},{3,1},{4,20},{5,7},{6,22},{7,5},{8,24},{9,11},... | collective-permute-start | bytes 2359304 | tf_op jit(solution)/shard_map/cond/branch_1_fun/ring1_first/ppermute | solution.py:36
  213.5 0.7 copy-start.4
  214.3 82.1 %all-gather.19.cloned.1.call-start = ((), (), s32[]{:S(2)}) async-start(), calls=%async_computation.4 | async-start | bytes 1966080 | tf_op jit(solution)/shard_map/all_gather | solution.py:412
  214.3 40.3 %collective-permute-start.25 = (bf16[2,384,1024]{2,1,0:T(8,128)(2,1)S(1)}, bf16[2,384,1024]{2,1,0:T(8,128)(2,1)}, u32[]{:S(2)}, u32[]{:S(2)}) collective-permute-start(bf16[2,384,1024]{2,1,0:T(8,128)(2,1)S(1)} %get-tuple-element.216), channel_id=1, source_target_pairs={{0,1},{1,0},{2,3},{3,2},{4,5},{5,4},{6,7},{7,6},{8,9},{9,8},{10,11... | collective-permute-start | bytes 4718600 | tf_op jit(solution)/shard_map/ring0_swap/ppermute | solution.py:36
  214.4 40.2 %collective-permute-start.26 = (bf16[2,384,1024]{2,1,0:T(8,128)(2,1)}, bf16[2,384,1024]{2,1,0:T(8,128)(2,1)}, u32[]{:S(2)}, u32[]{:S(2)}) collective-permute-start(bf16[2,384,1024]{2,1,0:T(8,128)(2,1)} %collective-permute-done.24), channel_id=1, source_target_pairs={{0,1},{1,0},{2,3},{3,2},{4,5},{5,4},{6,7},{7,6},{8,9},{9,8},{10,11... | collective-permute-start | bytes 4718600 | tf_op jit(solution)/shard_map/ring0_swap/ppermute | solution.py:36
  216.7 20.6 %collective-permute-start.4 = (bf16[384,1024]{1,0:T(8,128)(2,1)S(1)}, bf16[384,1024]{1,0:T(8,128)(2,1)}, u32[]{:S(2)}, u32[]{:S(2)}) collective-permute-start(bf16[384,1024]{1,0:T(8,128)(2,1)S(1)} %get-tuple-element.254), channel_id=1, source_target_pairs={{0,16},{1,17},{2,18},{3,19},{4,20},{5,21},{6,22},{7,23},{8,24},{9,... | collective-permute-start | bytes 2359304 | tf_op jit(solution)/shard_map/cond/branch_1_fun/column0_10/ppermute | solution.py:36
  218.4 36.2 %collective-permute-start.5 = (bf16[384,1024]{1,0:T(8,128)(2,1)S(1)}, bf16[384,1024]{1,0:T(8,128)(2,1)}, u32[]{:S(2)}, u32[]{:S(2)}) collective-permute-start(bf16[384,1024]{1,0:T(8,128)(2,1)S(1)} %get-tuple-element.253), channel_id=1, source_target_pairs={{0,2},{1,3},{2,0},{3,1},{4,6},{5,7},{6,4},{7,5},{8,10},{9,11},{10,... | collective-permute-start | bytes 2359304 | tf_op jit(solution)/shard_map/cond/branch_1_fun/column0_01/ppermute | solution.py:36
  218.7 35.9 %collective-permute-start.6 = (bf16[384,1024]{1,0:T(8,128)(2,1)S(1)}, bf16[384,1024]{1,0:T(8,128)(2,1)}, u32[]{:S(2)}, u32[]{:S(2)}) collective-permute-start(bf16[384,1024]{1,0:T(8,128)(2,1)S(1)} %get-tuple-element.252), channel_id=1, source_target_pairs={{0,18},{1,19},{2,16},{3,17},{4,22},{5,23},{6,20},{7,21},{8,26},{9,... | collective-permute-start | bytes 2359304 | tf_op jit(solution)/shard_map/cond/branch_1_fun/column0_11/ppermute | solution.py:36
  255.1 37.4 %collective-permute-start.7 = (bf16[2,384,1024]{2,1,0:T(8,128)(2,1)S(1)}, bf16[2,384,1024]{2,1,0:T(8,128)(2,1)}, u32[]{:S(2)}, u32[]{:S(2)}) collective-permute-start(bf16[2,384,1024]{2,1,0:T(8,128)(2,1)S(1)} %get-tuple-element.99), channel_id=1, source_target_pairs={{0,2},{1,17},{2,0},{3,19},{4,6},{5,21},{6,4},{7,23},{8,10},{9,25},... | collective-permute-start | bytes 4718600 | tf_op jit(solution)/shard_map/cond/branch_1_fun/ring1_second/ppermute | solution.py:36
  255.5 37.1 %collective-permute-start.11 = (bf16[2,384,1024]{2,1,0:T(8,128)(2,1)S(1)}, bf16[2,384,1024]{2,1,0:T(8,128)(2,1)}, u32[]{:S(2)}, u32[]{:S(2)}) collective-permute-start(bf16[2,384,1024]{2,1,0:T(8,128)(2,1)S(1)} %get-tuple-element.99), channel_id=1, source_target_pairs={{0,1},{1,0},{2,3},{3,2},{4,5},{5,4},{6,7},{7,6},{8,9},{9,8},{10,11... | collective-permute-start | bytes 4718600 | tf_op jit(solution)/shard_map/cond/branch_1_fun/ring1_swap/ppermute | solution.py:36
  256.8 25.8 %collective-permute-start.8 = (bf16[192,1024]{1,0:T(8,128)(2,1)S(1)}, bf16[192,1024]{1,0:T(8,128)(2,1)}, u32[]{:S(2)}, u32[]{:S(2)}) collective-permute-start(bf16[192,1024]{1,0:T(8,128)(2,1)S(1)} %get-tuple-element.257), channel_id=1, source_target_pairs={{0,16},{1,17},{2,18},{3,19},{4,20},{5,21},{6,22},{7,23},{8,24},{9,... | collective-permute-start | bytes 1179656 | tf_op jit(solution)/shard_map/cond/branch_1_fun/column1_half0_10/ppermute | solution.py:36
  258.3 34.3 %collective-permute-start.9 = (bf16[192,1024]{1,0:T(8,128)(2,1)S(1)}, bf16[192,1024]{1,0:T(8,128)(2,1)}, u32[]{:S(2)}, u32[]{:S(2)}) collective-permute-start(bf16[192,1024]{1,0:T(8,128)(2,1)S(1)} %get-tuple-element.256), channel_id=1, source_target_pairs={{0,2},{1,3},{2,0},{3,1},{4,6},{5,7},{6,4},{7,5},{8,10},{9,11},{10,... | collective-permute-start | bytes 1179656 | tf_op jit(solution)/shard_map/cond/branch_1_fun/column1_half0_01/ppermute | solution.py:36
  259.0 33.6 %collective-permute-start.10 = (bf16[192,1024]{1,0:T(8,128)(2,1)S(1)}, bf16[192,1024]{1,0:T(8,128)(2,1)}, u32[]{:S(2)}, u32[]{:S(2)}) collective-permute-start(bf16[192,1024]{1,0:T(8,128)(2,1)S(1)} %get-tuple-element.255), channel_id=1, source_target_pairs={{0,18},{1,19},{2,16},{3,17},{4,22},{5,23},{6,20},{7,21},{8,26},{9,... | collective-permute-start | bytes 1179656 | tf_op jit(solution)/shard_map/cond/branch_1_fun/column1_half0_11/ppermute | solution.py:36
  292.6 3.8 %collective-permute-start.12 = (bf16[2,384,1024]{2,1,0:T(8,128)(2,1)}, bf16[2,384,1024]{2,1,0:T(8,128)(2,1)}, u32[]{:S(2)}, u32[]{:S(2)}) collective-permute-start(bf16[2,384,1024]{2,1,0:T(8,128)(2,1)} %collective-permute-done.7), channel_id=1, source_target_pairs={{0,1},{1,0},{2,3},{3,2},{4,5},{5,4},{6,7},{7,6},{8,9},{9,8},{10,11... | collective-permute-start | bytes 4718600 | tf_op jit(solution)/shard_map/cond/branch_1_fun/ring1_swap/ppermute | solution.py:36
  296.3 5.0 %copy-start.1 = (bf16[768,1024]{1,0:T(8,128)(2,1)S(1)}, bf16[768,1024]{1,0:T(8,128)(2,1)}, u32[]{:S(2)}) copy-start(bf16[768,1024]{1,0:T(8,128)(2,1)} %all-gather.17.cloned.1.call-done) | copy-start | bytes 4718596
  297.8 18.4 %collective-permute-start.27 = (bf16[192,1024]{1,0:T(8,128)(2,1)S(1)}, bf16[192,1024]{1,0:T(8,128)(2,1)S(1)}, u32[]{:S(2)}, u32[]{:S(2)}) collective-permute-start(bf16[192,1024]{1,0:T(8,128)(2,1)S(1)} %get-tuple-element.260), channel_id=1, source_target_pairs={{0,16},{1,17},{2,18},{3,19},{4,20},{5,21},{6,22},{7,23},{8,24},{9,... | collective-permute-start | bytes 1179656 | tf_op jit(solution)/shard_map/column1_half1_10/ppermute | solution.py:36
  298.2 19.3 %collective-permute-start.28 = (bf16[192,1024]{1,0:T(8,128)(2,1)S(1)}, bf16[192,1024]{1,0:T(8,128)(2,1)S(1)}, u32[]{:S(2)}, u32[]{:S(2)}) collective-permute-start(bf16[192,1024]{1,0:T(8,128)(2,1)S(1)} %get-tuple-element.259), channel_id=1, source_target_pairs={{0,2},{1,3},{2,0},{3,1},{4,6},{5,7},{6,4},{7,5},{8,10},{9,11},{10,... | collective-permute-start | bytes 1179656 | tf_op jit(solution)/shard_map/column1_half1_01/ppermute | solution.py:36
  299.6 18.0 %collective-permute-start.29 = (bf16[192,1024]{1,0:T(8,128)(2,1)S(1)}, bf16[192,1024]{1,0:T(8,128)(2,1)S(1)}, u32[]{:S(2)}, u32[]{:S(2)}) collective-permute-start(bf16[192,1024]{1,0:T(8,128)(2,1)S(1)} %get-tuple-element.258), channel_id=1, source_target_pairs={{0,18},{1,19},{2,16},{3,17},{4,22},{5,23},{6,20},{7,21},{8,26},{9,... | collective-permute-start | bytes 1179656 | tf_op jit(solution)/shard_map/column1_half1_11/ppermute | solution.py:36
  301.3 16.2 %copy-start = (bf16[768,1024]{1,0:T(8,128)(2,1)S(1)}, bf16[768,1024]{1,0:T(8,128)(2,1)}, u32[]{:S(2)}) copy-start(bf16[768,1024]{1,0:T(8,128)(2,1)} %all-gather.19.cloned.1.call-done) | copy-start | bytes 4718596
Sparse Core Ops, SparseCore 0:
  8.9 68.7 all-gather.10
  80.8 63.2 all-gather.12
  147.6 63.2 all-gather.14
  214.4 35.7 all-gather.16
  254.8 35.3 all-gather.18
